TPU v7x, 32 devices: a whole 2x2x4 slice. The times are simulated.
32 devices in a mesh: fsdp: 2 (over core), ctx: 16 (over z, y, x).
Axes of the slice: x: 2, y: 2, z: 4, core: 2. Of those that a mesh axis runs over, the one named last changes fastest.
Arguments:
- inputs: bfloat16 [4, 2048, 1024], P('fsdp', 'ctx'), may hold values from -6 to 6
- lengths: int32 [4], P('fsdp'), may hold values from 512 to 2048, as said below
- w_query: bfloat16 [1024, 1024], P(('fsdp', 'ctx')), may hold values from -0.375 to 0.375
- b_query: bfloat16 [1024], P(('fsdp', 'ctx')), may hold values from -3 to 3
- w_key: bfloat16 [1024, 1024], P(('fsdp', 'ctx')), may hold values from -0.1875 to 0.1875
- w_value: bfloat16 [1024, 1024], P(('fsdp', 'ctx')), may hold values from -0.1875 to 0.1875
- b_value: bfloat16 [1024], P(('fsdp', 'ctx')), may hold values from -3 to 3
- w_out: bfloat16 [1024, 1024], P(('fsdp', 'ctx')), may hold values from -1.5 to 1.5
- b_out: bfloat16 [1024], P(('fsdp', 'ctx')), may hold values from -3 to 3
- first_gain: bfloat16 [1024], P(('fsdp', 'ctx')), may hold values from 0.099609375 to 1.8984375
- first_shift: bfloat16 [1024], P(('fsdp', 'ctx')), may hold values from -3 to 3
- w_expand: bfloat16 [1024, 4096], P(('fsdp', 'ctx')), may hold values from -0.1875 to 0.1875
- b_expand: bfloat16 [4096], P(('fsdp', 'ctx')), may hold values from -3 to 3
- w_reduce: bfloat16 [4096, 1024], P(('fsdp', 'ctx')), may hold values from -0.125 to 0.125
- b_reduce: bfloat16 [1024], P(('fsdp', 'ctx')), may hold values from -3 to 3
- second_gain: bfloat16 [1024], P(('fsdp', 'ctx')), may hold values from 0.099609375 to 1.8984375
- second_shift: bfloat16 [1024], P(('fsdp', 'ctx')), may hold values from -3 to 3
- cotangent: bfloat16 [4, 2048, 1024], P('fsdp', 'ctx'), may hold values from -6 to 6
Outputs:
- layer_out: bfloat16 [4, 2048, 1024], P('fsdp', 'ctx')
- input_grad: float32 [4, 2048, 1024], P('fsdp', 'ctx')
- w_query_grad: float32 [1024, 1024], P(('fsdp', 'ctx'))
- b_query_grad: float32 [1024], P(('fsdp', 'ctx'))
- w_key_grad: float32 [1024, 1024], P(('fsdp', 'ctx'))
- w_value_grad: float32 [1024, 1024], P(('fsdp', 'ctx'))
- b_value_grad: float32 [1024], P(('fsdp', 'ctx'))
- w_out_grad: float32 [1024, 1024], P(('fsdp', 'ctx'))
- b_out_grad: float32 [1024], P(('fsdp', 'ctx'))
- first_gain_grad: float32 [1024], P(('fsdp', 'ctx'))
- first_shift_grad: float32 [1024], P(('fsdp', 'ctx'))
- w_expand_grad: float32 [1024, 4096], P(('fsdp', 'ctx'))
- b_expand_grad: float32 [4096], P(('fsdp', 'ctx'))
- w_reduce_grad: float32 [4096, 1024], P(('fsdp', 'ctx'))
- b_reduce_grad: float32 [1024], P(('fsdp', 'ctx'))
- second_gain_grad: float32 [1024], P(('fsdp', 'ctx'))
- second_shift_grad: float32 [1024], P(('fsdp', 'ctx'))
Inputs may be any that keep to these rules, and one draw needn't show every extreme that they name: `lengths`: valid length of each sequence; positions from it on are padding. Exactly one sequence has 2048 valid positions.
All inputs are finite; a program needn't handle non-finite values.
Results may differ from a plain program's by a relative error of at most 0.029.
Values may be sent and summed in bfloat16 or wider, within the bound.
A program may use at most 256 MiB of HBM per device.

v0:
```python
from functools import partial
import math

import jax
import jax.numpy as jnp
from jax import lax
from jax.sharding import PartitionSpec as P

HEADS = 16


epsilon = 1e-05
masked_score = -1e30


def layer_norm(rows_in, gain, shift):
    center = rows_in - jnp.mean(rows_in, -1, keepdims=True)
    spread = jnp.mean(center * center, -1, keepdims=True)
    return center * lax.rsqrt(spread + epsilon) * gain + shift


def product(left, right):
    return jnp.dot(left, right, preferred_element_type=jnp.float32)


def outer_sum(left, right):
    return jnp.einsum("rd,re->de", left, right, preferred_element_type=jnp.float32)


def back_product(grad_rows, weight):
    return jnp.einsum("re,de->rd", grad_rows, weight, preferred_element_type=jnp.float32)


def over_blocks(step_fn, carry_state, pair_rows):
    key_count = pair_rows.shape[1]
    block_width = math.gcd(key_count, 512)

    def turn(turn_index, inner_state):
        block_pairs = lax.dynamic_slice_in_dim(pair_rows, turn_index * block_width, block_width, 1)
        return step_fn(inner_state, block_pairs, turn_index * block_width)

    return lax.fori_loop(0, key_count // block_width, turn, carry_state)


def shards(
    inputs,
    lengths,
    w_query,
    b_query,
    w_key,
    w_value,
    b_value,
    w_out,
    b_out,
    first_gain,
    first_shift,
    w_expand,
    b_expand,
    w_reduce,
    b_reduce,
    second_gain,
    second_shift,
    cotangent,
):
    gathered = (
        lax.all_gather(w_query, ("fsdp", "ctx"), axis=0, tiled=True),
        lax.all_gather(b_query, ("fsdp", "ctx"), axis=0, tiled=True),
        lax.all_gather(w_key, ("fsdp", "ctx"), axis=0, tiled=True),
        lax.all_gather(w_value, ("fsdp", "ctx"), axis=0, tiled=True),
        lax.all_gather(b_value, ("fsdp", "ctx"), axis=0, tiled=True),
        lax.all_gather(w_out, ("fsdp", "ctx"), axis=0, tiled=True),
        lax.all_gather(b_out, ("fsdp", "ctx"), axis=0, tiled=True),
        lax.all_gather(first_gain, ("fsdp", "ctx"), axis=0, tiled=True),
        lax.all_gather(first_shift, ("fsdp", "ctx"), axis=0, tiled=True),
        lax.all_gather(w_expand, ("fsdp", "ctx"), axis=0, tiled=True),
        lax.all_gather(b_expand, ("fsdp", "ctx"), axis=0, tiled=True),
        lax.all_gather(w_reduce, ("fsdp", "ctx"), axis=0, tiled=True),
        lax.all_gather(b_reduce, ("fsdp", "ctx"), axis=0, tiled=True),
        lax.all_gather(second_gain, ("fsdp", "ctx"), axis=0, tiled=True),
        lax.all_gather(second_shift, ("fsdp", "ctx"), axis=0, tiled=True),
    )
    (
        full_query,
        bias_query,
        full_key,
        full_value,
        bias_value,
        full_out,
        bias_out,
        gain_first,
        shift_first,
        full_expand,
        bias_expand,
        full_reduce,
        bias_reduce,
        gain_second,
        shift_second,
    ) = gathered
    seq_count, block_rows, model_width = inputs.shape
    total_rows = seq_count * block_rows
    head_size = model_width // HEADS
    score_scale = head_size ** (-0.5)
    own_first = lax.axis_index("ctx") * block_rows
    positions = own_first + jnp.arange(block_rows, dtype=jnp.int32)
    valid_rows = (positions[None, :] < lengths[:, None]).astype(jnp.float32).reshape(total_rows, 1)
    flat_rows = inputs.reshape(total_rows, model_width)
    queries = (product(flat_rows, full_query) + bias_query.astype(jnp.float32)).astype(jnp.bfloat16)
    key_rows = product(flat_rows, full_key).astype(jnp.bfloat16)
    value_rows = (product(flat_rows, full_value) + bias_value.astype(jnp.float32)).astype(
        jnp.bfloat16
    )
    query_heads = queries.reshape(seq_count, block_rows, HEADS, head_size)
    local_pairs = jnp.concatenate([key_rows, value_rows], -1).reshape(
        seq_count, block_rows, 2 * model_width
    )

    def key_allowed(first_row, key_count):
        return ((first_row + jnp.arange(key_count, dtype=jnp.int32))[None, :] < lengths[:, None])[
            :, None, None, :
        ]

    def split_pairs(block_pairs):
        key_count = block_pairs.shape[1]
        key_heads = block_pairs[:, :, :model_width].reshape(seq_count, key_count, HEADS, head_size)
        value_heads = block_pairs[:, :, model_width:].reshape(
            seq_count, key_count, HEADS, head_size
        )
        return (key_heads, value_heads, key_count)

    def forward_step(carry_state, block_pairs, first_row):
        running_max, running_sum, running_acc = carry_state
        key_heads, value_heads, key_count = split_pairs(block_pairs)
        allowed = key_allowed(first_row, key_count)
        scores = (
            jnp.einsum(
                "sqhd,skhd->shqk", query_heads, key_heads, preferred_element_type=jnp.float32
            )
            * score_scale
        )
        scores = jnp.where(allowed, scores, masked_score)
        new_max = jnp.maximum(running_max, jnp.max(scores, -1))
        factor = jnp.exp(running_max - new_max)
        exponents = jnp.where(allowed, jnp.exp(scores - new_max[..., None]), 0.0)
        new_sum = running_sum * factor + jnp.sum(exponents, -1)
        update = jnp.einsum(
            "shqk,skhd->sqhd",
            exponents.astype(jnp.bfloat16),
            value_heads,
            preferred_element_type=jnp.float32,
        )
        new_acc = running_acc * jnp.transpose(factor, (0, 2, 1))[..., None] + update
        return (new_max, new_sum, new_acc)

    start_state = (
        jnp.full((seq_count, HEADS, block_rows), masked_score, jnp.float32),
        jnp.zeros((seq_count, HEADS, block_rows), jnp.float32),
        jnp.zeros((seq_count, block_rows, HEADS, head_size), jnp.float32),
    )
    running_max, running_sum, running_acc = over_blocks(
        forward_step, start_state, lax.all_gather(local_pairs, "ctx", axis=1, tiled=True)
    )
    context_full = running_acc / jnp.transpose(running_sum, (0, 2, 1))[..., None]
    log_total = running_max + jnp.log(running_sum)
    context = context_full.reshape(total_rows, model_width).astype(jnp.bfloat16)
    attended = product(context, full_out) + bias_out.astype(jnp.float32)
    residual = flat_rows.astype(jnp.float32) + attended
    normed, first_pull = jax.vjp(
        layer_norm, residual, gain_first.astype(jnp.float32), shift_first.astype(jnp.float32)
    )
    normed_low = normed.astype(jnp.bfloat16)
    expanded = product(normed_low, full_expand) + bias_expand.astype(jnp.float32)
    activated, gelu_pull = jax.vjp(partial(jax.nn.gelu, approximate=False), expanded)
    activated_low = activated.astype(jnp.bfloat16)
    reduced = product(activated_low, full_reduce) + bias_reduce.astype(jnp.float32)
    final_rows, second_pull = jax.vjp(
        layer_norm,
        normed + reduced,
        gain_second.astype(jnp.float32),
        shift_second.astype(jnp.float32),
    )
    layer_out = (final_rows * valid_rows).astype(jnp.bfloat16).reshape(inputs.shape)
    d_output = cotangent.reshape(total_rows, model_width).astype(jnp.float32) * valid_rows
    d_second, second_gain_grad, second_shift_grad = second_pull(d_output)
    d_reduced = d_second.astype(jnp.bfloat16)
    reduce_grad = outer_sum(activated_low, d_reduced)
    reduce_bias_grad = jnp.sum(d_reduced.astype(jnp.float32), 0)
    (d_expanded_full,) = gelu_pull(back_product(d_reduced, full_reduce))
    d_expanded = d_expanded_full.astype(jnp.bfloat16)
    expand_grad = outer_sum(normed_low, d_expanded)
    expand_bias_grad = jnp.sum(d_expanded.astype(jnp.float32), 0)
    d_normed = d_second + back_product(d_expanded, full_expand)
    d_first, first_gain_grad, first_shift_grad = first_pull(d_normed)
    d_attended = d_first.astype(jnp.bfloat16)
    out_grad = outer_sum(context, d_attended)
    out_bias_grad = jnp.sum(d_attended.astype(jnp.float32), 0)
    d_context = back_product(d_attended, full_out).astype(jnp.bfloat16)
    d_context_heads = d_context.reshape(seq_count, block_rows, HEADS, head_size)
    delta = jnp.transpose(
        jnp.sum(d_context_heads.astype(jnp.float32) * context_full, -1), (0, 2, 1)
    )
    whole_length = block_rows * lax.axis_size("ctx")

    def score_grads(key_heads, value_heads, allowed):
        scores = (
            jnp.einsum(
                "sqhd,skhd->shqk", query_heads, key_heads, preferred_element_type=jnp.float32
            )
            * score_scale
        )
        probabilities = jnp.where(allowed, jnp.exp(scores - log_total[..., None]), 0.0)
        d_probs = jnp.einsum(
            "sqhd,skhd->shqk", d_context_heads, value_heads, preferred_element_type=jnp.float32
        )
        d_scores = (probabilities * (d_probs - delta[..., None])).astype(jnp.bfloat16)
        return (probabilities, d_scores)

    def backward_step(carry_state, block_pairs, first_row):
        grad_query, grad_pairs = carry_state
        key_heads, value_heads, key_count = split_pairs(block_pairs)
        probabilities, d_scores = score_grads(
            key_heads, value_heads, key_allowed(first_row, key_count)
        )
        grad_query = (
            grad_query
            + jnp.einsum("shqk,skhd->sqhd", d_scores, key_heads, preferred_element_type=jnp.float32)
            * score_scale
        )
        key_part = (
            jnp.einsum("shqk,sqhd->skhd", d_scores, query_heads, preferred_element_type=jnp.float32)
            * score_scale
        )
        value_part = jnp.einsum(
            "shqk,sqhd->skhd",
            probabilities.astype(jnp.bfloat16),
            d_context_heads,
            preferred_element_type=jnp.float32,
        )
        fresh = jnp.concatenate(
            [
                key_part.reshape(seq_count, key_count, model_width),
                value_part.reshape(seq_count, key_count, model_width),
            ],
            -1,
        )
        before = lax.dynamic_slice_in_dim(grad_pairs, first_row, key_count, 1)
        grad_pairs = lax.dynamic_update_slice_in_dim(grad_pairs, before + fresh, first_row, 1)
        return (grad_query, grad_pairs)

    query_zero = jnp.zeros((seq_count, block_rows, HEADS, head_size), jnp.float32)
    back_state = (query_zero, jnp.zeros((seq_count, whole_length, 2 * model_width), jnp.float32))
    back_result = over_blocks(
        backward_step, back_state, lax.all_gather(local_pairs, "ctx", axis=1, tiled=True)
    )
    grad_query = back_result[0]
    own_pairs = lax.psum_scatter(
        back_result[1].astype(jnp.bfloat16), "ctx", scatter_dimension=1, tiled=True
    ).astype(jnp.float32)
    d_keys = own_pairs[:, :, :model_width].reshape(total_rows, model_width).astype(jnp.bfloat16)
    d_values = own_pairs[:, :, model_width:].reshape(total_rows, model_width).astype(jnp.bfloat16)
    d_queries = grad_query.reshape(total_rows, model_width).astype(jnp.bfloat16)
    query_grad = outer_sum(flat_rows, d_queries)
    query_bias_grad = jnp.sum(d_queries.astype(jnp.float32), 0)
    key_grad = outer_sum(flat_rows, d_keys)
    value_grad = outer_sum(flat_rows, d_values)
    value_bias_grad = jnp.sum(d_values.astype(jnp.float32), 0)
    input_grad = (
        d_first
        + back_product(d_queries, full_query)
        + back_product(d_keys, full_key)
        + back_product(d_values, full_value)
    ).reshape(inputs.shape)
    shares = (
        lax.psum_scatter(query_grad, ("fsdp", "ctx"), scatter_dimension=0, tiled=True),
        lax.psum_scatter(query_bias_grad, ("fsdp", "ctx"), scatter_dimension=0, tiled=True),
        lax.psum_scatter(key_grad, ("fsdp", "ctx"), scatter_dimension=0, tiled=True),
        lax.psum_scatter(value_grad, ("fsdp", "ctx"), scatter_dimension=0, tiled=True),
        lax.psum_scatter(value_bias_grad, ("fsdp", "ctx"), scatter_dimension=0, tiled=True),
        lax.psum_scatter(out_grad, ("fsdp", "ctx"), scatter_dimension=0, tiled=True),
        lax.psum_scatter(out_bias_grad, ("fsdp", "ctx"), scatter_dimension=0, tiled=True),
        lax.psum_scatter(first_gain_grad, ("fsdp", "ctx"), scatter_dimension=0, tiled=True),
        lax.psum_scatter(first_shift_grad, ("fsdp", "ctx"), scatter_dimension=0, tiled=True),
        lax.psum_scatter(expand_grad, ("fsdp", "ctx"), scatter_dimension=0, tiled=True),
        lax.psum_scatter(expand_bias_grad, ("fsdp", "ctx"), scatter_dimension=0, tiled=True),
        lax.psum_scatter(reduce_grad, ("fsdp", "ctx"), scatter_dimension=0, tiled=True),
        lax.psum_scatter(reduce_bias_grad, ("fsdp", "ctx"), scatter_dimension=0, tiled=True),
        lax.psum_scatter(second_gain_grad, ("fsdp", "ctx"), scatter_dimension=0, tiled=True),
        lax.psum_scatter(second_shift_grad, ("fsdp", "ctx"), scatter_dimension=0, tiled=True),
    )
    return (
        layer_out,
        input_grad,
        shares[0],
        shares[1],
        shares[2],
        shares[3],
        shares[4],
        shares[5],
        shares[6],
        shares[7],
        shares[8],
        shares[9],
        shares[10],
        shares[11],
        shares[12],
        shares[13],
        shares[14],
    )


def solution(mesh):
    return jax.shard_map(
        shards,
        mesh=mesh,
        in_specs=(
            P("fsdp", "ctx", None),
            P("fsdp"),
            P(("fsdp", "ctx"), None),
            P(("fsdp", "ctx")),
            P(("fsdp", "ctx"), None),
            P(("fsdp", "ctx"), None),
            P(("fsdp", "ctx")),
            P(("fsdp", "ctx"), None),
            P(("fsdp", "ctx")),
            P(("fsdp", "ctx")),
            P(("fsdp", "ctx")),
            P(("fsdp", "ctx"), None),
            P(("fsdp", "ctx")),
            P(("fsdp", "ctx"), None),
            P(("fsdp", "ctx")),
            P(("fsdp", "ctx")),
            P(("fsdp", "ctx")),
            P("fsdp", "ctx", None),
        ),
        out_specs=(
            P("fsdp", "ctx", None),
            P("fsdp", "ctx", None),
            P(("fsdp", "ctx"), None),
            P(("fsdp", "ctx")),
            P(("fsdp", "ctx"), None),
            P(("fsdp", "ctx"), None),
            P(("fsdp", "ctx")),
            P(("fsdp", "ctx"), None),
            P(("fsdp", "ctx")),
            P(("fsdp", "ctx")),
            P(("fsdp", "ctx")),
            P(("fsdp", "ctx"), None),
            P(("fsdp", "ctx")),
            P(("fsdp", "ctx"), None),
            P(("fsdp", "ctx")),
            P(("fsdp", "ctx")),
            P(("fsdp", "ctx")),
        ),
        check_vma=False,
    )
```

profile of v0, /device:TPU:0, one launch (start us, length us, event | category | flops | bytes accessed | tf_op | source)
XLA Modules:
  0.0 2520.5 jit_solution(15900603768348728788)
XLA Ops:
  16.2 42.4 %all-reduce.18 = (bf16[1024]{0:T(1024)(128)(2,1)S(1)}, bf16[1024]{0:T(1024)(128)(2,1)S(1)}, bf16[1024]{0:T(1024)(128)(2,1)S(1)}, bf16[1024]{0:T(1024)(128)(2,1)S...) all-reduce(bf16[1024]{0:T(1024)(128)(2,1)S(1)} %dynamic-update-slic, ...), channel_id=1, replica_groups=mesh['fsdp'=2,'ctx'=16] {'fsdp','ctx'}, use_global_device_ids=true, to_apply=%add.2 | all-reduce | flops 8192 | bytes 32768
  58.5 11.6 all-gather.9.cloned.1.call-done
  72.6 55.7 %all-gather.11.cloned.1.call-done = bf16[1024,1024]{1,0:T(8,128)(2,1)} async-done(((bf16[32,1024]{1,0:T(8,128)(2,1)}), bf16[1024,1024]{1,0:T(8,128)(2,1)}) %all-gather.11.cloned.1.call-update) | async-done | bytes 2097168 | tf_op jit(solution)/shard_map/all_gather | solution.py:69
  134.3 66.2 %all-gather = bf16[32,1,128]{2,1,0:T(2,128)(2,1)S(1)} all-gather(bf16[1,1,128]{2,1,0:T(2,128)(2,1)S(1)} %bitcast.215), channel_id=1, replica_groups=mesh['fsdp'=2,'ctx'=16] {'fsdp','ctx'}, dimensions={0}, use_global_device_ids=true | all-gather | bytes 8448 | tf_op jit(solution)/shard_map/all_gather | solution.py:76
  205.0 232.6 %all-gather.13.cloned.1.call-done = bf16[2,2048,2048]{1,2,0:T(8,128)(2,1)} async-done(((bf16[2,128,2048]{1,2,0:T(8,128)(2,1)}), bf16[2,2048,2048]{1,2,0:T(8,128)(2,1)}) %all-gather.13.cloned.1.call-update) | async-done | bytes 16777232 | tf_op jit(solution)/shard_map/all_gather | solution.py:160
  437.6 40.0 %while.34 = (s32[]{:T(128)}, f32[2,16,128]{2,1,0:T(8,128)S(1)}, f32[2,16,128]{2,1,0:T(8,128)S(1)}, f32[2,128,16,64]{1,3,2,0:T(8,128)}, s32[2]{0:T(128)S(1)}, /*i...) while((s32[]{:T(128)}, f32[2,16,128]{2,1,0:T(8,128)S(1)}, ...), condition=%wide.region_3.4_spmd.clone, body=%wide.region_0.3_spmd.clone.sunk | while | flops 564946432 | bytes 49029388 | solution.py:42
  481.1 13.8 all-gather.17.cloned.1.call-done
  497.9 76.3 %all-gather.19.cloned.1.call-done = bf16[1024,4096]{1,0:T(8,128)(2,1)} async-done(((bf16[32,4096]{1,0:T(8,128)(2,1)}), bf16[1024,4096]{1,0:T(8,128)(2,1)}) %all-gather.19.cloned.1.call-update) | async-done | bytes 8388624 | tf_op jit(solution)/shard_map/all_gather | solution.py:75
  574.1 16.4 multiply_convert_fusion.1
  590.5 62.5 %all-gather.21.cloned.1.call-done = bf16[4096,1024]{1,0:T(8,128)(2,1)} async-done(((bf16[128,1024]{1,0:T(8,128)(2,1)}), bf16[4096,1024]{1,0:T(8,128)(2,1)}) %all-gather.21.cloned.1.call-update) | async-done | bytes 8388624 | tf_op jit(solution)/shard_map/all_gather | solution.py:77
  653.1 6.6 fusion.63
  663.2 7.1 convert_reduce_fusion
  670.3 7.5 multiply_reduce_fusion.2
  683.8 11.3 broadcast_in_dim.133
  695.1 75.1 %while.35 = (s32[]{:T(128)}, f32[2,128,16,64]{1,3,2,0:T(8,128)S(1)}, f32[2,2048,2048]{1,2,0:T(8,128)}, bf16[2,2048,2048]{1,2,0:T(8,128)(2,1)}, s32[2]{0:T(128)S(...) while((s32[]{:T(128)}, ...), condition=%wide.region_14.15_spmd.clone, body=%wide.region_13.14_spmd.clone.sunk | while | flops 1369179648 | bytes 90234088 | solution.py:42
  707.4 6.6 fusion.151
  726.2 6.6 fusion.151
  744.9 6.5 fusion.151
  763.6 6.5 fusion.151
  770.1 17.5 convert_element_type.187
  787.6 41.7 %copy.76 = bf16[2,2048,2048]{2,0,1:T(2,128)(2,1)} copy(bf16[2,2048,2048]{1,2,0:T(8,128)(2,1)} %convert_element_type.187) | data formatting | bytes 33554432
  829.4 17.3 copy.88
  861.6 9.8 fusion.55
  873.1 8.1 fusion.66
  881.4 310.4 %reduce-scatter.22.cloned.1.call-done = bf16[128,4096]{1,0:T(8,128)(2,1)} async-done(((bf16[2048,4096]{1,0:T(8,128)(2,1)}), bf16[128,4096]{1,0:T(8,128)(2,1)}) %reduce-scatter.22.cloned.1.call-update) | async-done | bytes 1048592
  1217.0 47.6 %all-reduce.17 = (f32[1024]{0:T(1024)S(1)}, f32[1024]{0:T(1024)S(1)}, f32[1024]{0:T(1024)S(1)}, f32[1024]{0:T(1024)S(1)}, f32[1024]{0:T(1024)S(1)}, /*index=5*/f...) all-reduce(f32[1024]{0:T(1024)S(1)} %reduce_sum.219, ...), channel_id=4, replica_groups=mesh['fsdp'=2,'ctx'=16] {'fsdp','ctx'}, use_global_device_ids=true, to_apply=%region_18.19.clone | all-reduce | flops 12288 | bytes 98304
  1275.9 68.4 %reduce-scatter.16.cloned.1.call-done = f32[32,1024]{1,0:T(8,128)} async-done(((f32[1024,1024]{1,0:T(8,128)}), f32[32,1024]{1,0:T(8,128)}) %reduce-scatter.16.cloned.1.call-update) | async-done | bytes 131088 | tf_op jit(solution)/shard_map/reduce_scatter | solution.py:278
  1344.3 149.3 %reduce-scatter.24.cloned.1.call-done = f32[32,1024]{1,0:T(8,128)} async-done(((f32[1024,1024]{1,0:T(8,128)}), f32[32,1024]{1,0:T(8,128)}) %reduce-scatter.24.cloned.1.call-update) | async-done | bytes 131088
  1493.6 358.3 %reduce-scatter.18.cloned.1.call-done = f32[32,4096]{1,0:T(8,128)} async-done(((f32[1024,4096]{1,0:T(8,128)}), f32[32,4096]{1,0:T(8,128)}) %reduce-scatter.18.cloned.1.call-update) | async-done | bytes 524304 | tf_op jit(solution)/shard_map/reduce_scatter | solution.py:282
  1851.8 362.7 %reduce-scatter.20.cloned.1.call-done = f32[128,1024]{1,0:T(8,128)} async-done(((f32[4096,1024]{1,0:T(8,128)}), f32[128,1024]{1,0:T(8,128)}) %reduce-scatter.20.cloned.1.call-update) | async-done | bytes 524304 | tf_op jit(solution)/shard_map/reduce_scatter | solution.py:284
  2214.6 149.7 %reduce-scatter.26.cloned.1.call-done = f32[32,1024]{1,0:T(8,128)} async-done(((f32[1024,1024]{1,0:T(8,128)}), f32[32,1024]{1,0:T(8,128)}) %reduce-scatter.26.cloned.1.call-update) | async-done | bytes 131088
  2364.3 149.4 %reduce-scatter.28.cloned.1.call-done = f32[32,1024]{1,0:T(8,128)} async-done(((f32[1024,1024]{1,0:T(8,128)}), f32[32,1024]{1,0:T(8,128)}) %reduce-scatter.28.cloned.1.call-update) | async-done | bytes 131088
  (282 shorter events, 178.4 us)
Async XLA Ops:
  7.2 62.9 %all-gather.9.cloned.1.call-start = ((), (), s32[]{:S(2)}) async-start(), calls=%async_computation.7 | async-start | bytes 2162688 | tf_op jit(solution)/shard_map/all_gather | solution.py:68
  7.9 120.4 %all-gather.11.cloned.1.call-start = ((), (), s32[]{:S(2)}) async-start(), calls=%async_computation.8 | async-start | bytes 2162688 | tf_op jit(solution)/shard_map/all_gather | solution.py:69
  8.7 192.5 %all-gather.15.cloned.1.call-start = ((), (), s32[]{:S(2)}) async-start(), calls=%async_computation.10 | async-start | bytes 2162688 | tf_op jit(solution)/shard_map/all_gather | solution.py:66
  9.4 428.2 %all-gather.13.cloned.1.call-start = ((), (), s32[]{:S(2)}) async-start(), calls=%async_computation.9 | async-start | bytes 17825792 | tf_op jit(solution)/shard_map/all_gather | solution.py:160
  72.6 61.8 %copy-start.37 = (bf16[128]{0:T(256)(128)(2,1)S(1)}, bf16[128]{0:T(256)(128)(2,1)}, u32[]{:S(2)}) copy-start(bf16[128]{0:T(256)(128)(2,1)} %param.34) | copy-start | bytes 772
  72.6 127.9 %copy-start.23 = (s32[2]{0:T(128)S(1)}, s32[2]{0:T(128)}, u32[]{:S(2)}) copy-start(s32[2]{0:T(128)} %param.23) | copy-start | bytes 28
  72.6 128.6 %copy-start.4 = (bf16[2,128,1024]{2,1,0:T(8,128)(2,1)S(1)}, bf16[2,128,1024]{2,1,0:T(8,128)(2,1)}, u32[]{:S(2)}) copy-start(bf16[2,128,1024]{2,1,0:T(8,128)(2,1)} %param.22) | copy-start | bytes 1572868
  132.2 362.7 %all-gather.17.cloned.1.call-start = ((), (), s32[]{:S(2)}) async-start(), calls=%async_computation.11 | async-start | bytes 2162688 | tf_op jit(solution)/shard_map/all_gather | solution.py:71
  132.8 441.3 %all-gather.19.cloned.1.call-start = ((), (), s32[]{:S(2)}) async-start(), calls=%async_computation.12 | async-start | bytes 8650752 | tf_op jit(solution)/shard_map/all_gather | solution.py:75
  133.4 519.7 %all-gather.21.cloned.1.call-start = ((), (), s32[]{:S(2)}) async-start(), calls=%async_computation.13 | async-start | bytes 8650752 | tf_op jit(solution)/shard_map/all_gather | solution.py:77
  134.1 1057.7 %reduce-scatter.22.cloned.1.call-start = ((), (), s32[]{:S(2)}) async-start(), calls=%async_computation.17 | async-start | bytes 17825792
  134.2 543.6 %copy-start.19 = (f32[1024]{0:T(1024)}, f32[1024]{0:T(1024)S(1)}, u32[]{:S(2)}) copy-start(f32[1024]{0:T(1024)S(1)} %convert_element_type.167) | copy-start | bytes 12292
  134.3 518.8 %copy-start.21 = (f32[1024]{0:T(1024)}, f32[1024]{0:T(1024)S(1)}, u32[]{:S(2)}) copy-start(f32[1024]{0:T(1024)S(1)} %convert_element_type.168) | copy-start | bytes 12292
  497.5 180.3 %copy-start = (f32[256,1024]{1,0:T(8,128)}, f32[256,1024]{1,0:T(8,128)S(1)}, u32[]{:S(2)}) copy-start(f32[256,1024]{1,0:T(8,128)S(1)} %get-tuple-element.540) | copy-start | bytes 3145732
  497.6 180.3 %copy-start.24 = (f32[256]{0:T(256)}, f32[256]{0:T(256)S(1)}, u32[]{:S(2)}) copy-start(f32[256]{0:T(256)S(1)} %broadcast_multiply_fusion.1) | copy-start | bytes 3076
  497.8 180.0 %copy-start.26 = (f32[256]{0:T(256)}, f32[256]{0:T(256)S(1)}, u32[]{:S(2)}) copy-start(f32[256]{0:T(256)S(1)} %fusion.52) | copy-start | bytes 3076
  653.1 10.2 slice-start
  653.1 6.9 copy-start.9
  653.1 10.2 slice-start.1
  663.2 7.1 copy-start.12
  670.3 7.5 copy-start.16
  846.7 497.6 %reduce-scatter.16.cloned.1.call-start = ((), (), s32[]{:S(2)}) async-start(), calls=%async_computation.14 | async-start | bytes 4325376 | tf_op jit(solution)/shard_map/reduce_scatter | solution.py:278
  850.6 642.9 %reduce-scatter.24.cloned.1.call-start = ((), (), s32[]{:S(2)}) async-start(), calls=%async_computation.18 | async-start | bytes 4325376
  860.4 991.4 %reduce-scatter.18.cloned.1.call-start = ((), (), s32[]{:S(2)}) async-start(), calls=%async_computation.15 | async-start | bytes 17301504 | tf_op jit(solution)/shard_map/reduce_scatter | solution.py:282
  871.5 1343.1 %reduce-scatter.20.cloned.1.call-start = ((), (), s32[]{:S(2)}) async-start(), calls=%async_computation.16 | async-start | bytes 17301504 | tf_op jit(solution)/shard_map/reduce_scatter | solution.py:284
  881.3 1483.0 %reduce-scatter.26.cloned.1.call-start = ((), (), s32[]{:S(2)}) async-start(), calls=%async_computation.19 | async-start | bytes 4325376
  1202.8 1310.9 %reduce-scatter.28.cloned.1.call-start = ((), (), s32[]{:S(2)}) async-start(), calls=%async_computation.20 | async-start | bytes 4325376
  1211.8 5.2 copy-start.29
  1211.8 5.2 copy-start.30
  1211.8 5.2 copy-start.31
  1211.9 5.2 copy-start.35
  1211.9 5.2 copy-start.36
  (28 other events, 50.4 us)
Sparse Core Ops, SparseCore 0:
  10.9 59.1 all-gather.8
  73.0 55.3 all-gather.10
  131.2 55.2 all-gather.14
  189.1 248.4 all-gather.12
  440.3 54.5 all-gather.16
  497.7 76.3 all-gather.18
  577.0 76.0 all-gather.20
  846.8 344.9 reduce-scatter.21
  1194.7 149.5 reduce-scatter.15
  1347.0 146.5 reduce-scatter.23
  1496.4 355.3 reduce-scatter.17
  1854.5 359.9 reduce-scatter.19
  2217.4 146.8 reduce-scatter.25
  2367.0 146.6 reduce-scatter.27
where the time goes:
time: 2530 us; the launch traced here: 2520 us
  waiting for transfers between devices  2000 us (79%)
  blocking collectives  156 us (6%)
  matrix products  144 us (6%)
  local copies, waits for them, and re-layouts  133 us (5%)
  other arithmetic  66.6 us (3%)
    unnamed x18, waiting for transfers between devices  763 us
    reduce_scatter x1, waiting for transfers between devices, shards(): lax.psum_scatter(reduce_grad, ('fsdp', 'ctx'), scatter_dimension=0, tiled...  363 us
    reduce_scatter x1, waiting for transfers between devices, shards(): lax.psum_scatter(expand_grad, ('fsdp', 'ctx'), scatter_dimension=0, tiled...  358 us
    all_gather x1, waiting for transfers between devices, shards(): lax.all_gather(local_pairs, 'ctx', axis=1, tiled=True)  233 us
    unnamed x111, local copies, waits for them, and re-layouts  98 us
    unnamed x2, blocking collectives  90 us
    all_gather x1, waiting for transfers between devices, shards(): lax.all_gather(w_expand, ('fsdp', 'ctx'), axis=0, tiled=True)  76.3 us
    reduce_scatter x1, waiting for transfers between devices, shards(): lax.psum_scatter(out_grad, ('fsdp', 'ctx'), scatter_dimension=0, tiled=True)  68.4 us
  transfers between devices with their start and end apart: 14, of which 13 were waited for; matrix products, arithmetic and copies ran while one was open for 6% of the time, Pallas kernels for 0%

commit v1 on v0

--- a/solution.py
+++ b/solution.py
@@ -4,6 +4,8 @@
 import jax
 import jax.numpy as jnp
 from jax import lax
+from jax.experimental import pallas as pl
+from jax.experimental.pallas import tpu as pltpu
 from jax.sharding import PartitionSpec as P
 
 HEADS = 16
@@ -42,7 +44,7 @@
     return lax.fori_loop(0, key_count // block_width, turn, carry_state)
 
 
-def shards(
+def general_shards(
     inputs,
     lengths,
     w_query,
@@ -307,7 +309,519 @@
     )
 
 
+MESH = pl.DeviceIdType.MESH
+MIB = 1024*1024
+
+def place():
+    core = lax.axis_index("fsdp"); chip = lax.axis_index("ctx")
+    return core, chip
+
+def greet(peers):
+    barrier = pltpu.get_barrier_semaphore()
+    for peer in peers:
+        pl.semaphore_signal(barrier, inc=1, device_id=peer, device_id_type=MESH)
+    pl.semaphore_wait(barrier, len(peers))
+
+class Mover:
+    def __init__(self, send_sem, recv_sem):
+        self.send_sem, self.recv_sem, self.used, self.started = send_sem, recv_sem, 0, []
+    def make(self, src, dst, peer):
+        i = self.used; self.used += 1
+        return pltpu.make_async_remote_copy(src_ref=src, dst_ref=dst, send_sem=self.send_sem.at[i],
+            recv_sem=self.recv_sem.at[i], device_id=peer, device_id_type=MESH)
+
+def flip(v, bits):
+    for b in (1, 2, 4, 8):
+        if bits & b:
+            v = v + b - 2 * b * lax.rem(lax.div(v, b), 2)
+    return v
+
+def gather_kernel(count, *refs):
+    srcs, outs = refs[:count], refs[count:2*count]
+    send_sem, recv_sem, local_sem = refs[2*count:]
+    core, chip = place()
+    sib = (1 - core, chip)
+    at = lambda bits: (core, flip(chip, bits))
+    Z = (0, 4, 8, 12)
+    greet([sib, at(1), at(2), at(4), at(8), at(12)])
+    mine = lambda bits: core * 16 + flip(chip, bits)
+    theirs = lambda bits: (1 - core) * 16 + flip(chip, bits)
+    sems = {}
+    def sem_of(a, tag):
+        return sems.setdefault((a, tag), len(sems))
+    pending = []
+    def send(a, tag, src, dst, peer):
+        i = sem_of(a, tag)
+        c = pltpu.make_async_remote_copy(src_ref=src, dst_ref=dst, send_sem=send_sem.at[i], recv_sem=recv_sem.at[i], device_id=peer, device_id_type=MESH)
+        c.start(); pending.append(c)
+    def arrived(a, tag, dst):
+        i = sem_of(a, tag)
+        pltpu.make_async_remote_copy(src_ref=dst, dst_ref=dst, send_sem=send_sem.at[i], recv_sem=recv_sem.at[i], device_id=sib, device_id_type=MESH).wait_recv()
+    locals_ = []
+    for a in range(count):
+        o = outs[a].at[mine(0)]
+        for bits in (4, 8, 12):
+            send(a, ("z", bits), srcs[a], o, at(bits))
+        send(a, ("x", 0), srcs[a], o, at(1))
+        send(a, ("y", 0), srcs[a], o, at(2))
+        send(a, ("s", 0), srcs[a], o, sib)
+        c = pltpu.make_async_copy(srcs[a], o, local_sem.at[a]); c.start(); locals_.append(c)
+    for a in range(count):
+        for z in (4, 8, 12):
+            b = outs[a].at[mine(z)]
+            arrived(a, ("z", z), b)
+            send(a, ("x", z), b, b, at(1))
+            send(a, ("y", z), b, b, at(2))
+            send(a, ("s", z), b, b, sib)
+    for a in range(count):
+        half = srcs[a].shape[0] // 2
+        for z in Z:
+            b = outs[a].at[mine(z + 1)]
+            arrived(a, ("x", z), b)
+            h = outs[a].at[mine(z + 1), pl.ds(0, half)]
+            send(a, ("dy", z), h, h, at(2))
+            send(a, ("s", z + 1), b, b, sib)
+            b = outs[a].at[mine(z + 2)]
+            arrived(a, ("y", z), b)
+            h = outs[a].at[mine(z + 2), pl.ds(half, half)]
+            send(a, ("dx", z), h, h, at(1))
+            send(a, ("s", z + 2), b, b, sib)
+    for a in range(count):
+        half = srcs[a].shape[0] // 2
+        for z in Z:
+            b = outs[a].at[mine(z + 3)]
+            arrived(a, ("dy", z), outs[a].at[mine(z + 3), pl.ds(0, half)])
+            arrived(a, ("dx", z), outs[a].at[mine(z + 3), pl.ds(half, half)])
+            send(a, ("s", z + 3), b, b, sib)
+    for a in range(count):
+        for z in range(16):
+            arrived(a, ("s", z), outs[a].at[theirs(z)])
+    for c in pending:
+        c.wait_send()
+    for c in locals_:
+        c.wait()
+
+def gather_all(shards, collective_id):
+    n = len(shards)
+    hbm = pl.BlockSpec(memory_space=pl.ANY)
+    return pl.pallas_call(
+        partial(gather_kernel, n),
+        out_shape=[jax.ShapeDtypeStruct((32,) + s.shape, s.dtype) for s in shards],
+        in_specs=[hbm] * n, out_specs=[hbm] * n,
+        scratch_shapes=[pltpu.SemaphoreType.DMA((35 * n,)), pltpu.SemaphoreType.DMA((35 * n,)), pltpu.SemaphoreType.DMA((n,))],
+        compiler_params=pltpu.CompilerParams(collective_id=collective_id, has_side_effects=True),
+        name="gather_weights",
+    )(*shards)
+
+def exchange_kernel(count, *refs):
+    srcs, outs = refs[:count], refs[count:2*count]
+    send_sem, recv_sem, local_sem = refs[2*count:]
+    core, chip = place()
+    greet([(core, flip(chip, b)) for b in range(1, 16)])
+    copies = []
+    for a in range(count):
+        for b in ORDER:
+            i = a * 16 + b
+            to = flip(chip, b)
+            c = pltpu.make_async_remote_copy(src_ref=srcs[a].at[to], dst_ref=outs[a].at[chip], send_sem=send_sem.at[i], recv_sem=recv_sem.at[i], device_id=(core, to), device_id_type=MESH)
+            c.start(); copies.append((c, a, to, i))
+        c0 = pltpu.make_async_copy(srcs[a].at[chip], outs[a].at[chip], local_sem.at[a]); c0.start(); copies.append((c0, None, None, None))
+    for c, a, to, i in copies:
+        if a is None: c.wait()
+        else:
+            c.wait_send()
+            pltpu.make_async_remote_copy(src_ref=outs[a].at[to], dst_ref=outs[a].at[to], send_sem=send_sem.at[i], recv_sem=recv_sem.at[i], device_id=(core, to), device_id_type=MESH).wait_recv()
+ORDER = (12, 8, 4, 15, 11, 7, 14, 13, 10, 9, 6, 5, 3, 2, 1)
+
+def exchange(blocks, collective_id, space=pl.ANY):
+    n = len(blocks)
+    hbm = pl.BlockSpec(memory_space=space)
+    return pl.pallas_call(
+        partial(exchange_kernel, n),
+        out_shape=[jax.ShapeDtypeStruct(s.shape, s.dtype) for s in blocks],
+        in_specs=[hbm] * n, out_specs=[hbm] * n,
+        scratch_shapes=[pltpu.SemaphoreType.DMA((16 * n,)), pltpu.SemaphoreType.DMA((16 * n,)), pltpu.SemaphoreType.DMA((n,))],
+        compiler_params=pltpu.CompilerParams(collective_id=collective_id, has_side_effects=True),
+        name="exchange_heads",
+    )(*blocks)
+
+def scatter_kernel(count, *refs):
+    g, outs = refs[:count], refs[count:2*count]
+    first, second, third, passed = (refs[(2+i)*count:(3+i)*count] for i in range(4))
+    send_sem, recv_sem = refs[6*count:]
+    core, chip = place()
+    at = lambda bits: (core, flip(chip, bits))
+    greet([at(1), at(2), at(4), at(8), at(12)])
+    sems = {}; pending = []
+    def pair(a, tag, src, dst, peer):
+        i = sems.setdefault((a, tag), len(sems))
+        return pltpu.make_async_remote_copy(src_ref=src, dst_ref=dst, send_sem=send_sem.at[i], recv_sem=recv_sem.at[i], device_id=peer, device_id_type=MESH)
+    def send(a, tag, src, dst, peer):
+        c = pair(a, tag, src, dst, peer); c.start(); pending.append(c)
+    def arrived(a, tag, dst):
+        pair(a, tag, dst, dst, at(1)).wait_recv()
+    ORD = (12, 8, 4, 0)
+    def add(rows, fn):
+        step = min(rows, 16)
+        @pl.loop(0, rows // step)
+        def _(i):
+            fn(pl.ds(pl.multiple_of(i * step, step), step))
+    for a in range(count):
+        half = g[a].shape[1] // 2
+        lo, hi = pl.ds(0, half), pl.ds(half, half)
+        for k, z in enumerate(ORD):
+            diag = flip(chip, z + 3)
+            send(a, ("1a", k), g[a].at[diag, lo], first[a].at[k, 0], at(2))
+            send(a, ("1b", k), g[a].at[diag, hi], first[a].at[k, 1], at(1))
+        for k, z in enumerate(ORD):
+            send(a, ("2xh", k), g[a].at[flip(chip, z + 1), hi], second[a].at[k, 0, hi], at(1))
+            send(a, ("2yl", k), g[a].at[flip(chip, z + 2), lo], second[a].at[k, 1, lo], at(2))
+    for a in range(count):
+        half = g[a].shape[1] // 2
+        lo, hi = pl.ds(0, half), pl.ds(half, half)
+        for k, z in enumerate(ORD):
+            xb, yb = flip(chip, z + 1), flip(chip, z + 2)
+            arrived(a, ("1a", k), first[a].at[k, 0])
+            def f(rows, a=a, k=k, xb=xb):
+                first[a][k, 0, rows] = first[a][k, 0, rows] + g[a][xb, rows]
+            add(half, f)
+            send(a, ("2xl", k), first[a].at[k, 0], second[a].at[k, 0, lo], at(1))
+            arrived(a, ("1b", k), first[a].at[k, 1])
+            def f(rows, a=a, k=k, yb=yb, half=half):
+                first[a][k, 1, rows] = first[a][k, 1, rows] + g[a][yb, pl.ds(pl.multiple_of(rows.start + half, 8), rows.size)]
+            add(half, f)
+            send(a, ("2yh", k), first[a].at[k, 1], second[a].at[k, 1, hi], at(2))
+    for a in range(count):
+        full = g[a].shape[1]
+        half = full // 2
+        lo, hi = pl.ds(0, half), pl.ds(half, half)
+        for k, z in enumerate(ORD):
+            arrived(a, ("2xh", k), second[a].at[k, 0, hi])
+            arrived(a, ("2yl", k), second[a].at[k, 1, lo])
+            arrived(a, ("2xl", k), second[a].at[k, 0, lo])
+            arrived(a, ("2yh", k), second[a].at[k, 1, hi])
+            zb = flip(chip, z)
+            def f(rows, a=a, k=k, zb=zb):
+                total = g[a][zb, rows].astype(jnp.float32) + second[a][k, 0, rows].astype(jnp.float32) + second[a][k, 1, rows].astype(jnp.float32)
+                if k < 3: passed[a][k, rows] = total.astype(passed[a].dtype)
+                else: outs[a][rows] = total
+            add(full, f)
+            if k < 3:
+                send(a, ("3", k), passed[a].at[k], third[a].at[k], at(z))
+    for a in range(count):
+        for k in range(3):
+            arrived(a, ("3", k), third[a].at[k])
+        def f(rows, a=a):
+            outs[a][rows] = outs[a][rows] + third[a][0, rows].astype(jnp.float32) + third[a][1, rows].astype(jnp.float32) + third[a][2, rows].astype(jnp.float32)
+        add(g[a].shape[1], f)
+    for c in pending:
+        c.wait_send()
+
+def scatter_all(grads, collective_id):
+    n = len(grads)
+    v = pl.BlockSpec(memory_space=pltpu.VMEM)
+    sc = []
+    for lead, halve in (((4, 2), 1), ((4, 2), 0), ((3,), 0), ((3,), 0)):
+        for x in grads:
+            _, r, c = x.shape
+            sc.append(pltpu.VMEM(lead + ((r // 2) if halve else r, c), x.dtype))
+    return pl.pallas_call(
+        partial(scatter_kernel, n),
+        out_shape=[jax.ShapeDtypeStruct(x.shape[1:], jnp.float32) for x in grads],
+        in_specs=[v] * n, out_specs=[v] * n,
+        scratch_shapes=sc + [pltpu.SemaphoreType.DMA((27 * n,)), pltpu.SemaphoreType.DMA((27 * n,))],
+        compiler_params=pltpu.CompilerParams(collective_id=collective_id, has_side_effects=True, vmem_limit_bytes=60 * MIB),
+        name="scatter_grads",
+    )(*grads)
+
+
+LOG2E = math.log2(math.e)
+
+
+def lanes(rows, upper):
+    lane = lax.broadcasted_iota(jnp.int32, (rows, 128), 1)
+    return lane >= 64 if upper else lane < 64
+
+
+def nt(a, b):
+    return lax.dot_general(a, b, (((1,), (1,)), ((), ())), preferred_element_type=jnp.float32)
+
+
+def attend_kernel(blk, lengths_ref, r_ref, ctx_ref, full_ref, lse_ref, vt_ref):
+    q = pl.program_id(0)
+    total = r_ref.shape[0] * 128
+
+    @pl.when(q == 0)
+    def _():
+        vt_ref[...] = r_ref[:, 2].reshape(total, 128).T
+
+    rows = pl.ds(q * (blk // 128), blk // 128)
+    parts = []
+    for s in range(2):
+        pair = r_ref[:, s].reshape(total, 128)
+        mine = r_ref[rows, s].reshape(blk, 128)
+        query = jnp.where(lanes(blk, True), pltpu.roll(mine.astype(jnp.float32), 64, 1), 0.0).astype(jnp.bfloat16)
+        scores = nt(pair, query) * (0.125 * LOG2E)
+        key = lax.broadcasted_iota(jnp.int32, scores.shape, 0)
+        scores = jnp.where(key < lengths_ref[s], scores, masked_score)
+        top = jnp.max(scores, 0, keepdims=True)
+        e = jnp.exp2(scores - top)
+        mass = jnp.sum(e, 0, keepdims=True)
+        o = jnp.dot(vt_ref[...], e.astype(jnp.bfloat16), preferred_element_type=jnp.float32)
+        parts.append(o[64 * s : 64 * s + 64] / mass)
+        lse_ref[s, pl.ds(q, 1), :] = top + jnp.log2(mass)
+    out = jnp.concatenate(parts, 0).T
+    full_ref[...] = out
+    ctx_ref[...] = out.astype(jnp.bfloat16)
+
+
+def attend(lengths, blocks, blk=256):
+    chips = blocks.shape[0]
+    total = chips * 128
+    return pl.pallas_call(
+        partial(attend_kernel, blk),
+        grid=(total // blk,),
+        out_shape=[
+            jax.ShapeDtypeStruct((total, 128), jnp.bfloat16),
+            jax.ShapeDtypeStruct((total, 128), jnp.float32),
+            jax.ShapeDtypeStruct((2, total // blk, blk), jnp.float32),
+        ],
+        in_specs=[pl.BlockSpec(memory_space=pltpu.SMEM), pl.BlockSpec(memory_space=pltpu.VMEM)],
+        out_specs=[
+            pl.BlockSpec((blk, 128), lambda q: (q, 0)),
+            pl.BlockSpec((blk, 128), lambda q: (q, 0)),
+            pl.BlockSpec((2, total // blk, blk), lambda q: (0, 0, 0)),
+        ],
+        scratch_shapes=[pltpu.VMEM((128, total), jnp.bfloat16)],
+        compiler_params=pltpu.CompilerParams(vmem_limit_bytes=56 * MIB),
+        name="attend",
+    )(lengths, blocks)
+
+
+def attend_back_kernel(blk, lengths_ref, r_ref, d_ref, full_ref, lse_ref, out_ref, pair_t, acc, acc_v):
+    q = pl.program_id(0)
+    total = r_ref.shape[0] * 128
+
+    @pl.when(q == 0)
+    def _():
+        for s in range(2):
+            pair_t[s] = r_ref[:, s].reshape(total, 128).T
+        acc[...] = jnp.zeros_like(acc)
+        acc_v[...] = jnp.zeros_like(acc_v)
+
+    rows = pl.ds(q * (blk // 128), blk // 128)
+    span = pl.ds(pl.multiple_of(q * blk, blk), blk)
+    d_mine = d_ref[span]
+    product_t = (d_mine.astype(jnp.float32) * full_ref[span]).T
+    values = r_ref[:, 2].reshape(total, 128)
+    for s in range(2):
+        pair = r_ref[:, s].reshape(total, 128)
+        mine = r_ref[rows, s].reshape(blk, 128)
+        query = jnp.where(lanes(blk, True), pltpu.roll(mine.astype(jnp.float32), 64, 1), 0.0).astype(jnp.bfloat16)
+        d_half = jnp.where(lanes(blk, s == 1), d_mine.astype(jnp.float32), 0.0).astype(jnp.bfloat16)
+        delta = jnp.sum(product_t[64 * s : 64 * s + 64], 0, keepdims=True)
+        scores = nt(pair, query) * (0.125 * LOG2E)
+        key = lax.broadcasted_iota(jnp.int32, scores.shape, 0)
+        probs = jnp.where(key < lengths_ref[s], jnp.exp2(scores - lse_ref[s, pl.ds(q, 1), :]), 0.0)
+        d_probs = nt(values, d_half)
+        d_scores = (probs * (d_probs - delta)).astype(jnp.bfloat16)
+        acc_v[...] += jnp.dot(probs.astype(jnp.bfloat16), d_half, preferred_element_type=jnp.float32)
+        acc[s] += jnp.dot(d_scores, query, preferred_element_type=jnp.float32)
+        d_query = jnp.dot(pair_t[s], d_scores, preferred_element_type=jnp.float32)
+        acc[s, span] += jnp.concatenate([d_query[64:], jnp.zeros((64, blk), jnp.float32)], 0).T
+
+    @pl.when(q == pl.num_programs(0) - 1)
+    def _():
+        for s in range(2):
+            out_ref[:, s] = (acc[s] * 0.125).astype(jnp.bfloat16).reshape(total // 128, 128, 128)
+        out_ref[:, 2] = acc_v[...].astype(jnp.bfloat16).reshape(total // 128, 128, 128)
+
+
+def attend_back(lengths, blocks, d_context, full, lse, blk=256):
+    chips = blocks.shape[0]
+    total = chips * 128
+    v = pl.BlockSpec(memory_space=pltpu.VMEM)
+    return pl.pallas_call(
+        partial(attend_back_kernel, blk),
+        grid=(total // blk,),
+        out_shape=jax.ShapeDtypeStruct(blocks.shape, jnp.bfloat16),
+        in_specs=[pl.BlockSpec(memory_space=pltpu.SMEM), v, v, v, v],
+        out_specs=v,
+        scratch_shapes=[
+            pltpu.VMEM((2, 128, total), jnp.bfloat16),
+            pltpu.VMEM((2, total, 128), jnp.float32),
+            pltpu.VMEM((total, 128), jnp.float32),
+        ],
+        compiler_params=pltpu.CompilerParams(vmem_limit_bytes=56 * MIB),
+        name="attend_back",
+    )(lengths, blocks, d_context, full, lse)
+
+
+def swap(x):
+    return lax.ppermute(x, "fsdp", [(0, 1), (1, 0)])
+
+
+def pack_heads(rows, seqs, count):
+    return rows.reshape(seqs, count, HEADS, 64).transpose(2, 1, 0, 3).reshape(HEADS, count, seqs * 64)
+
+
+def unpack_heads(blocks, seqs, count):
+    return blocks.reshape(HEADS, count, seqs, 64).transpose(2, 1, 0, 3).reshape(seqs * count, HEADS * 64)
+
+
+def chip_sum(left, right):
+    core = lax.axis_index("fsdp")
+    h = left.shape[1] // 2
+    own = lax.dynamic_slice_in_dim(left, core * h, h, 1)
+    other = swap(lax.dynamic_slice_in_dim(left, (1 - core) * h, h, 1))
+    grad = outer_sum(own, right) + outer_sum(other, swap(right))
+    return grad.astype(jnp.bfloat16).reshape(16, h // 16, right.shape[1])
+
+
+def fast_shards(
+    inputs,
+    lengths,
+    w_query,
+    b_query,
+    w_key,
+    w_value,
+    b_value,
+    w_out,
+    b_out,
+    first_gain,
+    first_shift,
+    w_expand,
+    b_expand,
+    w_reduce,
+    b_reduce,
+    second_gain,
+    second_shift,
+    cotangent,
+):
+    core = lax.axis_index("fsdp")
+    f32, bf16 = jnp.float32, jnp.bfloat16
+    seqs, count, width = inputs.shape
+    total = seqs * count
+    part = width // 32
+    ff = w_expand.shape[1]
+    heads_of = lambda w: w.reshape(part, HEADS, 64)
+    qk = jnp.concatenate([heads_of(w_query), heads_of(w_key)], -1).reshape(part, 2 * width)
+    small = [b_query, b_value, b_out, first_gain, first_shift, b_expand, b_reduce, second_gain, second_shift]
+    sizes = [b.shape[0] for b in small]
+    vec = jnp.concatenate(small + [jnp.zeros((part * 128 - sum(sizes),), bf16)]).reshape(part, 128)
+    g_qkv, g_vec, g_out, g_expand, g_reduce = gather_all(
+        [jnp.concatenate([qk, w_value], 1), vec, w_out, w_expand, w_reduce], 1
+    )
+    full_qkv = g_qkv.reshape(width, 3 * width)
+    full_out = g_out.reshape(width, width)
+    full_expand = g_expand.reshape(width, ff)
+    full_reduce = g_reduce.reshape(ff, width)
+    flat_vec = g_vec.reshape(32, part * 128)
+    offsets = [sum(sizes[:i]) for i in range(len(sizes) + 1)]
+    (bias_query, bias_value, bias_out, gain_first, shift_first, bias_expand, bias_reduce, gain_second, shift_second) = [
+        flat_vec[:, offsets[i] : offsets[i + 1]].reshape(-1).astype(f32) for i in range(len(sizes))
+    ]
+    own_first = lax.axis_index("ctx") * count
+    positions = own_first + jnp.arange(count, dtype=jnp.int32)
+    valid_rows = (positions[None, :] < lengths[:, None]).astype(f32).reshape(total, 1)
+    flat_rows = inputs.reshape(total, width)
+    bias_qk = jnp.concatenate([bias_query.reshape(HEADS, 64), jnp.zeros((HEADS, 64), f32)], 1).reshape(-1)
+    qkv = (product(flat_rows, full_qkv) + jnp.concatenate([bias_qk, bias_value])).astype(bf16)
+    blocks = jnp.concatenate(
+        [
+            qkv[:, : 2 * width].reshape(seqs, count, HEADS, 128).transpose(2, 0, 1, 3),
+            pack_heads(qkv[:, 2 * width :], seqs, count)[:, None],
+        ],
+        1,
+    )
+    (blocks,) = exchange([blocks], 2)
+    context_head, full_head, lse = attend(lengths, blocks)
+    (context_blocks,) = exchange([context_head.reshape(16, count, 128)], 3)
+    context = unpack_heads(context_blocks, seqs, count)
+    attended = product(context, full_out) + bias_out
+    residual = flat_rows.astype(f32) + attended
+    normed, first_pull = jax.vjp(layer_norm, residual, gain_first, shift_first)
+    normed_low = normed.astype(bf16)
+    expanded = product(normed_low, full_expand) + bias_expand
+    activated, gelu_pull = jax.vjp(partial(jax.nn.gelu, approximate=False), expanded)
+    activated_low = activated.astype(bf16)
+    reduced = product(activated_low, full_reduce) + bias_reduce
+    final_rows, second_pull = jax.vjp(layer_norm, normed + reduced, gain_second, shift_second)
+    layer_out = (final_rows * valid_rows).astype(bf16).reshape(inputs.shape)
+    d_output = cotangent.reshape(total, width).astype(f32) * valid_rows
+    d_second, second_gain_grad, second_shift_grad = second_pull(d_output)
+    d_reduced = d_second.astype(bf16)
+    reduce_grad = chip_sum(activated_low, d_reduced)
+    reduce_bias_grad = jnp.sum(d_reduced.astype(f32), 0)
+    (d_expanded_full,) = gelu_pull(back_product(d_reduced, full_reduce))
+    d_expanded = d_expanded_full.astype(bf16)
+    expand_grad = chip_sum(normed_low, d_expanded)
+    expand_bias_grad = jnp.sum(d_expanded.astype(f32), 0)
+    d_normed = d_second + back_product(d_expanded, full_expand)
+    d_first, first_gain_grad, first_shift_grad = first_pull(d_normed)
+    d_attended = d_first.astype(bf16)
+    out_grad = chip_sum(context, d_attended)
+    out_bias_grad = jnp.sum(d_attended.astype(f32), 0)
+    d_context = back_product(d_attended, full_out).astype(bf16)
+    (d_blocks,) = exchange([pack_heads(d_context, seqs, count)], 4)
+    d_heads = attend_back(lengths, blocks, d_blocks.reshape(16 * count, 128), full_head, lse)
+    (d_heads,) = exchange([d_heads], 5)
+    d_qk = d_heads[:, :2].transpose(1, 2, 0, 3).reshape(total, 2 * width)
+    d_qkv = jnp.concatenate([d_qk, unpack_heads(d_heads[:, 2], seqs, count)], 1)
+    qkv_grad = chip_sum(flat_rows, d_qkv)
+    input_grad = (d_first + back_product(d_qkv, full_qkv)).reshape(inputs.shape)
+    qkv_bias_grad = jnp.sum(d_qkv.astype(f32), 0)
+    query_bias_grad = qkv_bias_grad[: 2 * width].reshape(HEADS, 128)[:, :64].reshape(-1)
+    value_bias_grad = qkv_bias_grad[2 * width :]
+    small_grads = jnp.concatenate(
+        [
+            g.reshape(32, -1)
+            for g in (
+                query_bias_grad,
+                value_bias_grad,
+                out_bias_grad,
+                first_gain_grad,
+                first_shift_grad,
+                expand_bias_grad,
+                reduce_bias_grad,
+                second_gain_grad,
+                second_shift_grad,
+            )
+        ]
+        + [jnp.zeros((32, 2048 - sum(sizes)), f32)],
+        1,
+    ).reshape(2, 16, 16, 128)
+    vec_grad = lax.dynamic_index_in_dim(small_grads, core, 0, False) + swap(
+        lax.dynamic_index_in_dim(small_grads, 1 - core, 0, False)
+    )
+    s_reduce, s_expand, s_out, s_vec, s_qkv = scatter_all([reduce_grad, expand_grad, out_grad, vec_grad, qkv_grad], 6)
+    s_qk = s_qkv[:, : 2 * width].reshape(part, HEADS, 128)
+    s_vec = s_vec.reshape(-1)
+    v = [s_vec[offsets[i] : offsets[i + 1]] for i in range(len(sizes))]
+    return (
+        layer_out,
+        input_grad,
+        s_qk[:, :, :64].reshape(part, width),
+        v[0],
+        s_qk[:, :, 64:].reshape(part, width),
+        s_qkv[:, 2 * width :],
+        v[1],
+        s_out,
+        v[2],
+        v[3],
+        v[4],
+        s_expand,
+        v[5],
+        s_reduce,
+        v[6],
+        v[7],
+        v[8],
+    )
+
+
 def solution(mesh):
+    fast = mesh.shape["fsdp"] == 2 and mesh.shape["ctx"] == HEADS
+    shards = fast_shards if fast else general_shards
     return jax.shard_map(
         shards,
         mesh=mesh,

time: 2530 us -> 592 us (0.23)
  waiting for transfers between devices: 2000 us -> 0.02 us
  Pallas kernels: 0 us -> 442 us
  blocking collectives: 156 us -> 0 us
  local copies, waits for them, and re-layouts: 133 us -> 41.4 us
  other arithmetic: 66.6 us -> 8.43 us
  matrix products: 144 us -> 91 us
    reduce_scatter x3 -> x0, waiting for transfers between devices: 789 us -> none  [the longest x1 363 us: shards(): lax.psum_scatter(reduce_grad, ('fsdp', 'ctx'), scatter_dimension=0, tiled...]
    unnamed x18 -> x0, waiting for transfers between devices: 763 us -> none
    all_gather x7 -> x0, waiting for transfers between devices: 453 us -> none  [the longest x1 233 us: shards(): lax.all_gather(local_pairs, 'ctx', axis=1, tiled=True)]
    pallas_call x0 -> x8, Pallas kernels: none -> 442 us  [the longest x1 153 us: scatter_all(): pl.pallas_call(partial(scatter_kernel, n), out_shape=[jax.ShapeDtypeStruc...]
    unnamed x2 -> x0, blocking collectives: 90 us -> none
    unnamed x111 -> x48, local copies, waits for them, and re-layouts: 98 us -> 8.87 us
    all_gather x1 -> x0, blocking collectives: 66.2 us -> none  [shards(): lax.all_gather(b_expand, ('fsdp', 'ctx'), axis=0, tiled=True)]
    dot_general x28 -> x0, matrix products: 57.5 us -> none  [the longest x4 12.5 us: score_grads(): jnp.einsum('sqhd,skhd->shqk', d_context_heads, value_heads, preferred_ele...]
  transfers between devices with their start and end apart: 14 -> 9, of which waited for: 13 -> 0; matrix products, arithmetic and copies ran while one was open for 6% -> 14% of each run, Pallas kernels for 0% -> 14%
where the time goes in v1:
time: 592 us; the launch traced here: 586 us
  Pallas kernels  442 us (75%)
  matrix products  91 us (15%)
  local copies, waits for them, and re-layouts  41.4 us (7%)
  other arithmetic  8.43 us (1%)
    pallas_call x1, Pallas kernels, scatter_all(): pl.pallas_call(partial(scatter_kernel, n), out_shape=[jax.ShapeDtypeStruc...  153 us
    pallas_call x1, Pallas kernels, gather_all(): pl.pallas_call(partial(gather_kernel, n), out_shape=[jax.ShapeDtypeStruct...  121 us
    pallas_call x4, Pallas kernels, exchange(): pl.pallas_call(partial(exchange_kernel, n), out_shape=[jax.ShapeDtypeStru...  116 us
    dot_general x8, matrix products, outer_sum(): jnp.einsum('rd,re->de', left, right, preferred_element_type=jnp.float32)  36.3 us
    dot_general x4, matrix products, product(): return jnp.dot(left, right, preferred_element_type=jnp.float32)  30 us
    pallas_call x1, Pallas kernels, attend_back(): pl.pallas_call(partial(attend_back_kernel, blk), grid=(total // blk,), ou...  26.2 us
    pallas_call x1, Pallas kernels, attend(): pl.pallas_call(partial(attend_kernel, blk), grid=(total // blk,), out_sha...  25.8 us
    dot_general x4, matrix products, back_product(): jnp.einsum('re,de->rd', grad_rows, weight, preferred_element_type=jnp.flo...  24.7 us
  transfers between devices with their start and end apart: 9, of which 0 were waited for; matrix products, arithmetic and copies ran while one was open for 14% of the time, Pallas kernels for 14%

profile of v1, /device:TPU:0, one launch (start us, length us, event | category | flops | bytes accessed | tf_op | source)
XLA Modules:
  0.0 586.2 jit_solution(9808926714257696076)
XLA Ops:
  2.8 1.5 pad_maximum_fusion.1.refs_0_
  4.4 6.7 %concatenate.29 = bf16[4096]{0:T(1024)(128)(2,1)} concatenate(bf16[32]{0:T(256)(128)(2,1)} %param.21, bf16[32]{0:T(256)(128)(2,1)} %param.24, bf16[32]{0:T(256)(128)(2,1)} %param.26, bf16[32]{0:T(256)(128)(2,1)} %param.27, bf16[32]{0:T(256)(128)(2,1)} %param.28, bf16[128]{0:T(256)(128)(2,1)} %param.30, bf16[32]{0:T(256)(128)(2,1)} %param.32, bf16[32]{0:T(256)(128)(2,1)} %param.33, ...), dimensions={0} | concatenate | bytes 16384 | tf_op jit(solution)/shard_map/concatenate | solution.py:711
  11.0 120.7 %gather_weights.1 = (bf16[32,32,3072]{2,1,0:T(8,128)(2,1)}, bf16[32,32,128]{2,1,0:T(8,128)(2,1)}, bf16[32,32,1024]{2,1,0:T(8,128)(2,1)}, bf16[32,32,4096]{2,1,0:T(8,128)(2,1)}, bf16[32,128,1024]{2,1,0:T(8,128)(2,1)}) custom-call(bf16[32,3072]{1,0:T(8,128)(2,1)} %pad_maximum_fusion.1.refs_0_, bf16[32,128]{1,0:T(8,128)(2,1)} %bitcast.159, ...), custom_call_target="tpu_custom_call" | custom-call | tf_op jit(solution)/shard_map/gather_weights/pallas_call | solution.py:407
  133.1 5.0 fusion.7
  141.6 45.3 %exchange_heads.4.r_ref = bf16[16,3,128,128]{3,2,1,0:T(8,128)(2,1)} custom-call(bf16[16,3,128,128]{3,2,1,0:T(8,128)(2,1)} %pad_maximum_fusion.refs_0_), custom_call_target="tpu_custom_call" | custom-call | tf_op jit(solution)/shard_map/exchange_heads/pallas_call | solution.py:439
  186.8 25.8 %attend.1 = (bf16[2048,128]{1,0:T(8,128)(2,1)}, f32[2048,128]{1,0:T(8,128)}, f32[2,8,256]{2,1,0:T(8,128)}) custom-call(s32[2]{0:T(128)} %lengths_ref.3, bf16[16,3,128,128]{3,2,1,0:T(8,128)(2,1)} %exchange_heads.4.r_ref), custom_call_target="tpu_custom_call" | custom-call | tf_op jit(solution)/shard_map/attend/pallas_call | solution.py:581
  212.7 16.1 %exchange_heads.5 = bf16[16,128,128]{2,1,0:T(8,128)(2,1)} custom-call(bf16[16,128,128]{2,1,0:T(8,128)(2,1)} %bitcast.154), custom_call_target="tpu_custom_call" | custom-call | tf_op jit(solution)/shard_map/exchange_heads/pallas_call | solution.py:439
  230.8 2.4 fusion.33
  233.8 16.1 %multiply_convert_fusion = (bf16[256,4096]{1,0:T(8,128)(2,1)S(1)}, f32[256,4096]{1,0:T(8,128)}, f32[256,4096]{1,0:T(8,128)}) fusion(f32[4096]{0:T(1024)S(1)} %fusion.20, bf16[256,1024]{1,0:T(8,128)(2,1)S(1)} %fusion.13, bf16[1024,4096]{1,0:T(8,128)(2,1)} %bitcast.164), kind=kOutput, calls=%fused_computation.8 | convolution fusion | flops 2216689664 | bytes 19415040 | tf_op jit(solution)/shard_map/dot_general | solution.py:25
  252.4 6.5 %fusion.34 = (f32[256]{0:T(256)S(1)}, f32[256,1024]{1,0:T(8,128)S(1)}) fusion(f32[1024]{0:T(1024)S(1)} %reshape.376, bf16[256,4096]{1,0:T(8,128)(2,1)} %copy-done.2, bf16[4096,1024]{1,0:T(8,128)(2,1)} %bitcast.168, f32[1024]{0:T(1024)S(1)} %reshape.374, f32[1024]{0:T(1024)S(1)} %reshape.373, f32[256]{0:T(256)S(1)} %fusion.25, ...), kind=kOutput, calls=%fused_computation.109 | convolution fusion | flops 2149318400 | bytes 12598272 | tf_op jit(solution)/shard_map/dot_general | solution.py:25
  261.5 12.7 %convert_reduce_fusion = (f32[4096]{0:T(1024)S(1)}, bf16[256,4096]{1,0:T(8,128)(2,1)}) fusion(f32[256,4096]{1,0:T(8,128)} %get-tuple-element.59, f32[256,4096]{1,0:T(8,128)} %get-tuple-element.83, bf16[256,1024]{1,0:T(8,128)(2,1)S(1)} %get-tuple-element.49, bf16[4096,1024]{1,0:T(8,128)(2,1)} %bitcast.169), kind=kOutput, calls=%fused_computation.6 | convolution fusion | flops 2164256768 | bytes 19415040 | tf_op jit(solution)/shard_map/re,de->rd/dot_general | solution.py:33
  274.6 4.4 multiply_reduce_fusion.2
  281.1 1.8 convolution_convert_fusion
  284.4 17.2 %exchange_heads.6 = bf16[16,128,128]{2,1,0:T(8,128)(2,1)} custom-call(bf16[16,128,128]{2,1,0:T(8,128)(2,1)} %copy.45.refs_0_), custom_call_target="tpu_custom_call" | custom-call | tf_op jit(solution)/shard_map/exchange_heads/pallas_call | solution.py:439
  301.6 26.2 %attend_back.1.refs_0_ = bf16[16,3,128,128]{3,2,1,0:T(8,128)(2,1)} custom-call(s32[2]{0:T(128)} %lengths_ref.3, bf16[16,3,128,128]{3,2,1,0:T(8,128)(2,1)} %exchange_heads.4.r_ref, bf16[2048,128]{1,0:T(8,128)(2,1)} %bitcast.143, f32[2048,128]{1,0:T(8,128)} %get-tuple-element.36.full_ref, f32[2,8,256]{2,1,0:T(8,128)} %get-tuple-element.37.lse_ref), custom_call_target="tpu_custom_call" | custom-call | tf_op jit(solution)/shard_map/attend_back/pallas_call | solution.py:644
  327.8 37.9 %exchange_heads.7 = bf16[16,3,128,128]{3,2,1,0:T(8,128)(2,1)} custom-call(bf16[16,3,128,128]{3,2,1,0:T(8,128)(2,1)} %attend_back.1.refs_0_), custom_call_target="tpu_custom_call" | custom-call | tf_op jit(solution)/shard_map/exchange_heads/pallas_call | solution.py:439
  369.0 2.7 copy.52
  371.7 2.1 reshape.382
  376.4 5.8 convolution_add_fusion.3
  382.2 6.2 %fusion.18 = f32[512,4096]{1,0:T(8,128)} fusion(bf16[256,4096]{1,0:T(8,128)(2,1)} %get-tuple-element.51, bf16[256,1024]{1,0:T(8,128)(2,1)S(1)} %copy-done.7, s32[]{:T(128)S(6)} %select_n.25), kind=kOutput, calls=%fused_computation.64 | convolution fusion | flops 1073741824 | bytes 10747908 | tf_op jit(solution)/shard_map/rd,re->de/dot_general | solution.py:29
  388.4 3.7 fusion.14
  392.0 5.9 fusion.10
  399.6 1.6 fusion.16
  402.5 2.6 add_convert_fusion.4
  405.6 7.3 %add_convert_fusion.1 = bf16[2048,1024]{1,0:T(8,128)(2,1)} fusion(f32[2048,1024]{1,0:T(8,128)} %fusion.10, bf16[256,2048]{1,0:T(8,128)(2,1)} %collective-permute-done, bf16[256,1024]{1,0:T(8,128)(2,1)S(1)} %collective-permute-done.1), kind=kOutput, calls=%fused_computation.1 | convolution fusion | flops 1077936128 | bytes 14155776 | tf_op jit(solution)/shard_map/rd,re->de/dot_general | solution.py:29
  412.9 4.2 add_convert_fusion.2
  417.2 4.9 add_convert_fusion
  422.0 152.6 %scatter_grads.1 = (f32[128,1024]{1,0:T(8,128)}, f32[32,4096]{1,0:T(8,128)}, f32[32,1024]{1,0:T(8,128)}, f32[16,128]{1,0:T(8,128)}, f32[32,3072]{1,0:T(8,128)}) custom-call(bf16[16,128,1024]{2,1,0:T(8,128)(2,1)} %bitcast.126, bf16[16,32,4096]{2,1,0:T(8,128)(2,1)} %bitcast.127, bf16[16,32,1024]{2,1,0:T(8,128)(2,1)} %bitcast.132, ...), custom_call_target="tpu_custom_call" | custom-call | tf_op jit(solution)/shard_map/scatter_grads/pallas_call | solution.py:528
  575.6 1.6 slice.126
  577.2 1.6 fusion.32
  581.8 1.6 copy.74
  583.4 1.9 copy.75
  (145 shorter events, 32.5 us)
Async XLA Ops:
  141.6 89.2 %copy-start.3 = (bf16[2,128,1024]{2,1,0:T(8,128)(2,1)S(1)}, bf16[2,128,1024]{2,1,0:T(8,128)(2,1)}, u32[]{:S(2)}) copy-start(bf16[2,128,1024]{2,1,0:T(8,128)(2,1)} %param.18) | copy-start | bytes 1572868
  233.8 16.1 %copy-start.6 = (bf16[256,1024]{1,0:T(8,128)(2,1)}, bf16[256,1024]{1,0:T(8,128)(2,1)S(1)}, u32[]{:S(2)}) copy-start(bf16[256,1024]{1,0:T(8,128)(2,1)S(1)} %fusion.13) | copy-start | bytes 1572868
  233.8 18.6 %copy-start.12 = (s32[2]{0:T(128)S(1)}, s32[2]{0:T(128)}, u32[]{:S(2)}) copy-start(s32[2]{0:T(128)} %lengths_ref.3) | copy-start | bytes 28
  249.9 1.3 copy-start.2
  252.3 153.4 %collective-permute-start = (bf16[256,2048]{1,0:T(8,128)(2,1)}, bf16[256,2048]{1,0:T(8,128)(2,1)}, u32[]{:S(2)}, u32[]{:S(2)}) collective-permute-start(bf16[256,2048]{1,0:T(8,128)(2,1)} %constant_dynamic-slice_fusion.3), channel_id=1, source_target_pairs={{0,16},{16,0},{1,17},{17,1},{2,18},{18,2},{3,19},{19,3},{4,20},{20... | collective-permute-start | bytes 3145736 | tf_op jit(solution)/shard_map/ppermute | solution.py:661
  252.4 6.9 %copy-start = (bf16[2,128,1024]{2,1,0:T(8,128)(2,1)S(1)}, bf16[2,128,1024]{2,1,0:T(8,128)(2,1)}, u32[]{:S(2)}) copy-start(bf16[2,128,1024]{2,1,0:T(8,128)(2,1)} %param.35) | copy-start | bytes 1572868
  259.9 14.7 %slice-start.5 = ((s8[8388608]{0:T(1024)(128)(4,1)}), s8[4194304]{0:T(1024)(128)(4,1)S(1)}, s32[]{:S(2)}) async-start(s8[8388608]{0:T(1024)(128)(4,1)} %bitcast.165), calls=%async_computation.5 | async-start | bytes 8388608
  261.4 12.7 %copy-start.8 = (bf16[256,1024]{1,0:T(8,128)(2,1)}, bf16[256,1024]{1,0:T(8,128)(2,1)S(1)}, u32[]{:S(2)}) copy-start(bf16[256,1024]{1,0:T(8,128)(2,1)S(1)} %get-tuple-element.49) | copy-start | bytes 1572868
  261.4 13.2 %slice-start.6 = ((s8[8388608]{0:T(1024)(128)(4,1)}), s8[4194304]{0:T(1024)(128)(4,1)S(1)}, s32[]{:S(2)}) async-start(s8[8388608]{0:T(1024)(128)(4,1)} %bitcast.165), calls=%async_computation.6 | async-start | bytes 8388608
  274.1 143.0 %collective-permute-start.3 = (bf16[256,4096]{1,0:T(8,128)(2,1)}, bf16[256,4096]{1,0:T(8,128)(2,1)}, u32[]{:S(2)}, u32[]{:S(2)}) collective-permute-start(bf16[256,4096]{1,0:T(8,128)(2,1)} %get-tuple-element.51), channel_id=1, source_target_pairs={{0,16},{16,0},{1,17},{17,1},{2,18},{18,2},{3,19},{19,3},{4,20},{20... | collective-permute-start | bytes 6291464 | tf_op jit(solution)/shard_map/ppermute | solution.py:661
  279.0 2.1 copy-start.5
  279.4 5.0 copy-start.1
  280.4 122.1 %collective-permute-start.5 = (bf16[256,1024]{1,0:T(8,128)(2,1)}, bf16[256,1024]{1,0:T(8,128)(2,1)}, u32[]{:S(2)}, u32[]{:S(2)}) collective-permute-start(bf16[256,1024]{1,0:T(8,128)(2,1)} %get-tuple-element.53), channel_id=1, source_target_pairs={{0,16},{16,0},{1,17},{17,1},{2,18},{18,2},{3,19},{19,3},{4,20},{20... | collective-permute-start | bytes 1572872 | tf_op jit(solution)/shard_map/ppermute | solution.py:661
  365.7 2.3 slice-start.4
  373.9 39.0 %collective-permute-start.8 = (bf16[256,3072]{1,0:T(8,128)(2,1)S(1)}, bf16[256,3072]{1,0:T(8,128)(2,1)}, u32[]{:S(2)}, u32[]{:S(2)}) collective-permute-start(bf16[256,3072]{1,0:T(8,128)(2,1)S(1)} %constant_dynamic-update-slice_fusion), channel_id=1, source_target_pairs={{0,16},{16,0},{1,17},{17,1},{2,18},{18,2},{3,19},{19,3},{4,20},{20... | collective-permute-start | bytes 4718600 | tf_op jit(solution)/shard_map/ppermute | solution.py:661
  375.9 6.3 %copy-start.7 = (bf16[256,1024]{1,0:T(8,128)(2,1)S(1)}, bf16[256,1024]{1,0:T(8,128)(2,1)}, u32[]{:S(2)}) copy-start(bf16[256,1024]{1,0:T(8,128)(2,1)} %copy-done.6) | copy-start | bytes 1572868
  375.9 23.6 %collective-permute-start.6 = (f32[16,16,128]{2,1,0:T(8,128)}, f32[16,16,128]{2,1,0:T(8,128)S(1)}, u32[]{:S(2)}, u32[]{:S(2)}) collective-permute-start(f32[16,16,128]{2,1,0:T(8,128)} %dynamic-slice_bitcast_fusion), channel_id=1, source_target_pairs={{0,16},{16,0},{1,17},{17,1},{2,18},{18,2},{3,19},{19,3},{4,20},{20... | collective-permute-start | bytes 393224 | tf_op jit(solution)/shard_map/ppermute | solution.py:661
  382.2 6.2 %copy-start.4 = (bf16[2,128,1024]{2,1,0:T(8,128)(2,1)S(1)}, bf16[2,128,1024]{2,1,0:T(8,128)(2,1)}, u32[]{:S(2)}) copy-start(bf16[2,128,1024]{2,1,0:T(8,128)(2,1)} %param.18) | copy-start | bytes 1572868
  398.6 2.6 copy-start.9
  399.4 5.7 copy-start.11
  399.5 1.8 collective-permute-start.4
  399.6 13.3 %slice-start.2 = ((s8[6291456]{0:T(1024)(128)(4,1)}), s8[4194304]{0:T(1024)(128)(4,1)S(1)}, s32[]{:S(2)}) async-start(s8[6291456]{0:T(1024)(128)(4,1)} %bitcast.124), calls=%async_computation.2 | async-start | bytes 8388608
  401.3 3.9 collective-permute-start.1
  402.4 14.7 %collective-permute-start.2 = (bf16[256,512]{1,0:T(8,128)(2,1)}, bf16[256,512]{1,0:T(8,128)(2,1)S(1)}, u32[]{:S(2)}, u32[]{:S(2)}) collective-permute-start(bf16[256,512]{1,0:T(8,128)(2,1)} %constant_dynamic-slice_fusion.2), channel_id=1, source_target_pairs={{0,16},{16,0},{1,17},{17,1},{2,18},{18,2},{3,19},{19,3},{4,20},{20... | collective-permute-start | bytes 786440 | tf_op jit(solution)/shard_map/ppermute | solution.py:661
  402.5 14.6 %slice-start = ((s8[8388608]{0:T(1024)(128)(4,1)}), s8[4194304]{0:T(1024)(128)(4,1)S(1)}, s32[]{:S(2)}) async-start(s8[8388608]{0:T(1024)(128)(4,1)} %bitcast.122), calls=%async_computation | async-start | bytes 8388608
  405.1 7.8 %slice-start.3 = ((s8[6291456]{0:T(1024)(128)(4,1)}), s8[2097152]{0:T(1024)(128)(4,1)S(1)}, s32[]{:S(2)}) async-start(s8[6291456]{0:T(1024)(128)(4,1)} %bitcast.124), calls=%async_computation.3 | async-start | bytes 4194304
  405.1 12.0 %slice-start.1 = ((s8[8388608]{0:T(1024)(128)(4,1)}), s8[4194304]{0:T(1024)(128)(4,1)S(1)}, s32[]{:S(2)}) async-start(s8[8388608]{0:T(1024)(128)(4,1)} %bitcast.122), calls=%async_computation.1 | async-start | bytes 8388608
  405.1 7.8 %collective-permute-start.7 = (bf16[256,512]{1,0:T(8,128)(2,1)S(1)}, bf16[256,512]{1,0:T(8,128)(2,1)S(1)}, u32[]{:S(2)}, u32[]{:S(2)}) collective-permute-start(bf16[256,512]{1,0:T(8,128)(2,1)S(1)} %copy-done.11), channel_id=1, source_target_pairs={{0,16},{16,0},{1,17},{17,1},{2,18},{18,2},{3,19},{19,3},{4,20},{20... | collective-permute-start | bytes 786440 | tf_op jit(solution)/shard_map/ppermute | solution.py:661
  574.6 10.6 %copy-start.10 = (f32[128,1024]{1,0:T(8,128)S(1)}, f32[128,1024]{1,0:T(8,128)}, u32[]{:S(2)}) copy-start(f32[128,1024]{1,0:T(8,128)} %get-tuple-element.117) | copy-start | bytes 1572868

commit v2 on v0

--- a/solution.py
+++ b/solution.py
@@ -4,6 +4,8 @@
 import jax
 import jax.numpy as jnp
 from jax import lax
+from jax.experimental import pallas as pl
+from jax.experimental.pallas import tpu as pltpu
 from jax.sharding import PartitionSpec as P
 
 HEADS = 16
@@ -42,7 +44,7 @@
     return lax.fori_loop(0, key_count // block_width, turn, carry_state)
 
 
-def shards(
+def general_shards(
     inputs,
     lengths,
     w_query,
@@ -307,7 +309,857 @@
     )
 
 
+MESH = pl.DeviceIdType.MESH
+MIB = 1024*1024
+
+def place():
+    core = lax.axis_index("fsdp"); chip = lax.axis_index("ctx")
+    return core, chip
+
+def greet(peers):
+    barrier = pltpu.get_barrier_semaphore()
+    for peer in peers:
+        pl.semaphore_signal(barrier, inc=1, device_id=peer, device_id_type=MESH)
+    pl.semaphore_wait(barrier, len(peers))
+
+def flip(v, bits):
+    for b in (1, 2, 4, 8):
+        if bits & b:
+            v = v + b - 2 * b * lax.rem(lax.div(v, b), 2)
+    return v
+
+LOG2E = math.log2(math.e)
+
+
+def nt(a, b):
+    return lax.dot_general(a, b, (((1,), (1,)), ((), ())), preferred_element_type=jnp.float32)
+
+
+FULL_ORDER = (12, 8, 4, 15, 11, 7, 14, 13, 10, 9, 6, 5, 3, 2, 1)
+
+
+class Copies:
+    def __init__(self, send_sem, recv_sem):
+        self.send_sem, self.recv_sem = send_sem, recv_sem
+        self.names, self.sent = {}, []
+
+    def pair(self, name, src, dst, peer):
+        i = self.names.setdefault(name, len(self.names))
+        return pltpu.make_async_remote_copy(
+            src_ref=src,
+            dst_ref=dst,
+            send_sem=self.send_sem.at[i],
+            recv_sem=self.recv_sem.at[i],
+            device_id=peer,
+            device_id_type=MESH,
+        )
+
+    def send(self, name, src, dst, peer, like):
+        self.pair(name, src, dst, peer).start()
+        self.sent.append((name, like))
+
+    def arrived(self, name, dst, peer):
+        self.pair(name, dst, dst, peer).wait_recv()
+
+    def drain(self, peer):
+        for name, like in self.sent:
+            self.pair(name, like, like, peer).wait_send()
+
+
+class Gather:
+    def __init__(self, copies, name, src, out, local_sem):
+        self.copies, self.name, self.src, self.out, self.local_sem = copies, name, src, out, local_sem
+        self.core, self.chip = place()
+        self.sib = (1 - self.core, self.chip)
+        self.half = src.shape[0] // 2
+
+    def at(self, bits):
+        return (self.core, flip(self.chip, bits))
+
+    def block(self, bits, core=None):
+        return self.out.at[(self.core if core is None else core) * 16 + flip(self.chip, bits)]
+
+    def part(self, bits, upper):
+        return self.out.at[self.core * 16 + flip(self.chip, bits), pl.ds(self.half if upper else 0, self.half)]
+
+    def send(self, tag, src, dst, peer, half=False):
+        like = self.src.at[pl.ds(0, self.half)] if half else self.src
+        self.copies.send((self.name, tag), src, dst, peer, like)
+
+    def arrived(self, tag, dst):
+        self.copies.arrived((self.name, tag), dst, self.sib)
+
+    def start_z(self):
+        for z in (12, 8, 4):
+            self.send(("z", z), self.src, self.block(0), self.at(z))
+
+    def start_plane(self):
+        self.send(("x", 0), self.src, self.block(0), self.at(1))
+        self.send(("y", 0), self.src, self.block(0), self.at(2))
+        self.send(("s", 0), self.src, self.block(0), self.sib)
+        self.local = pltpu.make_async_copy(self.src, self.block(0), self.local_sem)
+        self.local.start()
+
+    def on_z(self, z):
+        b = self.block(z)
+        self.arrived(("z", z), b)
+        self.send(("x", z), b, b, self.at(1))
+        self.send(("y", z), b, b, self.at(2))
+        self.send(("s", z), b, b, self.sib)
+
+    def on_plane(self, z):
+        for bit, tag, further, upper in ((1, "x", 2, False), (2, "y", 1, True)):
+            b = self.block(z + bit)
+            self.arrived((tag, z), b)
+            h = self.part(z + bit, upper)
+            self.send(("d" + tag, z), h, h, self.at(further), True)
+            self.send(("s", z + bit), b, b, self.sib)
+
+    def on_diagonal(self, z):
+        self.arrived(("dx", z), self.part(z + 3, False))
+        self.arrived(("dy", z), self.part(z + 3, True))
+        b = self.block(z + 3)
+        self.send(("s", z + 3), b, b, self.sib)
+
+    def on_sibling(self):
+        for bits in range(16):
+            self.arrived(("s", bits), self.block(bits, 1 - self.core))
+        self.local.wait()
+
+
+def load_sequence(r_ref, s, kk_ref, vt_ref=None, vv_ref=None):
+    for j in range(r_ref.shape[1]):
+        span = pl.ds(j * 128, 128)
+        kk_ref[span] = r_ref[s, j, 64:128, :].astype(jnp.float32).T.astype(jnp.bfloat16)
+        if vt_ref is not None:
+            vt_ref[:, span] = r_ref[s, j, 128:192, :]
+        if vv_ref is not None:
+            vv_ref[span] = r_ref[s, j, 128:192, :].astype(jnp.float32).T.astype(jnp.bfloat16)
+
+
+def fwd_kernel(
+    x_ref, lengths_ref, s_qkv, s_bias, s_vec, s_out, s_expand, s_reduce,
+    o_vec, o_out, o_expand, o_reduce, o_qkv, o_pairs, o_ctx, o_full, lse_ref,
+    w_qkv, w_bias, send_blk, recv_blk, ctx_blk, ctx_recv, kk, vt,
+    send_sem, recv_sem, local_sem, hsend, hrecv, csend, crecv,
+):
+    f32, bf16 = jnp.float32, jnp.bfloat16
+    core, chip = place()
+    sib = (1 - core, chip)
+    greet([sib] + [(core, flip(chip, b)) for b in range(1, 16)])
+    copies = Copies(send_sem, recv_sem)
+    first = [
+        Gather(copies, 0, s_qkv, w_qkv, local_sem.at[0]),
+        Gather(copies, 1, s_bias, w_bias, local_sem.at[1]),
+    ]
+    rest = [
+        Gather(copies, 2, s_out, o_out, local_sem.at[2]),
+        Gather(copies, 3, s_vec, o_vec, local_sem.at[3]),
+        Gather(copies, 4, s_expand, o_expand, local_sem.at[4]),
+        Gather(copies, 5, s_reduce, o_reduce, local_sem.at[5]),
+    ]
+    for g in first:
+        g.start_z()
+        g.start_plane()
+    for z in (4, 8, 12):
+        for g in first:
+            g.on_z(z)
+    for g in rest[:3]:
+        g.start_z()
+    for z in (0, 4, 8, 12):
+        for g in first:
+            g.on_plane(z)
+    for z in (0, 4, 8, 12):
+        for g in first:
+            g.on_diagonal(z)
+    for g in first:
+        g.on_sibling()
+    keep = pltpu.make_async_copy(w_qkv, o_qkv, local_sem.at[6])
+    keep.start()
+
+    @pl.loop(0, 8)
+    def _(p):
+        w = w_qkv[:, :, pl.ds(pl.multiple_of(p * 384, 128), 384)].reshape(1024, 384)
+        t = jnp.dot(x_ref[...], w, preferred_element_type=f32).T
+        for i in range(2):
+            h = 2 * p + i
+            for part in range(3):
+                rows = t[192 * i + 64 * part : 192 * i + 64 * part + 64]
+                if part != 1:
+                    bias = jnp.concatenate([w_bias[2 * h + k, pl.ds(0 if part == 0 else 32, 32)] for k in range(2)], 0).astype(f32)
+                    rows = rows + jnp.concatenate([bias, bias], 1)
+                send_blk[h, pl.ds(64 * part, 64)] = rows.astype(bf16)
+
+    heads = []
+    for s in range(2):
+        for b in FULL_ORDER:
+            to = flip(chip, b)
+            i = s * 16 + b
+            c = pltpu.make_async_remote_copy(
+                src_ref=send_blk.at[to, :, pl.ds(128 * s, 128)],
+                dst_ref=recv_blk.at[s, chip],
+                send_sem=hsend.at[i],
+                recv_sem=hrecv.at[i],
+                device_id=(core, to),
+                device_id_type=MESH,
+            )
+            c.start()
+            heads.append(c)
+        recv_blk[s, chip] = send_blk[chip, :, pl.ds(128 * s, 128)]
+
+    def heads_here(s):
+        for b in FULL_ORDER:
+            i = s * 16 + b
+            here = recv_blk.at[s, flip(chip, b)]
+            pltpu.make_async_remote_copy(
+                src_ref=here, dst_ref=here, send_sem=hsend.at[i], recv_sem=hrecv.at[i], device_id=sib, device_id_type=MESH
+            ).wait_recv()
+
+    for g in rest:
+        g.start_plane()
+    rest[3].start_z()
+    events = []
+    for z in (4, 8, 12):
+        events.append(lambda z=z: [g.on_z(z) for g in rest[:3]])
+    events.append(lambda: [g.on_plane(0) for g in rest])
+    events.append(lambda: [g.on_diagonal(0) for g in rest])
+    for z in (4, 8, 12):
+        events.append(lambda z=z: [g.on_plane(z) for g in rest[:3]])
+    for z in (4, 8, 12):
+        events.append(lambda z=z: [rest[3].on_z(z)])
+    for z in (4, 8, 12):
+        events.append(lambda z=z: [g.on_diagonal(z) for g in rest[:3]])
+    for z in (4, 8, 12):
+        events.append(lambda z=z: [rest[3].on_plane(z)])
+    for z in (4, 8, 12):
+        events.append(lambda z=z: [rest[3].on_diagonal(z)])
+    events.append(lambda: [g.on_sibling() for g in rest])
+
+    def attend_sequence(s, during):
+        load_sequence(recv_blk, s, kk, vt_ref=vt)
+
+        @pl.loop(0, 8)
+        def _(step):
+            for k, event in enumerate(during):
+
+                @pl.when(step == k)
+                def _():
+                    event()
+
+            q = flip_by(step, chip // 2)
+            query = jnp.concatenate([recv_blk[s, 2 * q, 0:64, :], recv_blk[s, 2 * q + 1, 0:64, :]], 1)
+            scores = jnp.dot(kk[...], query, preferred_element_type=f32) * (0.125 * LOG2E)
+            key = lax.broadcasted_iota(jnp.int32, scores.shape, 0)
+            scores = jnp.where(key < lengths_ref[s], scores, masked_score)
+            top = jnp.max(scores, 0, keepdims=True)
+            e = jnp.exp2(scores - top)
+            mass = jnp.sum(e, 0, keepdims=True)
+            o = jnp.dot(vt[...], e.astype(bf16), preferred_element_type=f32) / mass
+            lse_ref[s, pl.ds(q, 1), :] = top + jnp.log2(mass)
+            o_full[s, :, pl.ds(pl.multiple_of(q * 256, 256), 256)] = o
+            for i in range(2):
+                to = 2 * q + i
+                ctx_blk[s, to] = o[:, 128 * i : 128 * i + 128].astype(bf16)
+
+                @pl.when(to != chip)
+                def _():
+                    pltpu.make_async_remote_copy(
+                        src_ref=ctx_blk.at[s, to],
+                        dst_ref=ctx_recv.at[chip, :, pl.ds(128 * s, 128)],
+                        send_sem=csend.at[s * 16 + to],
+                        recv_sem=crecv.at[s * 16 + chip],
+                        device_id=(core, to),
+                        device_id_type=MESH,
+                    ).start()
+
+        ctx_recv[chip, :, pl.ds(128 * s, 128)] = ctx_blk[s, chip]
+
+    PRE, FIRST, SECOND = 2, 2, 6
+    for event in events[:PRE]:
+        event()
+    heads_here(0)
+    attend_sequence(0, events[PRE : PRE + FIRST])
+    heads_here(1)
+    pairs_out = pltpu.make_async_copy(recv_blk, o_pairs, local_sem.at[7])
+    pairs_out.start()
+    attend_sequence(1, events[PRE + FIRST : PRE + FIRST + SECOND])
+    for event in events[PRE + FIRST + SECOND :]:
+        event()
+    for s in range(2):
+        for b in range(1, 16):
+            other = flip(chip, b)
+            here = ctx_recv.at[other, :, pl.ds(128 * s, 128)]
+            pltpu.make_async_remote_copy(
+                src_ref=ctx_blk.at[s, other],
+                dst_ref=here,
+                send_sem=csend.at[s * 16 + other],
+                recv_sem=crecv.at[s * 16 + other],
+                device_id=sib,
+                device_id_type=MESH,
+            ).wait()
+    ctx_out = pltpu.make_async_copy(ctx_recv, o_ctx, local_sem.at[8])
+    ctx_out.start()
+    for c in heads:
+        c.wait_send()
+    copies.drain(sib)
+    keep.wait()
+    pairs_out.wait()
+    ctx_out.wait()
+
+
+def flip_by(v, w):
+    out = 0
+    for b in (1, 2, 4):
+        p, q = lax.rem(lax.div(v, b), 2), lax.rem(lax.div(w, b), 2)
+        out = out + b * (p + q - 2 * p * q)
+    return out
+
+
+def forward_attention(rows, lengths, qkv, bias, vec, w_out, w_expand, w_reduce, collective_id):
+    v, hbm = pl.BlockSpec(memory_space=pltpu.VMEM), pl.BlockSpec(memory_space=pl.ANY)
+    f32, bf16 = jnp.float32, jnp.bfloat16
+    gathered = lambda x: jax.ShapeDtypeStruct((32,) + x.shape, x.dtype)
+    dma = pltpu.SemaphoreType.DMA
+    return pl.pallas_call(
+        fwd_kernel,
+        out_shape=[
+            gathered(vec),
+            gathered(w_out),
+            gathered(w_expand),
+            gathered(w_reduce),
+            gathered(qkv),
+            jax.ShapeDtypeStruct((2, 16, 192, 128), bf16),
+            jax.ShapeDtypeStruct((16, 64, 256), bf16),
+            jax.ShapeDtypeStruct((2, 64, 2048), f32),
+            jax.ShapeDtypeStruct((2, 8, 256), f32),
+        ],
+        in_specs=[v, pl.BlockSpec(memory_space=pltpu.SMEM)] + [hbm] * 6,
+        out_specs=[hbm] * 7 + [v, v],
+        scratch_shapes=[
+            pltpu.VMEM((32,) + qkv.shape, bf16),
+            pltpu.VMEM((32,) + bias.shape, bf16),
+            pltpu.VMEM((16, 192, 256), bf16),
+            pltpu.VMEM((2, 16, 192, 128), bf16),
+            pltpu.VMEM((2, 16, 64, 128), bf16),
+            pltpu.VMEM((16, 64, 256), bf16),
+            pltpu.VMEM((2048, 64), bf16),
+            pltpu.VMEM((64, 2048), bf16),
+            dma((210,)),
+            dma((210,)),
+            dma((9,)),
+            dma((32,)),
+            dma((32,)),
+            dma((32,)),
+            dma((32,)),
+        ],
+        compiler_params=pltpu.CompilerParams(
+            collective_id=collective_id, has_side_effects=True, vmem_limit_bytes=56 * MIB
+        ),
+        name="forward_attention",
+    )(rows, lengths, qkv, bias, vec, w_out, w_expand, w_reduce)
+
+
+class Scatter:
+    ORDER = (12, 8, 4, 0)
+
+    def __init__(self, copies, name, grads, out, bufs):
+        self.copies, self.name, self.grads, self.out = copies, name, grads, out
+        self.first, self.second, self.third, self.passed = bufs
+        self.core, self.chip = place()
+        self.rows = grads.shape[1]
+        self.half = self.rows // 2
+        self.lo, self.hi = pl.ds(0, self.half), pl.ds(self.half, self.half)
+        self.first_at = [[self.first.at[k, i] for i in range(2)] for k in range(4)]
+        self.second_at = [[self.second.at[k, i] for i in range(2)] for k in range(4)]
+        self.third_at = [self.third.at[k] for k in range(3)]
+        self.passed_at = [self.passed.at[k] for k in range(3)]
+
+    def at(self, bits):
+        return (self.core, flip(self.chip, bits))
+
+    def send(self, tag, src, dst, bits, half=True):
+        like = self.first_at[0][0] if half else self.passed_at[0]
+        self.copies.send((self.name, tag), src, dst, self.at(bits), like)
+
+    def arrived(self, tag, dst):
+        self.copies.arrived((self.name, tag), dst, self.at(1))
+
+    def add(self, rows, fn):
+        step = min(rows, 16)
+        if rows == step:
+            fn(0, step)
+            return
+
+        def turn(i, carry):
+            fn(pl.multiple_of(i * step, step), step)
+            return carry
+
+        lax.fori_loop(0, rows // step, turn, 0)
+
+    def start(self):
+        for k, z in enumerate(self.ORDER):
+            diag = flip(self.chip, z + 3)
+            self.send(("1a", k), self.grads.at[diag, self.lo], self.first_at[k][0], 2)
+            self.send(("1b", k), self.grads.at[diag, self.hi], self.first_at[k][1], 1)
+
+    def start_direct(self):
+        for k, z in enumerate(self.ORDER):
+            xb, yb = flip(self.chip, z + 1), flip(self.chip, z + 2)
+            self.send(("2xh", k), self.grads.at[xb, self.hi], self.second_at[k][0].at[self.hi], 1)
+            self.send(("2yl", k), self.grads.at[yb, self.lo], self.second_at[k][1].at[self.lo], 2)
+
+    def on_first(self, k):
+        z = self.ORDER[k]
+        for i, (tag, bit, upper) in enumerate((("1a", 1, False), ("1b", 2, True))):
+            owner = flip(self.chip, z + bit)
+            here = self.first_at[k][i]
+            self.arrived((tag, k), here)
+
+            def fn(start, size):
+                rows = pl.ds(start, size)
+                theirs = pl.ds(start + (self.half if upper else 0), size)
+                here[rows] = here[rows] + self.grads.at[owner][theirs]
+
+            self.add(self.half, fn)
+            self.send(("2" + "xy"[i] + "lh"[i], k), here, self.second_at[k][i].at[self.hi if upper else self.lo], bit)
+
+    def on_second(self, k):
+        z = self.ORDER[k]
+        self.arrived(("2xh", k), self.second_at[k][0].at[self.hi])
+        self.arrived(("2yl", k), self.second_at[k][1].at[self.lo])
+        self.arrived(("2xl", k), self.second_at[k][0].at[self.lo])
+        self.arrived(("2yh", k), self.second_at[k][1].at[self.hi])
+        owner = flip(self.chip, z)
+
+        def fn(start, size):
+            rows = pl.ds(start, size)
+            f32 = jnp.float32
+            total = self.grads.at[owner][rows].astype(f32) + self.second_at[k][0][rows].astype(f32)
+            total = total + self.second_at[k][1][rows].astype(f32)
+            if k < 3:
+                self.passed_at[k][rows] = total.astype(self.passed.dtype)
+            else:
+                self.out[rows] = total
+
+        self.add(self.rows, fn)
+        if k < 3:
+            self.send(("3", k), self.passed_at[k], self.third_at[k], z, False)
+
+    def on_third(self):
+        for k in range(3):
+            self.arrived(("3", k), self.third_at[k])
+
+        def fn(start, size):
+            rows = pl.ds(start, size)
+            total = self.out[rows]
+            for k in range(3):
+                total = total + self.third_at[k][rows].astype(jnp.float32)
+            self.out[rows] = total
+
+        self.add(self.rows, fn)
+
+
+def scatter_buffers(block, dtype):
+    rows, cols = block
+    return [
+        pltpu.VMEM((4, 2, rows // 2, cols), dtype),
+        pltpu.VMEM((4, 2, rows, cols), dtype),
+        pltpu.VMEM((3, rows, cols), dtype),
+        pltpu.VMEM((3, rows, cols), dtype),
+    ]
+
+
+def bwd_kernel(*refs):
+    f32, bf16 = jnp.float32, jnp.bfloat16
+    (lengths_ref, pairs, o_full, lse_ref, d_ctx, x_t, d_first, g_reduce, g_expand, g_out, g_vec, h_qkv) = refs[:12]
+    (o_reduce, o_expand, o_out, o_vec, o_qkv, o_input, o_bias) = refs[12:19]
+    bufs = [refs[19 + 4 * i : 23 + 4 * i] for i in range(5)]
+    (
+        g_qkv, w_qkv, d_recv, kk, vv, kt, acc, d_send, d_own, d_sib, b_own, b_sib, b_in,
+        send_sem, recv_sem, local_sem, dsend, drecv, qsend, qrecv,
+    ) = refs[39:]
+    core, chip = place()
+    sib = (1 - core, chip)
+    greet([sib] + [(core, flip(chip, b)) for b in range(1, 16)])
+    copies = Copies(send_sem, recv_sem)
+    rest = [
+        Scatter(copies, i, g, o, bufs[i])
+        for i, (g, o) in enumerate(((g_reduce, o_reduce), (g_expand, o_expand), (g_out, o_out), (g_vec, o_vec)))
+    ]
+    last = Scatter(copies, 4, g_qkv, o_qkv, bufs[4])
+    weights = pltpu.make_async_copy(h_qkv, w_qkv, local_sem.at[0])
+    weights.start()
+    sent = []
+
+    def exchange_out(s, b, src, dst, sends, recvs):
+        c = pltpu.make_async_remote_copy(
+            src_ref=src,
+            dst_ref=dst,
+            send_sem=sends.at[s * 16 + b],
+            recv_sem=recvs.at[s * 16 + b],
+            device_id=(core, flip(chip, b)),
+            device_id_type=MESH,
+        )
+        c.start()
+        sent.append(c)
+
+    def exchange_in(s, b, here, sends, recvs):
+        pltpu.make_async_remote_copy(
+            src_ref=here,
+            dst_ref=here,
+            send_sem=sends.at[s * 16 + b],
+            recv_sem=recvs.at[s * 16 + b],
+            device_id=sib,
+            device_id_type=MESH,
+        ).wait_recv()
+
+    for s in range(2):
+        lane = pl.ds(128 * s, 128)
+        for b in FULL_ORDER:
+            exchange_out(s, b, d_ctx.at[flip(chip, b), :, lane], d_recv.at[s, chip], dsend, drecv)
+        d_recv[s, chip] = d_ctx[chip, :, lane]
+    for r in rest:
+        r.start()
+    for r in rest:
+        r.start_direct()
+    b_own[...] = jnp.zeros_like(b_own)
+
+    def back_sequence(s, during):
+        load_sequence(pairs, s, kk, vt_ref=None, vv_ref=vv)
+        for j in range(16):
+            kt[:, pl.ds(j * 128, 128)] = pairs[s, j, 64:128, :]
+        acc[...] = jnp.zeros_like(acc)
+
+        @pl.loop(0, 8)
+        def _(q):
+            for k, event in enumerate(during):
+
+                @pl.when(q == k)
+                def _():
+                    event()
+
+            both = lambda ref, lo, hi: jnp.concatenate([ref[s, 2 * q, lo:hi, :], ref[s, 2 * q + 1, lo:hi, :]], 1)
+            query, d_out = both(pairs, 0, 64), both(d_recv, 0, 64)
+            span = pl.ds(pl.multiple_of(q * 256, 256), 256)
+            delta = jnp.sum(d_out.astype(f32) * o_full[s, :, span], 0, keepdims=True)
+            scores = jnp.dot(kk[...], query, preferred_element_type=f32) * (0.125 * LOG2E)
+            key = lax.broadcasted_iota(jnp.int32, scores.shape, 0)
+            probs = jnp.where(key < lengths_ref[s], jnp.exp2(scores - lse_ref[s, pl.ds(q, 1), :]), 0.0)
+            d_probs = jnp.dot(vv[...], d_out, preferred_element_type=f32)
+            d_scores = (probs * (d_probs - delta)).astype(bf16)
+            zero = jnp.zeros((64, 256), f32)
+            query_rows = jnp.concatenate([query.astype(f32), zero], 0).T.astype(bf16)
+            d_rows = jnp.concatenate([zero, d_out.astype(f32)], 0).T.astype(bf16)
+            acc[...] += jnp.dot(d_scores, query_rows, preferred_element_type=f32) + jnp.dot(
+                probs.astype(bf16), d_rows, preferred_element_type=f32
+            )
+            d_query = (jnp.dot(kt[...], d_scores, preferred_element_type=f32) * 0.125).astype(bf16)
+            for i in range(2):
+                part = d_query[:, 128 * i : 128 * i + 128]
+                d_send[s, 2 * q + i, 0:64, :] = part
+                b_own[0] += part.astype(f32)
+
+        for j in range(16):
+            t = acc[pl.ds(j * 128, 128)].T
+            d_send[s, j, 64:128, :] = (t[:64] * 0.125).astype(bf16)
+            value = t[64:].astype(bf16)
+            d_send[s, j, 128:192, :] = value
+            b_own[1] += value.astype(f32)
+        lane = pl.ds(128 * s, 128)
+        for b in FULL_ORDER:
+            exchange_out(s, b, d_send.at[s, flip(chip, b)], d_own.at[chip, :, lane], qsend, qrecv)
+        d_own[chip, :, lane] = d_send[s, chip]
+
+    events = [lambda k=k: [r.on_first(k) for r in rest] for k in range(4)]
+    events += [lambda k=k: [r.on_second(k) for r in rest] for k in range(4)]
+    FIRST, SECOND, WAIT = 0, 4, 2
+    for b in FULL_ORDER:
+        exchange_in(0, b, d_recv.at[0, flip(chip, b)], dsend, drecv)
+    back_sequence(0, events[:FIRST])
+    for b in FULL_ORDER:
+        exchange_in(1, b, d_recv.at[1, flip(chip, b)], dsend, drecv)
+    back_sequence(1, events[FIRST : FIRST + SECOND])
+
+    copies.send("bias sib", b_own, b_sib, sib, b_own)
+    for event in events[FIRST + SECOND : FIRST + SECOND + WAIT]:
+        event()
+    for s in range(2):
+        lane = pl.ds(128 * s, 128)
+        for b in FULL_ORDER:
+            exchange_in(s, b, d_own.at[flip(chip, b), :, lane], qsend, qrecv)
+        copies.send(("rows", s), d_own.at[:, :, lane], d_sib.at[:, :, lane], sib, d_own.at[:, :, lane])
+
+    copies.arrived("bias sib", b_sib, sib)
+    for s in range(2):
+        copies.arrived(("rows", s), d_sib.at[:, :, pl.ds(128 * s, 128)], sib)
+
+    @pl.loop(0, 8)
+    def _(p):
+        total = None
+        for i, rows in enumerate((d_own, d_sib)):
+            term = nt(x_t[:, 256 * i : 256 * i + 256], rows[pl.ds(2 * p, 2)].reshape(384, 256))
+            total = term if total is None else total + term
+        g_qkv[:, :, pl.ds(pl.multiple_of(p * 384, 128), 384)] = total.astype(bf16).reshape(16, 32, 384)
+
+    last.start()
+    last.start_direct()
+
+    b_sib[...] = b_sib[...] + b_own[...]
+    sender = core == lax.div(chip, 8)
+    for i in range(2):
+        to = lax.rem(2 * chip + i, 16)
+        rows = pl.ds(32 * i, 32)
+        c = pltpu.make_async_remote_copy(
+            src_ref=b_sib.at[:, rows],
+            dst_ref=b_in,
+            send_sem=local_sem.at[1 + i],
+            recv_sem=local_sem.at[3],
+            device_id=(core, to),
+            device_id_type=MESH,
+        )
+
+        @pl.when(sender & (to != chip))
+        def _():
+            c.start()
+
+        @pl.when(sender & (to == chip))
+        def _():
+            b_in[...] = b_sib[:, rows]
+
+    weights.wait()
+
+    @pl.loop(0, 4)
+    def _(i):
+        w = w_qkv[pl.ds(i * 8, 8)].reshape(256, 3072)
+        t = jnp.dot(w, d_own[...].reshape(3072, 256), preferred_element_type=f32).T
+        cols = pl.ds(pl.multiple_of(i * 256, 256), 256)
+        o_input[:, cols] = d_first[:, cols] + t
+
+    for event in events[FIRST + SECOND + WAIT :]:
+        event()
+    for k in range(4):
+        last.on_first(k)
+    for r in rest:
+        r.on_third()
+    for k in range(4):
+        last.on_second(k)
+    last.on_third()
+    for i in range(2):
+        to = lax.rem(2 * chip + i, 16)
+
+        @pl.when(sender & (to != chip))
+        def _():
+            pltpu.make_async_remote_copy(
+                src_ref=b_sib.at[:, pl.ds(32 * i, 32)],
+                dst_ref=b_in,
+                send_sem=local_sem.at[1 + i],
+                recv_sem=local_sem.at[3],
+                device_id=(core, to),
+                device_id_type=MESH,
+            ).wait_send()
+
+    @pl.when(8 * core + lax.div(chip, 2) != chip)
+    def _():
+        pltpu.make_async_remote_copy(
+            src_ref=b_in, dst_ref=b_in, send_sem=local_sem.at[1], recv_sem=local_sem.at[3], device_id=sib, device_id_type=MESH
+        ).wait_recv()
+
+    o_bias[...] = b_in[...]
+    for c in sent:
+        c.wait_send()
+    copies.drain(sib)
+
+
+def backward_attention(lengths, pairs, o_full, lse, d_ctx, x_t, d_first, grads, w_qkv, collective_id):
+    v, hbm = pl.BlockSpec(memory_space=pltpu.VMEM), pl.BlockSpec(memory_space=pl.ANY)
+    f32, bf16 = jnp.float32, jnp.bfloat16
+    dma = pltpu.SemaphoreType.DMA
+    blocks = [(g.shape[1:], g.dtype) for g in grads] + [((32, 3072), bf16)]
+    bufs = []
+    for block, dtype in blocks:
+        bufs += scatter_buffers(block, dtype)
+    return pl.pallas_call(
+        bwd_kernel,
+        out_shape=[jax.ShapeDtypeStruct(block, f32) for block, _ in blocks]
+        + [jax.ShapeDtypeStruct(d_first.shape, f32), jax.ShapeDtypeStruct((2, 32, 128), f32)],
+        in_specs=[pl.BlockSpec(memory_space=pltpu.SMEM)] + [v] * 10 + [hbm],
+        out_specs=[v] * 7,
+        scratch_shapes=bufs
+        + [
+            pltpu.VMEM((16, 32, 3072), bf16),
+            pltpu.VMEM((32, 32, 3072), bf16),
+            pltpu.VMEM((2, 16, 64, 128), bf16),
+            pltpu.VMEM((2048, 64), bf16),
+            pltpu.VMEM((2048, 64), bf16),
+            pltpu.VMEM((64, 2048), bf16),
+            pltpu.VMEM((2048, 128), f32),
+            pltpu.VMEM((2, 16, 192, 128), bf16),
+            pltpu.VMEM((16, 192, 256), bf16),
+            pltpu.VMEM((16, 192, 256), bf16),
+            pltpu.VMEM((2, 64, 128), f32),
+            pltpu.VMEM((2, 64, 128), f32),
+            pltpu.VMEM((2, 32, 128), f32),
+            dma((140,)),
+            dma((140,)),
+            dma((4,)),
+            dma((32,)),
+            dma((32,)),
+            dma((32,)),
+            dma((32,)),
+        ],
+        compiler_params=pltpu.CompilerParams(
+            collective_id=collective_id, has_side_effects=True, vmem_limit_bytes=62 * MIB
+        ),
+        name="backward_attention",
+    )(lengths, pairs, o_full, lse, d_ctx, x_t, d_first, *grads, w_qkv)
+
+
+def swap(x):
+    return lax.ppermute(x, "fsdp", [(0, 1), (1, 0)])
+
+
+def halves(left_t):
+    core = lax.axis_index("fsdp")
+    h = left_t.shape[0] // 2
+    own = lax.dynamic_slice_in_dim(left_t, core * h, h, 0)
+    return own, swap(lax.dynamic_slice_in_dim(left_t, (1 - core) * h, h, 0))
+
+
+def chip_sum(left, right):
+    core = lax.axis_index("fsdp")
+    h = left.shape[1] // 2
+    own = lax.dynamic_slice_in_dim(left, core * h, h, 1)
+    other = swap(lax.dynamic_slice_in_dim(left, (1 - core) * h, h, 1))
+    grad = outer_sum(own, right) + outer_sum(other, swap(right))
+    return grad.astype(jnp.bfloat16).reshape(16, h // 16, right.shape[1])
+
+
+def fast_shards(
+    inputs,
+    lengths,
+    w_query,
+    b_query,
+    w_key,
+    w_value,
+    b_value,
+    w_out,
+    b_out,
+    first_gain,
+    first_shift,
+    w_expand,
+    b_expand,
+    w_reduce,
+    b_reduce,
+    second_gain,
+    second_shift,
+    cotangent,
+):
+    core = lax.axis_index("fsdp")
+    f32, bf16 = jnp.float32, jnp.bfloat16
+    seqs, count, width = inputs.shape
+    total = seqs * count
+    part = width // 32
+    ff = w_expand.shape[1]
+    qkv = jnp.concatenate([w.reshape(part, HEADS, 64) for w in (w_query, w_key, w_value)], -1).reshape(part, 3 * width)
+    bias = jnp.concatenate([b_query, b_value])[:, None] + jnp.zeros((2 * part, 128), bf16)
+    small = [b_out, first_gain, first_shift, b_expand, b_reduce, second_gain, second_shift]
+    sizes = [b.shape[0] for b in small]
+    vec = jnp.concatenate(small + [jnp.zeros((part * 128 - sum(sizes),), bf16)]).reshape(part, 128)
+    flat_rows = inputs.reshape(total, width)
+    g_vec, g_out, g_expand, g_reduce, g_qkv, pairs, context_t, o_full, lse = forward_attention(
+        flat_rows, lengths, qkv, bias, vec, w_out, w_expand, w_reduce, 1
+    )
+    full_out = g_out.reshape(width, width)
+    full_expand = g_expand.reshape(width, ff)
+    full_reduce = g_reduce.reshape(ff, width)
+    flat_vec = g_vec.reshape(32, part * 128)
+    offsets = [sum(sizes[:i]) for i in range(len(sizes) + 1)]
+    (bias_out, gain_first, shift_first, bias_expand, bias_reduce, gain_second, shift_second) = [
+        flat_vec[:, offsets[i] : offsets[i + 1]].reshape(-1).astype(f32) for i in range(len(sizes))
+    ]
+    own_first = lax.axis_index("ctx") * count
+    positions = own_first + jnp.arange(count, dtype=jnp.int32)
+    valid_rows = (positions[None, :] < lengths[:, None]).astype(f32).reshape(total, 1)
+    context_t = context_t.reshape(width, total)
+    attended = outer_sum(context_t, full_out) + bias_out
+    residual = flat_rows.astype(f32) + attended
+    normed, first_pull = jax.vjp(layer_norm, residual, gain_first, shift_first)
+    normed_low = normed.astype(bf16)
+    expanded = product(normed_low, full_expand) + bias_expand
+    activated, gelu_pull = jax.vjp(partial(jax.nn.gelu, approximate=False), expanded)
+    activated_low = activated.astype(bf16)
+    reduced = product(activated_low, full_reduce) + bias_reduce
+    final_rows, second_pull = jax.vjp(layer_norm, normed + reduced, gain_second, shift_second)
+    layer_out = (final_rows * valid_rows).astype(bf16).reshape(inputs.shape)
+    d_output = cotangent.reshape(total, width).astype(f32) * valid_rows
+    d_second, second_gain_grad, second_shift_grad = second_pull(d_output)
+    d_reduced = d_second.astype(bf16)
+    reduce_grad = chip_sum(activated_low, d_reduced)
+    reduce_bias_grad = jnp.sum(d_reduced.astype(f32), 0)
+    (d_expanded_full,) = gelu_pull(back_product(d_reduced, full_reduce))
+    d_expanded = d_expanded_full.astype(bf16)
+    expand_grad = chip_sum(normed_low, d_expanded)
+    expand_bias_grad = jnp.sum(d_expanded.astype(f32), 0)
+    d_normed = d_second + back_product(d_expanded, full_expand)
+    d_first, first_gain_grad, first_shift_grad = first_pull(d_normed)
+    d_attended = d_first.astype(bf16)
+    context_own, context_other = halves(context_t)
+    out_grad = product(context_own, d_attended) + product(context_other, swap(d_attended))
+    out_grad = out_grad.astype(bf16).reshape(16, part, width)
+    out_bias_grad = jnp.sum(d_attended.astype(f32), 0)
+    d_context_t = back_product(full_out, d_attended).astype(bf16).reshape(HEADS, 64, total)
+    x_t = jnp.concatenate(halves(flat_rows.T), 1)
+    small_grads = jnp.concatenate(
+        [
+            g.reshape(32, -1)
+            for g in (
+                out_bias_grad,
+                first_gain_grad,
+                first_shift_grad,
+                expand_bias_grad,
+                reduce_bias_grad,
+                second_gain_grad,
+                second_shift_grad,
+            )
+        ]
+        + [jnp.zeros((32, 2048 - sum(sizes)), f32)],
+        1,
+    ).reshape(2, 16, 16, 128)
+    vec_grad = lax.dynamic_index_in_dim(small_grads, core, 0, False) + swap(
+        lax.dynamic_index_in_dim(small_grads, 1 - core, 0, False)
+    )
+    s_reduce, s_expand, s_out, s_vec, s_qkv, input_grad, s_bias = backward_attention(
+        lengths, pairs, o_full, lse, d_context_t, x_t, d_first, [reduce_grad, expand_grad, out_grad, vec_grad], g_qkv, 2
+    )
+    s_qkv = s_qkv.reshape(part, HEADS, 3, 64)
+    s_query, s_key, s_value = (s_qkv[:, :, i].reshape(part, width) for i in range(3))
+    s_bias = jnp.sum(s_bias, -1)
+    s_vec = s_vec.reshape(-1)
+    v = [s_vec[offsets[i] : offsets[i + 1]] for i in range(len(sizes))]
+    return (
+        layer_out,
+        input_grad.reshape(inputs.shape),
+        s_query,
+        s_bias[0],
+        s_key,
+        s_value,
+        s_bias[1],
+        s_out,
+        v[0],
+        v[1],
+        v[2],
+        s_expand,
+        v[3],
+        s_reduce,
+        v[4],
+        v[5],
+        v[6],
+    )
+
+
 def solution(mesh):
+    fast = mesh.shape["fsdp"] == 2 and mesh.shape["ctx"] == HEADS
+    shards = fast_shards if fast else general_shards
     return jax.shard_map(
         shards,
         mesh=mesh,

time: 2530 us -> 458 us (0.18)
  waiting for transfers between devices: 2000 us -> 0.02 us
  Pallas kernels: 0 us -> 331 us
  blocking collectives: 156 us -> 0 us
  local copies, waits for them, and re-layouts: 133 us -> 33.5 us
  matrix products: 144 us -> 71.7 us
  other arithmetic: 66.6 us -> 9.24 us
    reduce_scatter x3 -> x0, waiting for transfers between devices: 789 us -> none  [the longest x1 363 us: shards(): lax.psum_scatter(reduce_grad, ('fsdp', 'ctx'), scatter_dimension=0, tiled...]
    unnamed x18 -> x0, waiting for transfers between devices: 763 us -> none
    all_gather x7 -> x0, waiting for transfers between devices: 453 us -> none  [the longest x1 233 us: shards(): lax.all_gather(local_pairs, 'ctx', axis=1, tiled=True)]
    pallas_call x0 -> x2, Pallas kernels: none -> 331 us  [the longest x1 169 us: backward_attention(): pl.pallas_call(bwd_kernel, out_shape=[jax.ShapeDtypeStruct(block, f32) fo...]
    unnamed x111 -> x38, local copies, waits for them, and re-layouts: 98 us -> 6.82 us
    unnamed x2 -> x0, blocking collectives: 90 us -> none
    all_gather x1 -> x0, blocking collectives: 66.2 us -> none  [shards(): lax.all_gather(b_expand, ('fsdp', 'ctx'), axis=0, tiled=True)]
    dot_general x28 -> x0, matrix products: 57.5 us -> none  [the longest x4 12.5 us: score_grads(): jnp.einsum('sqhd,skhd->shqk', d_context_heads, value_heads, preferred_ele...]
  transfers between devices with their start and end apart: 14 -> 8, of which waited for: 13 -> 0; matrix products, arithmetic and copies ran while one was open for 6% -> 20% of each run, Pallas kernels for 0% -> 36%
where the time goes in v2:
time: 458 us; the launch traced here: 450 us
  Pallas kernels  331 us (72%)
  matrix products  71.7 us (16%)
  local copies, waits for them, and re-layouts  33.5 us (7%)
  other arithmetic  9.24 us (2%)
    pallas_call x1, Pallas kernels, backward_attention(): pl.pallas_call(bwd_kernel, out_shape=[jax.ShapeDtypeStruct(block, f32) fo...  169 us
    pallas_call x1, Pallas kernels, forward_attention(): pl.pallas_call(fwd_kernel, out_shape=[gathered(vec), gathered(w_out), gat...  162 us
    dot_general x4, matrix products, product(): return jnp.dot(left, right, preferred_element_type=jnp.float32)  26.4 us
    dot_general x5, matrix products, outer_sum(): jnp.einsum('rd,re->de', left, right, preferred_element_type=jnp.float32)  25.4 us
    dot_general x3, matrix products, back_product(): jnp.einsum('re,de->rd', grad_rows, weight, preferred_element_type=jnp.flo...  19.9 us
  transfers between devices with their start and end apart: 8, of which 0 were waited for; matrix products, arithmetic and copies ran while one was open for 20% of the time, Pallas kernels for 36%

profile of v2, /device:TPU:0, one launch (start us, length us, event | category | flops | bytes accessed | tf_op | source)
XLA Modules:
  0.0 450.3 jit_solution(11064669530857385771)
XLA Ops:
  0.7 1.8 dynamic-slice_bitcast_fusion.1
  3.0 1.0 reshape.270
  4.0 1.0 reshape.269
  5.0 1.0 reshape.268
  7.8 5.4 %concatenate.17 = bf16[4096]{0:T(1024)(128)(2,1)} concatenate(bf16[32]{0:T(256)(128)(2,1)} %param.26, bf16[32]{0:T(256)(128)(2,1)} %param.27, bf16[32]{0:T(256)(128)(2,1)} %param.28, bf16[128]{0:T(256)(128)(2,1)} %param.30, bf16[32]{0:T(256)(128)(2,1)} %param.32, bf16[32]{0:T(256)(128)(2,1)} %param.33, bf16[32]{0:T(256)(128)(2,1)} %param.34, bf16[3776]{0:T(1024)(128)(2,1)S(1)} %broadcast_in_dim.12), dimensions={0} | concatenate | bytes 16384 | tf_op jit(solution)/shard_map/concatenate | solution.py:1067
  13.9 162.2 %forward_attention.1 = (bf16[32,32,128]{2,1,0:T(8,128)(2,1)}, bf16[32,32,1024]{2,1,0:T(8,128)(2,1)}, bf16[32,32,4096]{2,1,0:T(8,128)(2,1)}, bf16[32,128,1024]{2,...) custom-call(bf16[256,1024]{1,0:T(8,128)(2,1)} %bitcast.77, ...), custom_call_target="tpu_custom_call" | custom-call | tf_op jit(solution)/shard_map/forward_attention/pallas_call | solution.py:623
  176.1 1.1 copy.40
  177.5 2.6 fusion.27
  180.7 15.7 %multiply_convert_fusion = (bf16[256,4096]{1,0:T(8,128)(2,1)S(1)}, f32[256,4096]{1,0:T(8,128)}, f32[256,4096]{1,0:T(8,128)}) fusion(f32[4096]{0:T(1024)S(1)} %fusion.16, bf16[256,1024]{1,0:T(8,128)(2,1)S(1)} %fusion.11, bf16[1024,4096]{1,0:T(8,128)(2,1)} %bitcast.98), kind=kOutput, calls=%fused_computation.7 | convolution fusion | flops 2216689664 | bytes 19415040 | tf_op jit(solution)/shard_map/dot_general | solution.py:25
  196.3 1.4 copy-done.2
  197.7 1.2 constant_dynamic-slice_fusion.2
  198.9 1.3 collective-permute-start.1
  200.3 6.5 %fusion.28 = (f32[256]{0:T(256)S(1)}, f32[256,1024]{1,0:T(8,128)S(1)}) fusion(f32[1024]{0:T(1024)S(1)} %reshape.298, bf16[256,4096]{1,0:T(8,128)(2,1)} %copy-done.2, bf16[4096,1024]{1,0:T(8,128)(2,1)} %bitcast.102, f32[1024]{0:T(1024)S(1)} %reshape.296, f32[1024]{0:T(1024)S(1)} %reshape.295, f32[256]{0:T(256)S(1)} %fusion.20, ...), kind=kOutput, calls=%fused_computation.96 | convolution fusion | flops 2149318400 | bytes 12598272 | tf_op jit(solution)/shard_map/dot_general | solution.py:25
  207.8 1.3 fusion.24
  209.3 12.8 %convert_reduce_fusion = (f32[4096]{0:T(1024)S(1)}, bf16[256,4096]{1,0:T(8,128)(2,1)}) fusion(f32[256,4096]{1,0:T(8,128)} %get-tuple-element.69, f32[256,4096]{1,0:T(8,128)} %get-tuple-element.91, bf16[256,1024]{1,0:T(8,128)(2,1)S(1)} %get-tuple-element.58, bf16[4096,1024]{1,0:T(8,128)(2,1)} %bitcast.103), kind=kOutput, calls=%fused_computation.5 | convolution fusion | flops 2164256768 | bytes 19415040 | tf_op jit(solution)/shard_map/re,de->rd/dot_general | solution.py:33
  222.3 4.4 multiply_reduce_fusion.2
  227.1 1.3 convert_reduce_fusion.2
  230.5 6.2 %fusion.14 = f32[512,4096]{1,0:T(8,128)} fusion(bf16[256,4096]{1,0:T(8,128)(2,1)} %get-tuple-element.60, bf16[256,1024]{1,0:T(8,128)(2,1)S(1)} %fusion.11, s32[]{:T(128)S(6)} %select_n.23), kind=kOutput, calls=%fused_computation.56 | convolution fusion | flops 1073741824 | bytes 10747908 | tf_op jit(solution)/shard_map/rd,re->de/dot_general | solution.py:29
  236.8 4.5 %fusion.8 = f32[2048,1024]{1,0:T(8,128)} fusion(bf16[256,1024]{1,0:T(8,128)(2,1)S(1)} %get-tuple-element.58, bf16[256,4096]{1,0:T(8,128)(2,1)S(1)} %copy-done.3, s32[]{:T(128)S(6)} %select_n.25), kind=kOutput, calls=%fused_computation.36 | convolution fusion | flops 1073741824 | bytes 9961476 | tf_op jit(solution)/shard_map/rd,re->de/dot_general | solution.py:29
  241.3 2.6 convolution_convert_fusion
  244.0 1.5 fusion.12
  247.4 1.6 bitcast_add_fusion.refs_10_
  250.0 1.0 copy.36.refs_5_
  251.4 2.8 add_convert_fusion.3
  254.2 7.2 %add_convert_fusion.1 = bf16[2048,1024]{1,0:T(8,128)(2,1)} fusion(f32[2048,1024]{1,0:T(8,128)} %fusion.8, bf16[256,2048]{1,0:T(8,128)(2,1)} %collective-permute-done.1, bf16[256,1024]{1,0:T(8,128)(2,1)S(1)} %collective-permute-done.2), kind=kOutput, calls=%fused_computation.1 | convolution fusion | flops 1077936128 | bytes 14155776 | tf_op jit(solution)/shard_map/rd,re->de/dot_general | solution.py:29
  261.4 4.9 %add_convert_fusion = bf16[512,4096]{1,0:T(8,128)(2,1)} fusion(f32[512,4096]{1,0:T(8,128)S(1)} %bitcast.73, bf16[256,512]{1,0:T(8,128)(2,1)S(1)} %collective-permute-done.3, bf16[256,4096]{1,0:T(8,128)(2,1)} %collective-permute-done.4), kind=kOutput, calls=%fused_computation | convolution fusion | flops 1077936128 | bytes 14942208 | tf_op jit(solution)/shard_map/rd,re->de/dot_general | solution.py:29
  266.3 168.9 %backward_attention.1 = (f32[128,1024]{1,0:T(8,128)}, f32[32,4096]{1,0:T(8,128)}, f32[32,1024]{1,0:T(8,128)}, f32[16,128]{1,0:T(8,128)}, f32[32,3072]{1,0:T(8,12...) custom-call(s32[2]{0:T(128)} %refs_0_.1, bf16[2,16,192,128]{3,2,1,0:T(8,128)(2,1)} %get-tuple-element.38.refs_1_, ...), custom_call_target="tpu_custom_call" | custom-call | tf_op jit(solution)/shard_map/backward_attention/pallas_call | solution.py:981
  435.2 1.5 fusion.26
  436.7 1.3 slice.89
  438.0 1.6 reshape.292
  439.6 2.2 slice_reduce_fusion
  447.2 1.9 copy.47
  (99 shorter events, 17.3 us)
Async XLA Ops:
  0.7 176.9 %copy-start = (bf16[2,128,1024]{2,1,0:T(8,128)(2,1)S(1)}, bf16[2,128,1024]{2,1,0:T(8,128)(2,1)}, u32[]{:S(2)}) copy-start(bf16[2,128,1024]{2,1,0:T(8,128)(2,1)} %param.18) | copy-start | bytes 1572868
  2.5 244.8 %collective-permute-start = (bf16[512,256]{0,1:T(8,128)(2,1)}, bf16[512,256]{0,1:T(8,128)(2,1)}, u32[]{:S(2)}, u32[]{:S(2)}) collective-permute-start(bf16[512,256]{0,1:T(8,128)(2,1)} %get-tuple-element.72), channel_id=1, source_target_pairs={{0,16},{16,0},{1,17},{17,1},{2,18},{18,2},{3,19},{19,3},{4,20},{20... | collective-permute-start | bytes 786440 | tf_op jit(solution)/shard_map/ppermute | solution.py:1018
  180.7 19.6 %copy-start.11 = (s32[2]{0:T(128)S(1)}, s32[2]{0:T(128)}, u32[]{:S(2)}) copy-start(s32[2]{0:T(128)} %refs_0_.1) | copy-start | bytes 28
  196.3 1.4 copy-start.2
  198.9 55.3 %collective-permute-start.1 = (bf16[256,2048]{1,0:T(8,128)(2,1)}, bf16[256,2048]{1,0:T(8,128)(2,1)}, u32[]{:S(2)}, u32[]{:S(2)}) collective-permute-start(bf16[256,2048]{1,0:T(8,128)(2,1)} %constant_dynamic-slice_fusion.2), channel_id=1, source_target_pairs={{0,16},{16,0},{1,17},{17,1},{2,18},{18,2},{3,19},{19,3},{4,20},{20... | collective-permute-start | bytes 3145736 | tf_op jit(solution)/shard_map/ppermute | solution.py:1018
  200.3 6.9 %copy-start.1 = (bf16[2,128,1024]{2,1,0:T(8,128)(2,1)S(1)}, bf16[2,128,1024]{2,1,0:T(8,128)(2,1)}, u32[]{:S(2)}) copy-start(bf16[2,128,1024]{2,1,0:T(8,128)(2,1)} %param.35) | copy-start | bytes 1572868
  207.8 14.5 %slice-start.2 = ((s8[8388608]{0:T(1024)(128)(4,1)}), s8[4194304]{0:T(1024)(128)(4,1)S(1)}, s32[]{:S(2)}) async-start(s8[8388608]{0:T(1024)(128)(4,1)} %bitcast.99), calls=%async_computation.2 | async-start | bytes 8388608
  209.3 27.5 %copy-start.6 = (bf16[256,1024]{1,0:T(8,128)(2,1)}, bf16[256,1024]{1,0:T(8,128)(2,1)S(1)}, u32[]{:S(2)}) copy-start(bf16[256,1024]{1,0:T(8,128)(2,1)S(1)} %get-tuple-element.58) | copy-start | bytes 1572868
  209.3 13.0 %slice-start.3 = ((s8[8388608]{0:T(1024)(128)(4,1)}), s8[4194304]{0:T(1024)(128)(4,1)S(1)}, s32[]{:S(2)}) async-start(s8[8388608]{0:T(1024)(128)(4,1)} %bitcast.99), calls=%async_computation.3 | async-start | bytes 8388608
  222.2 39.2 %collective-permute-start.4 = (bf16[256,4096]{1,0:T(8,128)(2,1)}, bf16[256,4096]{1,0:T(8,128)(2,1)}, u32[]{:S(2)}, u32[]{:S(2)}) collective-permute-start(bf16[256,4096]{1,0:T(8,128)(2,1)} %get-tuple-element.60), channel_id=1, source_target_pairs={{0,16},{16,0},{1,17},{17,1},{2,18},{18,2},{3,19},{19,3},{4,20},{20... | collective-permute-start | bytes 6291464 | tf_op jit(solution)/shard_map/ppermute | solution.py:1018
  228.4 23.0 %collective-permute-start.6 = (bf16[256,1024]{1,0:T(8,128)(2,1)}, bf16[256,1024]{1,0:T(8,128)(2,1)}, u32[]{:S(2)}, u32[]{:S(2)}) collective-permute-start(bf16[256,1024]{1,0:T(8,128)(2,1)} %get-tuple-element.62), channel_id=1, source_target_pairs={{0,16},{16,0},{1,17},{17,1},{2,18},{18,2},{3,19},{19,3},{4,20},{20... | collective-permute-start | bytes 1572872 | tf_op jit(solution)/shard_map/ppermute | solution.py:1018
  229.7 0.8 copy-start.8
  230.5 16.4 %collective-permute-start.7 = (f32[16,16,128]{2,1,0:T(8,128)}, f32[16,16,128]{2,1,0:T(8,128)S(1)}, u32[]{:S(2)}, u32[]{:S(2)}) collective-permute-start(f32[16,16,128]{2,1,0:T(8,128)} %dynamic-slice_bitcast_fusion.2), channel_id=1, source_target_pairs={{0,16},{16,0},{1,17},{17,1},{2,18},{18,2},{3,19},{19,3},{4,20},{20... | collective-permute-start | bytes 393224 | tf_op jit(solution)/shard_map/ppermute | solution.py:1018
  230.5 6.3 %copy-start.3 = (bf16[256,4096]{1,0:T(8,128)(2,1)S(1)}, bf16[256,4096]{1,0:T(8,128)(2,1)}, u32[]{:S(2)}) copy-start(bf16[256,4096]{1,0:T(8,128)(2,1)} %copy-done.2) | copy-start | bytes 6291460
  236.8 4.5 %copy-start.5 = (bf16[32,32,1024]{2,1,0:T(8,128)(2,1)S(1)}, bf16[32,32,1024]{2,1,0:T(8,128)(2,1)}, u32[]{:S(2)}) copy-start(bf16[32,32,1024]{2,1,0:T(8,128)(2,1)} %get-tuple-element.34) | copy-start | bytes 6291460
  241.3 2.6 copy-start.4
  246.9 7.3 %collective-permute-start.2 = (bf16[256,1024]{1,0:T(8,128)(2,1)}, bf16[256,1024]{1,0:T(8,128)(2,1)S(1)}, u32[]{:S(2)}, u32[]{:S(2)}) collective-permute-start(bf16[256,1024]{1,0:T(8,128)(2,1)} %copy-done.6), channel_id=1, source_target_pairs={{0,16},{16,0},{1,17},{17,1},{2,18},{18,2},{3,19},{19,3},{4,20},{20... | collective-permute-start | bytes 1572872 | tf_op jit(solution)/shard_map/ppermute | solution.py:1018
  247.4 3.6 collective-permute-start.5
  251.0 10.4 %collective-permute-start.3 = (bf16[256,512]{1,0:T(8,128)(2,1)}, bf16[256,512]{1,0:T(8,128)(2,1)S(1)}, u32[]{:S(2)}, u32[]{:S(2)}) collective-permute-start(bf16[256,512]{1,0:T(8,128)(2,1)} %constant_dynamic-slice_fusion.1), channel_id=1, source_target_pairs={{0,16},{16,0},{1,17},{17,1},{2,18},{18,2},{3,19},{19,3},{4,20},{20... | collective-permute-start | bytes 786440 | tf_op jit(solution)/shard_map/ppermute | solution.py:1018
  251.4 10.0 %slice-start = ((s8[8388608]{0:T(1024)(128)(4,1)}), s8[4194304]{0:T(1024)(128)(4,1)S(1)}, s32[]{:S(2)}) async-start(s8[8388608]{0:T(1024)(128)(4,1)} %bitcast.72), calls=%async_computation | async-start | bytes 8388608
  254.2 7.2 %slice-start.1 = ((s8[8388608]{0:T(1024)(128)(4,1)}), s8[4194304]{0:T(1024)(128)(4,1)S(1)}, s32[]{:S(2)}) async-start(s8[8388608]{0:T(1024)(128)(4,1)} %bitcast.72), calls=%async_computation.1 | async-start | bytes 8388608
  435.2 10.4 %copy-start.7 = (f32[256,1024]{1,0:T(8,128)S(1)}, f32[256,1024]{1,0:T(8,128)}, u32[]{:S(2)}) copy-start(f32[256,1024]{1,0:T(8,128)} %get-tuple-element.42) | copy-start | bytes 3145732
  435.2 11.3 %copy-start.10 = (f32[32,1024]{1,0:T(8,128)S(1)}, f32[32,1024]{1,0:T(8,128)}, u32[]{:S(2)}) copy-start(f32[32,1024]{1,0:T(8,128)} %get-tuple-element.119) | copy-start | bytes 393220
  435.2 13.9 %copy-start.9 = (f32[128,1024]{1,0:T(8,128)S(1)}, f32[128,1024]{1,0:T(8,128)}, u32[]{:S(2)}) copy-start(f32[128,1024]{1,0:T(8,128)} %get-tuple-element.125) | copy-start | bytes 1572868

commit v3 on v2

--- a/solution.py
+++ b/solution.py
@@ -469,6 +469,8 @@
     for z in (0, 4, 8, 12):
         for g in first:
             g.on_plane(z)
+    for g in rest:
+        g.start_plane()
     for z in (0, 4, 8, 12):
         for g in first:
             g.on_diagonal(z)
@@ -477,16 +479,18 @@
     keep = pltpu.make_async_copy(w_qkv, o_qkv, local_sem.at[6])
     keep.start()
 
-    @pl.loop(0, 8)
-    def _(p):
-        w = w_qkv[:, :, pl.ds(pl.multiple_of(p * 384, 128), 384)].reshape(1024, 384)
-        t = jnp.dot(x_ref[...], w, preferred_element_type=f32).T
-        for i in range(2):
-            h = 2 * p + i
-            for part in range(3):
-                rows = t[192 * i + 64 * part : 192 * i + 64 * part + 64]
+    for part in range(3):
+
+        @pl.loop(0, 4)
+        def _(p):
+            w = w_qkv[:, :, pl.ds(pl.multiple_of(part * 1024 + p * 256, 256), 256)].reshape(1024, 256)
+            t = jnp.dot(x_ref[...], w, preferred_element_type=f32).T
+            for i in range(4):
+                h = 4 * p + i
+                rows = t[64 * i : 64 * i + 64]
                 if part != 1:
-                    bias = jnp.concatenate([w_bias[2 * h + k, pl.ds(0 if part == 0 else 32, 32)] for k in range(2)], 0).astype(f32)
+                    own = pl.ds(0 if part == 0 else 32, 32)
+                    bias = jnp.concatenate([w_bias[2 * h + k, own] for k in range(2)], 0).astype(f32)
                     rows = rows + jnp.concatenate([bias, bias], 1)
                 send_blk[h, pl.ds(64 * part, 64)] = rows.astype(bf16)
 
@@ -515,13 +519,11 @@
                 src_ref=here, dst_ref=here, send_sem=hsend.at[i], recv_sem=hrecv.at[i], device_id=sib, device_id_type=MESH
             ).wait_recv()
 
-    for g in rest:
-        g.start_plane()
     rest[3].start_z()
     events = []
+    events.append(lambda: [g.on_plane(0) for g in rest])
     for z in (4, 8, 12):
         events.append(lambda z=z: [g.on_z(z) for g in rest[:3]])
-    events.append(lambda: [g.on_plane(0) for g in rest])
     events.append(lambda: [g.on_diagonal(0) for g in rest])
     for z in (4, 8, 12):
         events.append(lambda z=z: [g.on_plane(z) for g in rest[:3]])
@@ -574,7 +576,7 @@
 
         ctx_recv[chip, :, pl.ds(128 * s, 128)] = ctx_blk[s, chip]
 
-    PRE, FIRST, SECOND = 2, 2, 6
+    PRE, FIRST, SECOND = 5, 3, 6
     for event in events[:PRE]:
         event()
     heads_here(0)
@@ -664,7 +666,7 @@
 
     def __init__(self, copies, name, grads, out, bufs):
         self.copies, self.name, self.grads, self.out = copies, name, grads, out
-        self.first, self.second, self.third, self.passed = bufs
+        self.first, self.second, self.third = bufs
         self.core, self.chip = place()
         self.rows = grads.shape[1]
         self.half = self.rows // 2
@@ -672,13 +674,12 @@
         self.first_at = [[self.first.at[k, i] for i in range(2)] for k in range(4)]
         self.second_at = [[self.second.at[k, i] for i in range(2)] for k in range(4)]
         self.third_at = [self.third.at[k] for k in range(3)]
-        self.passed_at = [self.passed.at[k] for k in range(3)]
 
     def at(self, bits):
         return (self.core, flip(self.chip, bits))
 
     def send(self, tag, src, dst, bits, half=True):
-        like = self.first_at[0][0] if half else self.passed_at[0]
+        like = self.first_at[0][0] if half else self.third_at[0]
         self.copies.send((self.name, tag), src, dst, self.at(bits), like)
 
     def arrived(self, tag, dst):
@@ -737,13 +738,13 @@
             total = self.grads.at[owner][rows].astype(f32) + self.second_at[k][0][rows].astype(f32)
             total = total + self.second_at[k][1][rows].astype(f32)
             if k < 3:
-                self.passed_at[k][rows] = total.astype(self.passed.dtype)
+                self.second_at[k][0][rows] = total.astype(self.second.dtype)
             else:
                 self.out[rows] = total
 
         self.add(self.rows, fn)
         if k < 3:
-            self.send(("3", k), self.passed_at[k], self.third_at[k], z, False)
+            self.send(("3", k), self.second_at[k][0], self.third_at[k], z, False)
 
     def on_third(self):
         for k in range(3):
@@ -765,19 +766,22 @@
         pltpu.VMEM((4, 2, rows // 2, cols), dtype),
         pltpu.VMEM((4, 2, rows, cols), dtype),
         pltpu.VMEM((3, rows, cols), dtype),
-        pltpu.VMEM((3, rows, cols), dtype),
     ]
 
 
 def bwd_kernel(*refs):
     f32, bf16 = jnp.float32, jnp.bfloat16
-    (lengths_ref, pairs, o_full, lse_ref, d_ctx, x_t, d_first, g_reduce, g_expand, g_out, g_vec, h_qkv) = refs[:12]
-    (o_reduce, o_expand, o_out, o_vec, o_qkv, o_input, o_bias) = refs[12:19]
-    bufs = [refs[19 + 4 * i : 23 + 4 * i] for i in range(5)]
     (
-        g_qkv, w_qkv, d_recv, kk, vv, kt, acc, d_send, d_own, d_sib, b_own, b_sib, b_in,
-        send_sem, recv_sem, local_sem, dsend, drecv, qsend, qrecv,
-    ) = refs[39:]
+        lengths_ref, pairs, o_full, lse_ref, x_t, normed_t, context_t, d_second, scaled, spread, gain, g_reduce, vec_in,
+        h_slope, h_reduce, h_expand, h_out, h_qkv,
+    ) = refs[:18]
+    (o_reduce, o_expand, o_out, o_vec, o_qkv, o_input, o_bias) = refs[18:25]
+    bufs = [refs[25 + 3 * i : 28 + 3 * i] for i in range(5)]
+    (
+        g_expand, g_out, g_vec, g_qkv, w_qkv, d_recv, kk, vv, kt, acc, d_send, d_own, d_sib, b_own, b_sib, b_in,
+        slopes, w_reduce, w_expand, w_out, e_own, e_sib, d_first, a_own, a_sib, d_ctx, rows_sum, e_sum, vec_own, vec_sib,
+        send_sem, recv_sem, local_sem, dsend, drecv, qsend, qrecv, esend, erecv, wsem,
+    ) = refs[40:]
     core, chip = place()
     sib = (1 - core, chip)
     greet([sib] + [(core, flip(chip, b)) for b in range(1, 16)])
@@ -787,8 +791,77 @@
         for i, (g, o) in enumerate(((g_reduce, o_reduce), (g_expand, o_expand), (g_out, o_out), (g_vec, o_vec)))
     ]
     last = Scatter(copies, 4, g_qkv, o_qkv, bufs[4])
-    weights = pltpu.make_async_copy(h_qkv, w_qkv, local_sem.at[0])
-    weights.start()
+    rest[0].start()
+    rest[0].start_direct()
+    out_weights = pltpu.make_async_copy(h_out, w_out, local_sem.at[4])
+    out_weights.start()
+
+    def fetch(c, slot):
+        return (
+            pltpu.make_async_copy(h_reduce.at[pl.ds(c * 4, 4)], w_reduce.at[slot], wsem.at[slot, 0]),
+            pltpu.make_async_copy(
+                h_expand.at[:, :, pl.ds(pl.multiple_of(c * 512, 512), 512)], w_expand.at[slot], wsem.at[slot, 1]
+            ),
+            pltpu.make_async_copy(h_slope.at[:, pl.ds(pl.multiple_of(c * 512, 512), 512)], slopes.at[slot], wsem.at[slot, 2]),
+        )
+
+    for c in fetch(0, 0):
+        c.start()
+    a_own[...] = d_second[...].astype(bf16)
+    d_first[...] = d_second[...]
+
+    def e_copy(c):
+        return pltpu.make_async_remote_copy(
+            src_ref=e_own.at[c],
+            dst_ref=e_sib.at[c],
+            send_sem=esend.at[c],
+            recv_sem=erecv.at[c],
+            device_id=sib,
+            device_id_type=MESH,
+        )
+
+    @pl.loop(0, 8)
+    def _(c):
+        slot = lax.rem(c, 2)
+
+        @pl.when(c < 7)
+        def _():
+            for copy in fetch(c + 1, 1 - slot):
+                copy.start()
+
+        for copy in fetch(c, slot):
+            copy.wait()
+        d_active = nt(a_own[...], w_reduce[slot].reshape(512, 1024))
+        d_expanded = (d_active * slopes[slot].astype(f32)).astype(bf16)
+        e_own[c] = d_expanded
+        e_copy(c).start()
+        e_sum[pl.ds(c, 1)] = jnp.sum(d_expanded.astype(f32), 0, keepdims=True)
+        d_first[...] += nt(d_expanded, w_expand[slot].reshape(1024, 512))
+
+    rows_sum[...] = jnp.zeros_like(rows_sum)
+
+    @pl.loop(0, 4)
+    def _(i):
+        span = pl.ds(pl.multiple_of(i * 64, 64), 64)
+        d_normed, x_hat = d_first[span], scaled[span]
+        pulled = d_normed * gain[...]
+        level = jnp.mean(pulled, -1, keepdims=True)
+        slope = jnp.mean(pulled * x_hat, -1, keepdims=True)
+        d_rows = spread[span] * (pulled - level - x_hat * slope)
+        d_low = d_rows.astype(bf16)
+        d_first[span] = d_rows
+        a_own[span] = d_low
+        rows_sum[0:1] += jnp.sum(d_low.astype(f32), 0, keepdims=True)
+        rows_sum[1:2] += jnp.sum(d_normed * x_hat, 0, keepdims=True)
+        rows_sum[2:3] += jnp.sum(d_normed, 0, keepdims=True)
+
+    out_weights.wait()
+
+    @pl.loop(0, 4)
+    def _(i):
+        t = nt(w_out[pl.ds(i * 8, 8)].reshape(256, 1024), a_own[...])
+        d_ctx[pl.ds(i * 4, 4)] = t.astype(bf16).reshape(4, 64, 256)
+
     sent = []
 
     def exchange_out(s, b, src, dst, sends, recvs):
@@ -818,11 +891,53 @@
         for b in FULL_ORDER:
             exchange_out(s, b, d_ctx.at[flip(chip, b), :, lane], d_recv.at[s, chip], dsend, drecv)
         d_recv[s, chip] = d_ctx[chip, :, lane]
-    for r in rest:
+    copies.send("a", a_own, a_sib, sib, a_own)
+
+    vec_own[...] = vec_in[...]
+    owner = lax.broadcasted_iota(jnp.int32, (32, 1024), 0)
+    column = lax.broadcasted_iota(jnp.int32, (32, 1024), 1)
+    place_in = lax.rem(lax.broadcasted_iota(jnp.int32, (1024, 128), 0), 32)
+    pick = jnp.where(place_in == lax.broadcasted_iota(jnp.int32, (1024, 128), 1), 1.0, 0.0).astype(bf16)
+    for r in range(3):
+        spread_row = jnp.where(lax.div(column, 32) == owner, rows_sum[r : r + 1], 0.0)
+        top = spread_row.astype(bf16)
+        low = (spread_row - top.astype(f32)).astype(bf16)
+        vec_own[:, r, :] = jnp.dot(top, pick, preferred_element_type=f32) + jnp.dot(low, pick, preferred_element_type=f32)
+    for o in range(32):
+        vec_own[o, 3:4, :] = e_sum[o // 4 : o // 4 + 1, 128 * (o % 4) : 128 * (o % 4) + 128]
+    own_half, other_half = pl.ds(core * 16, 16), pl.ds((1 - core) * 16, 16)
+    copies.send("v", vec_own.at[other_half], vec_sib, sib, vec_sib)
+
+    for k in range(4):
+        rest[0].on_first(k)
+
+    @pl.loop(0, 8)
+    def _(c):
+        e_copy(c).wait()
+        g = jnp.dot(normed_t[:, :256], e_own[c], preferred_element_type=f32)
+        g = g + jnp.dot(normed_t[:, 256:], e_sib[c], preferred_element_type=f32)
+        g_expand[:, :, pl.ds(pl.multiple_of(c * 512, 512), 512)] = g.astype(bf16).reshape(16, 32, 512)
+
+    rest[1].start()
+    rest[1].start_direct()
+    copies.arrived("a", a_sib, sib)
+    for i in range(4):
+        cols = slice(256 * i, 256 * i + 256)
+        g = jnp.dot(context_t[:, :256], a_own[:, cols], preferred_element_type=f32)
+        g = g + jnp.dot(context_t[:, 256:], a_sib[:, cols], preferred_element_type=f32)
+        g_out[:, :, cols] = g.astype(bf16).reshape(16, 32, 256)
+    copies.arrived("v", vec_sib, sib)
+    g_vec[...] = vec_own[own_half] + vec_sib[...]
+    for r in rest[2:]:
         r.start()
-    for r in rest:
         r.start_direct()
     b_own[...] = jnp.zeros_like(b_own)
+
+    def fetch_qkv(i, slot):
+        return pltpu.make_async_copy(h_qkv.at[pl.ds(i * 8, 8)], w_qkv.at[slot], local_sem.at[5 + slot])
+
+    fetch_qkv(0, 0).start()
+    fetch_qkv(1, 1).start()
 
     def back_sequence(s, during):
         load_sequence(pairs, s, kk, vt_ref=None, vv_ref=vv)
@@ -870,8 +985,10 @@
             exchange_out(s, b, d_send.at[s, flip(chip, b)], d_own.at[chip, :, lane], qsend, qrecv)
         d_own[chip, :, lane] = d_send[s, chip]
 
-    events = [lambda k=k: [r.on_first(k) for r in rest] for k in range(4)]
-    events += [lambda k=k: [r.on_second(k) for r in rest] for k in range(4)]
+    for k in range(4):
+        rest[0].on_second(k)
+    events = [lambda k=k: [r.on_first(k) for r in rest[1:]] for k in range(4)]
+    events += [lambda k=k: [r.on_second(k) for r in rest[1:]] for k in range(4)]
     FIRST, SECOND, WAIT = 0, 4, 2
     for b in FULL_ORDER:
         exchange_in(0, b, d_recv.at[0, flip(chip, b)], dsend, drecv)
@@ -893,13 +1010,17 @@
     for s in range(2):
         copies.arrived(("rows", s), d_sib.at[:, :, pl.ds(128 * s, 128)], sib)
 
-    @pl.loop(0, 8)
-    def _(p):
-        total = None
-        for i, rows in enumerate((d_own, d_sib)):
-            term = nt(x_t[:, 256 * i : 256 * i + 256], rows[pl.ds(2 * p, 2)].reshape(384, 256))
-            total = term if total is None else total + term
-        g_qkv[:, :, pl.ds(pl.multiple_of(p * 384, 128), 384)] = total.astype(bf16).reshape(16, 32, 384)
+    for part in range(3):
+
+        @pl.loop(0, 4)
+        def _(p):
+            total = None
+            for i, rows in enumerate((d_own, d_sib)):
+                right = rows[pl.ds(4 * p, 4), pl.ds(64 * part, 64)].reshape(256, 256)
+                term = nt(x_t[:, 256 * i : 256 * i + 256], right)
+                total = term if total is None else total + term
+            cols = pl.ds(pl.multiple_of(part * 1024 + p * 256, 256), 256)
+            g_qkv[:, :, cols] = total.astype(bf16).reshape(16, 32, 256)
 
     last.start()
     last.start_direct()
@@ -926,14 +1047,17 @@
         def _():
             b_in[...] = b_sib[:, rows]
 
-    weights.wait()
-
-    @pl.loop(0, 4)
-    def _(i):
-        w = w_qkv[pl.ds(i * 8, 8)].reshape(256, 3072)
-        t = jnp.dot(w, d_own[...].reshape(3072, 256), preferred_element_type=f32).T
-        cols = pl.ds(pl.multiple_of(i * 256, 256), 256)
-        o_input[:, cols] = d_first[:, cols] + t
+    for i in range(4):
+        fetch_qkv(i, i % 2).wait()
+        t = None
+        for part in range(3):
+            w = w_qkv[i % 2, :, :, 1024 * part : 1024 * part + 1024].reshape(256, 1024)
+            term = jnp.dot(w, d_own[:, 64 * part : 64 * part + 64].reshape(1024, 256), preferred_element_type=f32)
+            t = term if t is None else t + term
+        if i < 2:
+            fetch_qkv(i + 2, i).start()
+        cols = slice(256 * i, 256 * i + 256)
+        o_input[:, cols] = d_first[:, cols] + t.T
 
     for event in events[FIRST + SECOND + WAIT :]:
         event()
@@ -970,48 +1094,75 @@
     copies.drain(sib)
 
 
-def backward_attention(lengths, pairs, o_full, lse, d_ctx, x_t, d_first, grads, w_qkv, collective_id):
+def backward_attention(
+    lengths, pairs, o_full, lse, x_t, normed_t, context_t, d_second, scaled, spread, gain, g_reduce, vec_in,
+    slope, w_reduce, w_expand, w_out, w_qkv, collective_id,
+):
     v, hbm = pl.BlockSpec(memory_space=pltpu.VMEM), pl.BlockSpec(memory_space=pl.ANY)
     f32, bf16 = jnp.float32, jnp.bfloat16
     dma = pltpu.SemaphoreType.DMA
-    blocks = [(g.shape[1:], g.dtype) for g in grads] + [((32, 3072), bf16)]
+    blocks = [((128, 1024), bf16), ((32, 4096), bf16), ((32, 1024), bf16), ((16, 128), f32), ((32, 3072), bf16)]
     bufs = []
     for block, dtype in blocks:
         bufs += scatter_buffers(block, dtype)
+    vmem = lambda shape, dtype=bf16: pltpu.VMEM(shape, dtype)
     return pl.pallas_call(
         bwd_kernel,
         out_shape=[jax.ShapeDtypeStruct(block, f32) for block, _ in blocks]
-        + [jax.ShapeDtypeStruct(d_first.shape, f32), jax.ShapeDtypeStruct((2, 32, 128), f32)],
-        in_specs=[pl.BlockSpec(memory_space=pltpu.SMEM)] + [v] * 10 + [hbm],
+        + [jax.ShapeDtypeStruct((256, 1024), f32), jax.ShapeDtypeStruct((2, 32, 128), f32)],
+        in_specs=[pl.BlockSpec(memory_space=pltpu.SMEM)] + [v] * 12 + [hbm] * 5,
         out_specs=[v] * 7,
         scratch_shapes=bufs
         + [
-            pltpu.VMEM((16, 32, 3072), bf16),
-            pltpu.VMEM((32, 32, 3072), bf16),
-            pltpu.VMEM((2, 16, 64, 128), bf16),
-            pltpu.VMEM((2048, 64), bf16),
-            pltpu.VMEM((2048, 64), bf16),
-            pltpu.VMEM((64, 2048), bf16),
-            pltpu.VMEM((2048, 128), f32),
-            pltpu.VMEM((2, 16, 192, 128), bf16),
-            pltpu.VMEM((16, 192, 256), bf16),
-            pltpu.VMEM((16, 192, 256), bf16),
-            pltpu.VMEM((2, 64, 128), f32),
-            pltpu.VMEM((2, 64, 128), f32),
-            pltpu.VMEM((2, 32, 128), f32),
-            dma((140,)),
-            dma((140,)),
-            dma((4,)),
+            vmem((16, 32, 4096)),
+            vmem((16, 32, 1024)),
+            vmem((16, 16, 128), f32),
+            vmem((16, 32, 3072)),
+            vmem((2, 8, 32, 3072)),
+            vmem((2, 16, 64, 128)),
+            vmem((2048, 64)),
+            vmem((2048, 64)),
+            vmem((64, 2048)),
+            vmem((2048, 128), f32),
+            vmem((2, 16, 192, 128)),
+            vmem((16, 192, 256)),
+            vmem((16, 192, 256)),
+            vmem((2, 64, 128), f32),
+            vmem((2, 64, 128), f32),
+            vmem((2, 32, 128), f32),
+            vmem((2, 256, 512)),
+            vmem((2, 4, 128, 1024)),
+            vmem((2, 32, 32, 512)),
+            vmem((32, 32, 1024)),
+            vmem((8, 256, 512)),
+            vmem((8, 256, 512)),
+            vmem((256, 1024), f32),
+            vmem((256, 1024)),
+            vmem((256, 1024)),
+            vmem((16, 64, 256)),
+            vmem((8, 1024), f32),
+            vmem((8, 512), f32),
+            vmem((32, 16, 128), f32),
+            vmem((16, 16, 128), f32),
+            dma((144,)),
+            dma((144,)),
+            dma((7,)),
             dma((32,)),
             dma((32,)),
             dma((32,)),
             dma((32,)),
+            dma((8,)),
+            dma((8,)),
+            dma((2, 3)),
         ],
         compiler_params=pltpu.CompilerParams(
-            collective_id=collective_id, has_side_effects=True, vmem_limit_bytes=62 * MIB
+            collective_id=collective_id, has_side_effects=True, vmem_limit_bytes=63 * MIB
         ),
         name="backward_attention",
-    )(lengths, pairs, o_full, lse, d_ctx, x_t, d_first, *grads, w_qkv)
+    )(
+        lengths, pairs, o_full, lse, x_t, normed_t, context_t, d_second, scaled, spread, gain, g_reduce, vec_in,
+        slope, w_reduce, w_expand, w_out, w_qkv,
+    )
 
 
 def swap(x):
@@ -1054,17 +1205,15 @@
     second_shift,
     cotangent,
 ):
-    core = lax.axis_index("fsdp")
     f32, bf16 = jnp.float32, jnp.bfloat16
     seqs, count, width = inputs.shape
     total = seqs * count
     part = width // 32
     ff = w_expand.shape[1]
-    qkv = jnp.concatenate([w.reshape(part, HEADS, 64) for w in (w_query, w_key, w_value)], -1).reshape(part, 3 * width)
+    qkv = jnp.concatenate([w_query, w_key, w_value], 1)
     bias = jnp.concatenate([b_query, b_value])[:, None] + jnp.zeros((2 * part, 128), bf16)
     small = [b_out, first_gain, first_shift, b_expand, b_reduce, second_gain, second_shift]
-    sizes = [b.shape[0] for b in small]
-    vec = jnp.concatenate(small + [jnp.zeros((part * 128 - sum(sizes),), bf16)]).reshape(part, 128)
+    vec = sum(jnp.pad(b[None, :], ((r, part - 1 - r), (0, 128 - b.shape[0]))) for r, b in enumerate(small))
     flat_rows = inputs.reshape(total, width)
     g_vec, g_out, g_expand, g_reduce, g_qkv, pairs, context_t, o_full, lse = forward_attention(
         flat_rows, lengths, qkv, bias, vec, w_out, w_expand, w_reduce, 1
@@ -1072,22 +1221,23 @@
     full_out = g_out.reshape(width, width)
     full_expand = g_expand.reshape(width, ff)
     full_reduce = g_reduce.reshape(ff, width)
-    flat_vec = g_vec.reshape(32, part * 128)
-    offsets = [sum(sizes[:i]) for i in range(len(sizes) + 1)]
-    (bias_out, gain_first, shift_first, bias_expand, bias_reduce, gain_second, shift_second) = [
-        flat_vec[:, offsets[i] : offsets[i + 1]].reshape(-1).astype(f32) for i in range(len(sizes))
-    ]
+    bias_out, gain_first, shift_first, bias_expand, bias_reduce, gain_second, shift_second = (
+        g_vec[:, r, : b.shape[0]].reshape(1, -1).astype(f32) for r, b in enumerate(small)
+    )
     own_first = lax.axis_index("ctx") * count
     positions = own_first + jnp.arange(count, dtype=jnp.int32)
     valid_rows = (positions[None, :] < lengths[:, None]).astype(f32).reshape(total, 1)
     context_t = context_t.reshape(width, total)
-    attended = outer_sum(context_t, full_out) + bias_out
-    residual = flat_rows.astype(f32) + attended
-    normed, first_pull = jax.vjp(layer_norm, residual, gain_first, shift_first)
+    residual = flat_rows.astype(f32) + outer_sum(context_t, full_out) + bias_out
+    center = residual - jnp.mean(residual, -1, keepdims=True)
+    spread = lax.rsqrt(jnp.mean(center * center, -1, keepdims=True) + epsilon)
+    scaled = center * spread
+    normed = scaled * gain_first + shift_first
     normed_low = normed.astype(bf16)
     expanded = product(normed_low, full_expand) + bias_expand
-    activated, gelu_pull = jax.vjp(partial(jax.nn.gelu, approximate=False), expanded)
-    activated_low = activated.astype(bf16)
+    share = 0.5 * (1.0 + lax.erf(expanded * math.sqrt(0.5)))
+    slope = (share + expanded * jnp.exp(-0.5 * expanded * expanded) * (1.0 / math.sqrt(2.0 * math.pi))).astype(bf16)
+    activated_low = (expanded * share).astype(bf16)
     reduced = product(activated_low, full_reduce) + bias_reduce
     final_rows, second_pull = jax.vjp(layer_norm, normed + reduced, gain_second, shift_second)
     layer_out = (final_rows * valid_rows).astype(bf16).reshape(inputs.shape)
@@ -1096,46 +1246,18 @@
     d_reduced = d_second.astype(bf16)
     reduce_grad = chip_sum(activated_low, d_reduced)
     reduce_bias_grad = jnp.sum(d_reduced.astype(f32), 0)
-    (d_expanded_full,) = gelu_pull(back_product(d_reduced, full_reduce))
-    d_expanded = d_expanded_full.astype(bf16)
-    expand_grad = chip_sum(normed_low, d_expanded)
-    expand_bias_grad = jnp.sum(d_expanded.astype(f32), 0)
-    d_normed = d_second + back_product(d_expanded, full_expand)
-    d_first, first_gain_grad, first_shift_grad = first_pull(d_normed)
-    d_attended = d_first.astype(bf16)
-    context_own, context_other = halves(context_t)
-    out_grad = product(context_own, d_attended) + product(context_other, swap(d_attended))
-    out_grad = out_grad.astype(bf16).reshape(16, part, width)
-    out_bias_grad = jnp.sum(d_attended.astype(f32), 0)
-    d_context_t = back_product(full_out, d_attended).astype(bf16).reshape(HEADS, 64, total)
-    x_t = jnp.concatenate(halves(flat_rows.T), 1)
-    small_grads = jnp.concatenate(
-        [
-            g.reshape(32, -1)
-            for g in (
-                out_bias_grad,
-                first_gain_grad,
-                first_shift_grad,
-                expand_bias_grad,
-                reduce_bias_grad,
-                second_gain_grad,
-                second_shift_grad,
-            )
-        ]
-        + [jnp.zeros((32, 2048 - sum(sizes)), f32)],
-        1,
-    ).reshape(2, 16, 16, 128)
-    vec_grad = lax.dynamic_index_in_dim(small_grads, core, 0, False) + swap(
-        lax.dynamic_index_in_dim(small_grads, 1 - core, 0, False)
-    )
+    vec_in = sum(
+        jnp.pad(g.reshape(32, 1, part), ((0, 0), (r, 15 - r), (0, 128 - part)))
+        for r, g in ((4, reduce_bias_grad), (5, second_gain_grad), (6, second_shift_grad))
+    )
+    both = lambda rows_t: jnp.concatenate(halves(rows_t), 1)
     s_reduce, s_expand, s_out, s_vec, s_qkv, input_grad, s_bias = backward_attention(
-        lengths, pairs, o_full, lse, d_context_t, x_t, d_first, [reduce_grad, expand_grad, out_grad, vec_grad], g_qkv, 2
-    )
-    s_qkv = s_qkv.reshape(part, HEADS, 3, 64)
-    s_query, s_key, s_value = (s_qkv[:, :, i].reshape(part, width) for i in range(3))
+        lengths, pairs, o_full, lse, both(flat_rows.T), both(normed_low.T), both(context_t), d_second, scaled, spread,
+        gain_first, reduce_grad, vec_in, slope, g_reduce, g_expand, g_out, g_qkv, 2,
+    )
+    s_query, s_key, s_value = (s_qkv[:, width * i : width * (i + 1)] for i in range(3))
     s_bias = jnp.sum(s_bias, -1)
-    s_vec = s_vec.reshape(-1)
-    v = [s_vec[offsets[i] : offsets[i + 1]] for i in range(len(sizes))]
+    v = [s_vec[r, : b.shape[0]] for r, b in enumerate(small)]
     return (
         layer_out,
         input_grad.reshape(inputs.shape),

time: 458 us -> 399 us (0.87); the launches traced: 450 us -> 396 us
  matrix products: 71.7 us -> 26 us
  local copies, waits for them, and re-layouts: 33.5 us -> 22.7 us
  other arithmetic: 9.24 us -> 16.8 us
    dot_general x3 -> x0, matrix products: 19.9 us -> none  [back_product(): jnp.einsum('re,de->rd', grad_rows, weight, preferred_element_type=jnp.flo...]
    dot_general x4 -> x2, matrix products: 26.4 us -> 10.5 us  [product(): return jnp.dot(left, right, preferred_element_type=jnp.float32)]
    dot_general x5 -> x3, matrix products: 25.4 us -> 15.5 us  [outer_sum(): jnp.einsum('rd,re->de', left, right, preferred_element_type=jnp.float32)]
    pallas_call x1, Pallas kernels: 162 us -> 154 us  [forward_attention(): pl.pallas_call(fwd_kernel, out_shape=[gathered(vec), gathered(w_out), gat...]
    reshape x11 -> x3, local copies, waits for them, and re-layouts: 5.95 us -> 0.26 us  [fast_shards(): g.reshape(32, 1, part)]
    pallas_call x1, Pallas kernels: 169 us -> 174 us  [backward_attention(): pl.pallas_call(bwd_kernel, out_shape=[jax.ShapeDtypeStruct(block, f32) fo...]
  transfers between devices with their start and end apart: 8 -> 5, of which waited for: 0 -> 0; matrix products, arithmetic and copies ran while one was open for 20% -> 5% of each run, Pallas kernels for 36% -> 0%
where the time goes in v3:
time: 399 us; the launch traced here: 396 us
  Pallas kernels  328 us (82%)
  matrix products  26 us (7%)
  local copies, waits for them, and re-layouts  22.7 us (6%)
  other arithmetic  16.8 us (4%)
    pallas_call x1, Pallas kernels, backward_attention(): pl.pallas_call(bwd_kernel, out_shape=[jax.ShapeDtypeStruct(block, f32) fo...  174 us
    pallas_call x1, Pallas kernels, forward_attention(): pl.pallas_call(fwd_kernel, out_shape=[gathered(vec), gathered(w_out), gat...  154 us
    dot_general x3, matrix products, outer_sum(): jnp.einsum('rd,re->de', left, right, preferred_element_type=jnp.float32)  15.5 us
    dot_general x2, matrix products, product(): return jnp.dot(left, right, preferred_element_type=jnp.float32)  10.5 us
  transfers between devices with their start and end apart: 5, of which 0 were waited for; matrix products, arithmetic and copies ran while one was open for 5% of the time, Pallas kernels for 0%

profile of v3, /device:TPU:0, one launch (start us, length us, event | category | flops | bytes accessed | tf_op | source)
XLA Modules:
  0.0 396.4 jit_solution(12134428561465793072)
XLA Ops:
  1.4 1.6 pad_maximum_fusion.3.s_qkv
  3.0 1.4 pad_add_fusion.1.s_vec
  5.0 153.6 %forward_attention.1 = (bf16[32,32,128]{2,1,0:T(8,128)(2,1)}, bf16[32,32,1024]{2,1,0:T(8,128)(2,1)}, bf16[32,32,4096]{2,1,0:T(8,128)(2,1)}, bf16[32,128,1024]{2,...) custom-call(bf16[256,1024]{1,0:T(8,128)(2,1)} %bitcast.72, ...), custom_call_target="tpu_custom_call" | custom-call | tf_op jit(solution)/shard_map/forward_attention/pallas_call | solution.py:625
  158.6 1.8 convert_reduce_fusion.2
  160.4 0.9 slice_convert_fusion
  161.3 2.7 fusion.17
  164.8 8.1 %fusion.4 = (bf16[256,4096]{1,0:T(8,128)(2,1)}, bf16[256,4096]{1,0:T(8,128)(2,1)S(1)}) fusion(f32[4096]{0:T(1024)S(1)} %bitcast.80, bf16[256,1024]{1,0:T(8,128)(2,1)S(1)} %get-tuple-element.62, bf16[1024,4096]{1,0:T(8,128)(2,1)} %bitcast.67), kind=kOutput, calls=%fused_computation.7 | convolution fusion | flops 2160066560 | bytes 13123584 | tf_op jit(solution)/shard_map/dot_general | solution.py:25
  172.9 2.4 fusion.18
  176.4 1.3 fusion.15
  177.8 1.3 convert_reduce_fusion
  179.1 1.1 collective-permute-start.4
  180.2 2.3 constant_dynamic-slice_fusion
  182.6 1.8 dynamic-slice_bitcast_fusion.1
  184.9 1.8 constant_dynamic-slice_fusion.2
  186.7 0.8 dynamic-slice_bitcast_fusion.3
  188.0 0.9 slice_convert_fusion.1
  188.9 5.6 %fusion.7 = f32[2048,1024]{1,0:T(8,128)} fusion(bf16[256,1024]{1,0:T(8,128)(2,1)} %get-tuple-element.58, bf16[256,4096]{1,0:T(8,128)(2,1)S(1)} %copy-done.4, s32[]{:T(128)S(6)} %select_n.18), kind=kOutput, calls=%fused_computation.19 | convolution fusion | flops 1073741824 | bytes 9961476 | tf_op jit(solution)/shard_map/rd,re->de/dot_general | solution.py:29
  195.7 0.8 copy.39.refs_9_
  197.2 1.0 pad_maximum_fusion.1
  198.2 1.0 copy.38.refs_5_
  199.2 1.0 pad_maximum_fusion
  200.2 1.0 copy.37.refs_4_
  201.2 1.8 pad_maximum_fusion.2.refs_6_
  203.0 7.2 %add_convert_fusion = bf16[2048,1024]{1,0:T(8,128)(2,1)} fusion(f32[2048,1024]{1,0:T(8,128)} %fusion.7, bf16[256,2048]{1,0:T(8,128)(2,1)} %collective-permute-done.3, bf16[256,1024]{1,0:T(8,128)(2,1)} %collective-permute-done.4), kind=kOutput, calls=%fused_computation | convolution fusion | flops 1077936128 | bytes 14155776 | tf_op jit(solution)/shard_map/rd,re->de/dot_general | solution.py:29
  210.2 174.4 %backward_attention.1 = (f32[128,1024]{1,0:T(8,128)}, f32[32,4096]{1,0:T(8,128)}, f32[32,1024]{1,0:T(8,128)}, f32[16,128]{1,0:T(8,128)}, f32[32,3072]{1,0:T(8,12...) custom-call(s32[2]{0:T(128)} %refs_0_.1, bf16[2,16,192,128]{3,2,1,0:T(8,128)(2,1)} %get-tuple-element.38.refs_1_, ...), custom_call_target="tpu_custom_call" | custom-call | tf_op jit(solution)/shard_map/backward_attention/pallas_call | solution.py:1109
  384.6 1.2 slice_bitcast_fusion.3
  385.8 0.8 reduce_sum.107
  386.7 1.4 slice_bitcast_fusion
  388.1 1.8 fusion.16
  389.9 2.3 copy.44
  392.2 1.6 copy.45
  393.8 1.9 copy.46
  (61 shorter events, 7.0 us)
Async XLA Ops:
  164.5 8.4 %slice-start = ((s8[8388608]{0:T(1024)(128)(4,1)}), s8[4194304]{0:T(1024)(128)(4,1)S(1)}, s32[]{:S(2)}) async-start(s8[8388608]{0:T(1024)(128)(4,1)} %bitcast.68), calls=%async_computation | async-start | bytes 8388608
  164.8 8.1 %copy-start.5 = (bf16[256,1024]{1,0:T(8,128)(2,1)}, bf16[256,1024]{1,0:T(8,128)(2,1)S(1)}, u32[]{:S(2)}) copy-start(bf16[256,1024]{1,0:T(8,128)(2,1)S(1)} %get-tuple-element.62) | copy-start | bytes 1572868
  164.8 8.1 %copy-start.2 = (f32[256,1024]{1,0:T(8,128)}, f32[256,1024]{1,0:T(8,128)S(1)}, u32[]{:S(2)}) copy-start(f32[256,1024]{1,0:T(8,128)S(1)} %get-tuple-element.63.refs_8_) | copy-start | bytes 3145732
  164.8 8.1 %slice-start.1 = ((s8[8388608]{0:T(1024)(128)(4,1)}), s8[4194304]{0:T(1024)(128)(4,1)S(1)}, s32[]{:S(2)}) async-start(s8[8388608]{0:T(1024)(128)(4,1)} %bitcast.68), calls=%async_computation.1 | async-start | bytes 8388608
  172.9 2.5 copy-start.3
  172.9 2.8 copy-start.9
  172.9 2.9 copy-start.1
  177.7 8.9 %copy-start = (bf16[2,128,1024]{2,1,0:T(8,128)(2,1)S(1)}, bf16[2,128,1024]{2,1,0:T(8,128)(2,1)}, u32[]{:S(2)}) copy-start(bf16[2,128,1024]{2,1,0:T(8,128)(2,1)} %param.18) | copy-start | bytes 1572868
  177.7 11.1 %copy-start.4 = (bf16[256,4096]{1,0:T(8,128)(2,1)S(1)}, bf16[256,4096]{1,0:T(8,128)(2,1)}, u32[]{:S(2)}) copy-start(bf16[256,4096]{1,0:T(8,128)(2,1)} %copy-done.3) | copy-start | bytes 6291460
  179.1 23.9 %collective-permute-start.4 = (bf16[256,1024]{1,0:T(8,128)(2,1)}, bf16[256,1024]{1,0:T(8,128)(2,1)}, u32[]{:S(2)}, u32[]{:S(2)}) collective-permute-start(bf16[256,1024]{1,0:T(8,128)(2,1)} %get-tuple-element.58), channel_id=1, source_target_pairs={{0,16},{16,0},{1,17},{17,1},{2,18},{18,2},{3,19},{19,3},{4,20},{20... | collective-permute-start | bytes 1572872 | tf_op jit(solution)/shard_map/ppermute | solution.py:1169
  182.5 20.5 %collective-permute-start.3 = (bf16[256,2048]{1,0:T(8,128)(2,1)}, bf16[256,2048]{1,0:T(8,128)(2,1)}, u32[]{:S(2)}, u32[]{:S(2)}) collective-permute-start(bf16[256,2048]{1,0:T(8,128)(2,1)} %constant_dynamic-slice_fusion), channel_id=1, source_target_pairs={{0,16},{16,0},{1,17},{17,1},{2,18},{18,2},{3,19},{19,3},{4,20},{20... | collective-permute-start | bytes 3145736 | tf_op jit(solution)/shard_map/ppermute | solution.py:1169
  184.4 12.8 %collective-permute-start.1 = (bf16[512,256]{0,1:T(8,128)(2,1)}, bf16[512,256]{0,1:T(8,128)(2,1)}, u32[]{:S(2)}, u32[]{:S(2)}) collective-permute-start(bf16[512,256]{0,1:T(8,128)(2,1)} %get-tuple-element.70), channel_id=1, source_target_pairs={{0,16},{16,0},{1,17},{17,1},{2,18},{18,2},{3,19},{19,3},{4,20},{20... | collective-permute-start | bytes 786440 | tf_op jit(solution)/shard_map/ppermute | solution.py:1169
  186.6 14.6 %collective-permute-start.2 = (bf16[512,256]{1,0:T(8,128)(2,1)}, bf16[512,256]{1,0:T(8,128)(2,1)}, u32[]{:S(2)}, u32[]{:S(2)}) collective-permute-start(bf16[512,256]{1,0:T(8,128)(2,1)} %get-tuple-element.68), channel_id=1, source_target_pairs={{0,16},{16,0},{1,17},{17,1},{2,18},{18,2},{3,19},{19,3},{4,20},{20... | collective-permute-start | bytes 786440 | tf_op jit(solution)/shard_map/ppermute | solution.py:1169
  187.5 11.7 %collective-permute-start = (bf16[512,256]{0,1:T(8,128)(2,1)}, bf16[512,256]{0,1:T(8,128)(2,1)}, u32[]{:S(2)}, u32[]{:S(2)}) collective-permute-start(bf16[512,256]{0,1:T(8,128)(2,1)} %get-tuple-element.72), channel_id=1, source_target_pairs={{0,16},{16,0},{1,17},{17,1},{2,18},{18,2},{3,19},{19,3},{4,20},{20... | collective-permute-start | bytes 786440 | tf_op jit(solution)/shard_map/ppermute | solution.py:1169
  188.9 8.4 %copy-start.6 = (bf16[512,256]{0,1:T(8,128)(2,1)S(1)}, bf16[512,256]{0,1:T(8,128)(2,1)}, u32[]{:S(2)}) copy-start(bf16[512,256]{0,1:T(8,128)(2,1)} %get-tuple-element.69) | copy-start | bytes 786436
  188.9 10.3 %copy-start.7 = (bf16[512,256]{0,1:T(8,128)(2,1)S(1)}, bf16[512,256]{0,1:T(8,128)(2,1)}, u32[]{:S(2)}) copy-start(bf16[512,256]{0,1:T(8,128)(2,1)} %get-tuple-element.71) | copy-start | bytes 786436
  384.6 11.1 %copy-start.8 = (f32[128,1024]{1,0:T(8,128)S(1)}, f32[128,1024]{1,0:T(8,128)}, u32[]{:S(2)}) copy-start(f32[128,1024]{1,0:T(8,128)} %get-tuple-element.122) | copy-start | bytes 1572868

commit v4 on v3

--- a/solution.py
+++ b/solution.py
@@ -439,9 +439,11 @@
 
 def fwd_kernel(
     x_ref, lengths_ref, s_qkv, s_bias, s_vec, s_out, s_expand, s_reduce,
-    o_vec, o_out, o_expand, o_reduce, o_qkv, o_pairs, o_ctx, o_full, lse_ref,
-    w_qkv, w_bias, send_blk, recv_blk, ctx_blk, ctx_recv, kk, vt,
-    send_sem, recv_sem, local_sem, hsend, hrecv, csend, crecv,
+    o_out, o_expand, o_reduce, o_qkv, o_pairs, o_full, lse_ref,
+    o_rows, o_scaled, o_spread, o_active, o_slope, o_turned, o_active_t,
+    w_qkv, w_bias, w_vec, w_out, w_expand, send_blk, recv_blk, ctx_blk, ctx_recv, kk, vt,
+    e_row, x_turned, n_turned, normed, stage, turned, active_t, ctx_sib,
+    send_sem, recv_sem, local_sem, hsend, hrecv, csend, crecv, tsend, trecv, wsem,
 ):
     f32, bf16 = jnp.float32, jnp.bfloat16
     core, chip = place()
@@ -454,13 +456,30 @@
     ]
     rest = [
         Gather(copies, 2, s_out, o_out, local_sem.at[2]),
-        Gather(copies, 3, s_vec, o_vec, local_sem.at[3]),
+        Gather(copies, 3, s_vec, w_vec, local_sem.at[3]),
         Gather(copies, 4, s_expand, o_expand, local_sem.at[4]),
         Gather(copies, 5, s_reduce, o_reduce, local_sem.at[5]),
     ]
     for g in first:
         g.start_z()
         g.start_plane()
+
+    def turn(slot, src, kept):
+        c = pltpu.make_async_remote_copy(
+            src_ref=src,
+            dst_ref=turned.at[slot, 1],
+            send_sem=tsend.at[slot],
+            recv_sem=trecv.at[slot],
+            device_id=sib,
+            device_id_type=MESH,
+        )
+        c.start()
+        turned[slot, 0] = kept[...]
+        return c
+
+    for i in range(4):
+        x_turned[i // 2, 256 * (i % 2) : 256 * (i % 2) + 256] = x_ref[:, 256 * i : 256 * i + 256].astype(f32).T.astype(bf16)
+    swaps = [turn(0, x_turned.at[1 - core], x_turned.at[core])]
     for z in (4, 8, 12):
         for g in first:
             g.on_z(z)
@@ -520,8 +539,7 @@
             ).wait_recv()
 
     rest[3].start_z()
-    events = []
-    events.append(lambda: [g.on_plane(0) for g in rest])
+    events = [lambda: [g.on_plane(0) for g in rest]]
     for z in (4, 8, 12):
         events.append(lambda z=z: [g.on_z(z) for g in rest[:3]])
     events.append(lambda: [g.on_diagonal(0) for g in rest])
@@ -531,11 +549,11 @@
         events.append(lambda z=z: [rest[3].on_z(z)])
     for z in (4, 8, 12):
         events.append(lambda z=z: [g.on_diagonal(z) for g in rest[:3]])
+    READY = len(events)
     for z in (4, 8, 12):
         events.append(lambda z=z: [rest[3].on_plane(z)])
     for z in (4, 8, 12):
         events.append(lambda z=z: [rest[3].on_diagonal(z)])
-    events.append(lambda: [g.on_sibling() for g in rest])
 
     def attend_sequence(s, during):
         load_sequence(recv_blk, s, kk, vt_ref=vt)
@@ -576,7 +594,7 @@
 
         ctx_recv[chip, :, pl.ds(128 * s, 128)] = ctx_blk[s, chip]
 
-    PRE, FIRST, SECOND = 5, 3, 6
+    PRE, FIRST, SECOND = 5, 3, 3
     for event in events[:PRE]:
         event()
     heads_here(0)
@@ -585,8 +603,34 @@
     pairs_out = pltpu.make_async_copy(recv_blk, o_pairs, local_sem.at[7])
     pairs_out.start()
     attend_sequence(1, events[PRE + FIRST : PRE + FIRST + SECOND])
-    for event in events[PRE + FIRST + SECOND :]:
+    for event in events[PRE + FIRST + SECOND : READY]:
         event()
+    for g in rest[:3]:
+        g.on_sibling()
+    out_weights = pltpu.make_async_copy(o_out, w_out, local_sem.at[6 + 2])
+    out_weights.start()
+
+    def fetch(c, slot):
+        cols = pl.ds(pl.multiple_of(c * 512, 512), 512)
+        return pltpu.make_async_copy(o_expand.at[:, :, cols], w_expand.at[slot], wsem.at[slot])
+
+    fetch(0, 0).start()
+
+    owner = lax.broadcasted_iota(jnp.int32, (32, 1024), 0)
+    column = lax.broadcasted_iota(jnp.int32, (32, 1024), 1)
+    lane = lax.broadcasted_iota(jnp.int32, (128, 1024), 0)
+    pick = jnp.where(lax.rem(lax.broadcasted_iota(jnp.int32, (128, 1024), 1), 32) == lane, 1.0, 0.0).astype(bf16)
+    o_rows[...] = jnp.zeros_like(o_rows)
+    for r in range(7):
+        choose = jnp.where(column == owner * 32 + r, 1.0, 0.0).astype(bf16)
+        piece = jnp.dot(choose, w_vec[...].reshape(1024, 128), preferred_element_type=f32)
+        if r == 3:
+            for o in range(32):
+                e_row[o // 4 : o // 4 + 1, 128 * (o % 4) : 128 * (o % 4) + 128] = piece[o : o + 1]
+        else:
+            spread_row = jnp.dot(piece.astype(bf16), pick, preferred_element_type=f32)
+            o_rows[r : r + 1] = jnp.sum(jnp.where(lax.div(column, 32) == owner, spread_row, 0.0), 0, keepdims=True)
+
     for s in range(2):
         for b in range(1, 16):
             other = flip(chip, b)
@@ -599,14 +643,103 @@
                 device_id=sib,
                 device_id_type=MESH,
             ).wait()
-    ctx_out = pltpu.make_async_copy(ctx_recv, o_ctx, local_sem.at[8])
-    ctx_out.start()
+    mine, others = pl.ds(core * 8, 8), pl.ds((1 - core) * 8, 8)
+    swaps.append(
+        pltpu.make_async_remote_copy(
+            src_ref=ctx_recv.at[others],
+            dst_ref=ctx_sib,
+            send_sem=tsend.at[2],
+            recv_sem=trecv.at[2],
+            device_id=sib,
+            device_id_type=MESH,
+        )
+    )
+    swaps[-1].start()
+    turned[2, 0] = ctx_recv[mine].reshape(512, 256)
+    out_weights.wait()
+    for i in range(4):
+        rows = ctx_recv[4 * i : 4 * i + 4].reshape(256, 256).astype(f32).T.astype(bf16)
+        term = jnp.dot(rows, w_out[8 * i : 8 * i + 8].reshape(256, 1024), preferred_element_type=f32)
+        if i == 0:
+            o_scaled[...] = term + (x_ref[...].astype(f32) + o_rows[0:1])
+        else:
+            o_scaled[...] += term
+
+    @pl.loop(0, 4)
+    def _(i):
+        span = pl.ds(pl.multiple_of(i * 64, 64), 64)
+        residual = o_scaled[span]
+        center = residual - jnp.mean(residual, -1, keepdims=True)
+        spread = lax.rsqrt(jnp.mean(center * center, -1, keepdims=True) + epsilon)
+        x_hat = center * spread
+        o_scaled[span] = x_hat
+        o_spread[span] = jnp.broadcast_to(spread, (64, 128))
+        normed[span] = (x_hat * o_rows[1:2] + o_rows[2:3]).astype(bf16)
+
+    for i in range(4):
+        n_turned[i // 2, 256 * (i % 2) : 256 * (i % 2) + 256] = normed[:, 256 * i : 256 * i + 256].astype(f32).T.astype(bf16)
+    swaps.append(turn(1, n_turned.at[1 - core], n_turned.at[core]))
+
+    def active_copy(j):
+        return pltpu.make_async_remote_copy(
+            src_ref=stage.at[j],
+            dst_ref=active_t.at[1, j],
+            send_sem=tsend.at[3 + j],
+            recv_sem=trecv.at[3 + j],
+            device_id=sib,
+            device_id_type=MESH,
+        )
+
+    last_events = events[READY:]
+
+    @pl.loop(0, 8)
+    def _(c):
+        for k, event in enumerate(last_events[:8]):
+
+            @pl.when(c == k)
+            def _():
+                event()
+
+        slot = lax.rem(c, 2)
+
+        @pl.when(c < 7)
+        def _():
+            fetch(c + 1, 1 - slot).start()
+
+        fetch(c, slot).wait()
+        expanded = jnp.dot(normed[...], w_expand[slot].reshape(1024, 512), preferred_element_type=f32) + e_row[pl.ds(c, 1)]
+        share = 0.5 * (1.0 + lax.erf(expanded * math.sqrt(0.5)))
+        bell = jnp.exp(-0.5 * expanded * expanded) * (1.0 / math.sqrt(2.0 * math.pi))
+        o_slope[c] = (share + expanded * bell).astype(bf16)
+        active = (expanded * share).astype(bf16)
+        o_active[c] = active
+        across = active.astype(f32).T.astype(bf16)
+        j = lax.rem(c, 4)
+
+        @pl.when(lax.div(c, 4) == core)
+        def _():
+            active_t[0, j] = across
+
+        @pl.when(lax.div(c, 4) != core)
+        def _():
+            stage[j] = across
+            active_copy(j).start()
+
+    for event in last_events[8:]:
+        event()
+    rest[3].on_sibling()
+    for c in swaps:
+        c.wait()
+    turned[2, 1] = ctx_sib[...].reshape(512, 256)
+    for j in range(4):
+        active_copy(j).wait()
+    o_turned[...] = turned[...]
+    o_active_t[...] = active_t[...]
     for c in heads:
         c.wait_send()
     copies.drain(sib)
     keep.wait()
     pairs_out.wait()
-    ctx_out.wait()
 
 
 def flip_by(v, w):
@@ -622,30 +755,48 @@
     f32, bf16 = jnp.float32, jnp.bfloat16
     gathered = lambda x: jax.ShapeDtypeStruct((32,) + x.shape, x.dtype)
     dma = pltpu.SemaphoreType.DMA
+    array = jax.ShapeDtypeStruct
+    vmem = lambda shape, dtype=bf16: pltpu.VMEM(shape, dtype)
     return pl.pallas_call(
         fwd_kernel,
         out_shape=[
-            gathered(vec),
             gathered(w_out),
             gathered(w_expand),
             gathered(w_reduce),
             gathered(qkv),
-            jax.ShapeDtypeStruct((2, 16, 192, 128), bf16),
-            jax.ShapeDtypeStruct((16, 64, 256), bf16),
-            jax.ShapeDtypeStruct((2, 64, 2048), f32),
-            jax.ShapeDtypeStruct((2, 8, 256), f32),
+            array((2, 16, 192, 128), bf16),
+            array((2, 64, 2048), f32),
+            array((2, 8, 256), f32),
+            array((8, 1024), f32),
+            array((256, 1024), f32),
+            array((256, 128), f32),
+            array((8, 256, 512), bf16),
+            array((8, 256, 512), bf16),
+            array((3, 2, 512, 256), bf16),
+            array((2, 4, 512, 256), bf16),
         ],
         in_specs=[v, pl.BlockSpec(memory_space=pltpu.SMEM)] + [hbm] * 6,
-        out_specs=[hbm] * 7 + [v, v],
+        out_specs=[hbm] * 5 + [v] * 9,
         scratch_shapes=[
-            pltpu.VMEM((32,) + qkv.shape, bf16),
-            pltpu.VMEM((32,) + bias.shape, bf16),
-            pltpu.VMEM((16, 192, 256), bf16),
-            pltpu.VMEM((2, 16, 192, 128), bf16),
-            pltpu.VMEM((2, 16, 64, 128), bf16),
-            pltpu.VMEM((16, 64, 256), bf16),
-            pltpu.VMEM((2048, 64), bf16),
-            pltpu.VMEM((64, 2048), bf16),
+            vmem((32,) + qkv.shape),
+            vmem((32,) + bias.shape),
+            vmem((32,) + vec.shape),
+            vmem((32,) + w_out.shape),
+            vmem((2, 32, 32, 512)),
+            vmem((16, 192, 256)),
+            vmem((2, 16, 192, 128)),
+            vmem((2, 16, 64, 128)),
+            vmem((16, 64, 256)),
+            vmem((2048, 64)),
+            vmem((64, 2048)),
+            vmem((8, 512), f32),
+            vmem((2, 512, 256)),
+            vmem((2, 512, 256)),
+            vmem((256, 1024)),
+            vmem((4, 512, 256)),
+            vmem((3, 2, 512, 256)),
+            vmem((2, 4, 512, 256)),
+            vmem((8, 64, 256)),
             dma((210,)),
             dma((210,)),
             dma((9,)),
@@ -653,9 +804,12 @@
             dma((32,)),
             dma((32,)),
             dma((32,)),
+            dma((7,)),
+            dma((7,)),
+            dma((2,)),
         ],
         compiler_params=pltpu.CompilerParams(
-            collective_id=collective_id, has_side_effects=True, vmem_limit_bytes=56 * MIB
+            collective_id=collective_id, has_side_effects=True, vmem_limit_bytes=60 * MIB
         ),
         name="forward_attention",
     )(rows, lengths, qkv, bias, vec, w_out, w_expand, w_reduce)
@@ -772,16 +926,16 @@
 def bwd_kernel(*refs):
     f32, bf16 = jnp.float32, jnp.bfloat16
     (
-        lengths_ref, pairs, o_full, lse_ref, x_t, normed_t, context_t, d_second, scaled, spread, gain, g_reduce, vec_in,
-        h_slope, h_reduce, h_expand, h_out, h_qkv,
-    ) = refs[:18]
-    (o_reduce, o_expand, o_out, o_vec, o_qkv, o_input, o_bias) = refs[18:25]
-    bufs = [refs[25 + 3 * i : 28 + 3 * i] for i in range(5)]
+        lengths_ref, pairs, o_full, lse_ref, rows_t, active_t, cotangent, scaled, spread, vectors,
+        h_active, h_slope, h_reduce, h_expand, h_out, h_qkv,
+    ) = refs[:16]
+    (o_layer, o_reduce, o_expand, o_out, o_vec, o_qkv, o_input, o_bias) = refs[16:24]
+    bufs = [refs[24 + 3 * i : 27 + 3 * i] for i in range(5)]
     (
-        g_expand, g_out, g_vec, g_qkv, w_qkv, d_recv, kk, vv, kt, acc, d_send, d_own, d_sib, b_own, b_sib, b_in,
-        slopes, w_reduce, w_expand, w_out, e_own, e_sib, d_first, a_own, a_sib, d_ctx, rows_sum, e_sum, vec_own, vec_sib,
+        g_reduce, g_expand, g_out, g_vec, g_qkv, w_qkv, d_recv, kk, vv, kt, acc, d_send, d_own, d_sib, b_own, b_sib, b_in,
+        slopes, w_reduce, w_expand, w_out, e_own, e_sib, d_first, a_own, a_sib, d_ctx, rows_sum, e_sum, vec_own, vec_sib, r_own, r_sib,
         send_sem, recv_sem, local_sem, dsend, drecv, qsend, qrecv, esend, erecv, wsem,
-    ) = refs[40:]
+    ) = refs[39:]
     core, chip = place()
     sib = (1 - core, chip)
     greet([sib] + [(core, flip(chip, b)) for b in range(1, 16)])
@@ -791,24 +945,76 @@
         for i, (g, o) in enumerate(((g_reduce, o_reduce), (g_expand, o_expand), (g_out, o_out), (g_vec, o_vec)))
     ]
     last = Scatter(copies, 4, g_qkv, o_qkv, bufs[4])
+    out_weights = pltpu.make_async_copy(h_out, w_out, local_sem.at[4])
+    out_weights.start()
+
+    def fetch(c, slot, back):
+        cols = pl.ds(pl.multiple_of(c * 512, 512), 512)
+        copies_in = [
+            pltpu.make_async_copy(h_reduce.at[pl.ds(c * 4, 4)], w_reduce.at[slot], wsem.at[slot, 0]),
+            pltpu.make_async_copy((h_slope if back else h_active).at[c], slopes.at[slot], wsem.at[slot, 2]),
+        ]
+        if back:
+            copies_in.append(pltpu.make_async_copy(h_expand.at[:, :, cols], w_expand.at[slot], wsem.at[slot, 1]))
+        return copies_in
+
+    for c in fetch(0, 0, False):
+        c.start()
+    d_first[...] = scaled[...] * vectors[1:2] + (vectors[2:3] + vectors[4:5])
+
+    @pl.loop(0, 8)
+    def _(c):
+        slot = lax.rem(c, 2)
+
+        @pl.when(c < 7)
+        def _():
+            for copy in fetch(c + 1, 1 - slot, False):
+                copy.start()
+
+        @pl.when(c == 7)
+        def _():
+            for copy in fetch(0, 0, True):
+                copy.start()
+
+        for copy in fetch(c, slot, False):
+            copy.wait()
+        d_first[...] += jnp.dot(slopes[slot], w_reduce[slot].reshape(512, 1024), preferred_element_type=f32)
+
+    rows_sum[...] = jnp.zeros_like(rows_sum)
+
+    @pl.loop(0, 4)
+    def _(i):
+        span = pl.ds(pl.multiple_of(i * 64, 64), 64)
+        total = d_first[span]
+        center = total - jnp.mean(total, -1, keepdims=True)
+        width = lax.rsqrt(jnp.mean(center * center, -1, keepdims=True) + epsilon)
+        x_hat = center * width
+        row = chip * 128 + lax.rem(i, 2) * 64 + lax.broadcasted_iota(jnp.int32, (64, 1024), 0)
+        valid = row < lengths_ref[lax.div(i, 2)]
+        o_layer[span] = jnp.where(valid, x_hat * vectors[5:6] + vectors[6:7], 0.0).astype(bf16)
+        d_output = jnp.where(valid, cotangent[span].astype(f32), 0.0)
+        pulled = d_output * vectors[5:6]
+        level = jnp.mean(pulled, -1, keepdims=True)
+        slope = jnp.mean(pulled * x_hat, -1, keepdims=True)
+        d_rows = width * (pulled - level - x_hat * slope)
+        d_low = d_rows.astype(bf16)
+        d_first[span] = d_rows
+        r_own[span] = d_low
+        rows_sum[4:5] += jnp.sum(d_low.astype(f32), 0, keepdims=True)
+        rows_sum[5:6] += jnp.sum(d_output * x_hat, 0, keepdims=True)
+        rows_sum[6:7] += jnp.sum(d_output, 0, keepdims=True)
+
+    copies.send("r", r_own, r_sib, sib, r_own)
+    copies.arrived("r", r_sib, sib)
+
+    @pl.loop(0, 4)
+    def _(j):
+        g = jnp.dot(active_t[0, j], r_own[...], preferred_element_type=f32)
+        g = g + jnp.dot(active_t[1, j], r_sib[...], preferred_element_type=f32)
+        g_reduce[pl.ds(j * 4, 4)] = g.astype(bf16).reshape(4, 128, 1024)
+
     rest[0].start()
     rest[0].start_direct()
-    out_weights = pltpu.make_async_copy(h_out, w_out, local_sem.at[4])
-    out_weights.start()
-
-    def fetch(c, slot):
-        return (
-            pltpu.make_async_copy(h_reduce.at[pl.ds(c * 4, 4)], w_reduce.at[slot], wsem.at[slot, 0]),
-            pltpu.make_async_copy(
-                h_expand.at[:, :, pl.ds(pl.multiple_of(c * 512, 512), 512)], w_expand.at[slot], wsem.at[slot, 1]
-            ),
-            pltpu.make_async_copy(h_slope.at[:, pl.ds(pl.multiple_of(c * 512, 512), 512)], slopes.at[slot], wsem.at[slot, 2]),
-        )
-
-    for c in fetch(0, 0):
-        c.start()
-    a_own[...] = d_second[...].astype(bf16)
-    d_first[...] = d_second[...]
 
     def e_copy(c):
         return pltpu.make_async_remote_copy(
@@ -826,28 +1032,26 @@
 
         @pl.when(c < 7)
         def _():
-            for copy in fetch(c + 1, 1 - slot):
+            for copy in fetch(c + 1, 1 - slot, True):
                 copy.start()
 
-        for copy in fetch(c, slot):
+        for copy in fetch(c, slot, True):
             copy.wait()
-        d_active = nt(a_own[...], w_reduce[slot].reshape(512, 1024))
+        d_active = nt(r_own[...], w_reduce[slot].reshape(512, 1024))
         d_expanded = (d_active * slopes[slot].astype(f32)).astype(bf16)
         e_own[c] = d_expanded
         e_copy(c).start()
         e_sum[pl.ds(c, 1)] = jnp.sum(d_expanded.astype(f32), 0, keepdims=True)
         d_first[...] += nt(d_expanded, w_expand[slot].reshape(1024, 512))
 
-    rows_sum[...] = jnp.zeros_like(rows_sum)
-
     @pl.loop(0, 4)
     def _(i):
         span = pl.ds(pl.multiple_of(i * 64, 64), 64)
         d_normed, x_hat = d_first[span], scaled[span]
-        pulled = d_normed * gain[...]
+        pulled = d_normed * vectors[1:2]
         level = jnp.mean(pulled, -1, keepdims=True)
         slope = jnp.mean(pulled * x_hat, -1, keepdims=True)
-        d_rows = spread[span] * (pulled - level - x_hat * slope)
+        d_rows = spread[span, 0:1] * (pulled - level - x_hat * slope)
         d_low = d_rows.astype(bf16)
         d_first[span] = d_rows
         a_own[span] = d_low
@@ -893,12 +1097,12 @@
         d_recv[s, chip] = d_ctx[chip, :, lane]
     copies.send("a", a_own, a_sib, sib, a_own)
 
-    vec_own[...] = vec_in[...]
+    vec_own[...] = jnp.zeros_like(vec_own)
     owner = lax.broadcasted_iota(jnp.int32, (32, 1024), 0)
     column = lax.broadcasted_iota(jnp.int32, (32, 1024), 1)
     place_in = lax.rem(lax.broadcasted_iota(jnp.int32, (1024, 128), 0), 32)
     pick = jnp.where(place_in == lax.broadcasted_iota(jnp.int32, (1024, 128), 1), 1.0, 0.0).astype(bf16)
-    for r in range(3):
+    for r in (0, 1, 2, 4, 5, 6):
         spread_row = jnp.where(lax.div(column, 32) == owner, rows_sum[r : r + 1], 0.0)
         top = spread_row.astype(bf16)
         low = (spread_row - top.astype(f32)).astype(bf16)
@@ -914,8 +1118,8 @@
     @pl.loop(0, 8)
     def _(c):
         e_copy(c).wait()
-        g = jnp.dot(normed_t[:, :256], e_own[c], preferred_element_type=f32)
-        g = g + jnp.dot(normed_t[:, 256:], e_sib[c], preferred_element_type=f32)
+        g = jnp.dot(rows_t[1, 0], e_own[c], preferred_element_type=f32)
+        g = g + jnp.dot(rows_t[1, 1], e_sib[c], preferred_element_type=f32)
         g_expand[:, :, pl.ds(pl.multiple_of(c * 512, 512), 512)] = g.astype(bf16).reshape(16, 32, 512)
 
     rest[1].start()
@@ -923,8 +1127,8 @@
     copies.arrived("a", a_sib, sib)
     for i in range(4):
         cols = slice(256 * i, 256 * i + 256)
-        g = jnp.dot(context_t[:, :256], a_own[:, cols], preferred_element_type=f32)
-        g = g + jnp.dot(context_t[:, 256:], a_sib[:, cols], preferred_element_type=f32)
+        g = jnp.dot(rows_t[2, 0], a_own[:, cols], preferred_element_type=f32)
+        g = g + jnp.dot(rows_t[2, 1], a_sib[:, cols], preferred_element_type=f32)
         g_out[:, :, cols] = g.astype(bf16).reshape(16, 32, 256)
     copies.arrived("v", vec_sib, sib)
     g_vec[...] = vec_own[own_half] + vec_sib[...]
@@ -989,7 +1193,7 @@
         rest[0].on_second(k)
     events = [lambda k=k: [r.on_first(k) for r in rest[1:]] for k in range(4)]
     events += [lambda k=k: [r.on_second(k) for r in rest[1:]] for k in range(4)]
-    FIRST, SECOND, WAIT = 0, 4, 2
+    FIRST, SECOND, WAIT = 0, 0, 4
     for b in FULL_ORDER:
         exchange_in(0, b, d_recv.at[0, flip(chip, b)], dsend, drecv)
     back_sequence(0, events[:FIRST])
@@ -1017,7 +1221,7 @@
             total = None
             for i, rows in enumerate((d_own, d_sib)):
                 right = rows[pl.ds(4 * p, 4), pl.ds(64 * part, 64)].reshape(256, 256)
-                term = nt(x_t[:, 256 * i : 256 * i + 256], right)
+                term = nt(rows_t[0, i], right)
                 total = term if total is None else total + term
             cols = pl.ds(pl.multiple_of(part * 1024 + p * 256, 256), 256)
             g_qkv[:, :, cols] = total.astype(bf16).reshape(16, 32, 256)
@@ -1095,8 +1299,8 @@
 
 
 def backward_attention(
-    lengths, pairs, o_full, lse, x_t, normed_t, context_t, d_second, scaled, spread, gain, g_reduce, vec_in,
-    slope, w_reduce, w_expand, w_out, w_qkv, collective_id,
+    lengths, pairs, o_full, lse, rows_t, active_t, cotangent, scaled, spread, vectors,
+    active, slope, w_reduce, w_expand, w_out, w_qkv, collective_id,
 ):
     v, hbm = pl.BlockSpec(memory_space=pltpu.VMEM), pl.BlockSpec(memory_space=pl.ANY)
     f32, bf16 = jnp.float32, jnp.bfloat16
@@ -1108,12 +1312,14 @@
     vmem = lambda shape, dtype=bf16: pltpu.VMEM(shape, dtype)
     return pl.pallas_call(
         bwd_kernel,
-        out_shape=[jax.ShapeDtypeStruct(block, f32) for block, _ in blocks]
+        out_shape=[jax.ShapeDtypeStruct((256, 1024), bf16)]
+        + [jax.ShapeDtypeStruct(block, f32) for block, _ in blocks]
         + [jax.ShapeDtypeStruct((256, 1024), f32), jax.ShapeDtypeStruct((2, 32, 128), f32)],
-        in_specs=[pl.BlockSpec(memory_space=pltpu.SMEM)] + [v] * 12 + [hbm] * 5,
-        out_specs=[v] * 7,
+        in_specs=[pl.BlockSpec(memory_space=pltpu.SMEM)] + [v] * 9 + [hbm] * 6,
+        out_specs=[v] * 8,
         scratch_shapes=bufs
         + [
+            vmem((16, 128, 1024)),
             vmem((16, 32, 4096)),
             vmem((16, 32, 1024)),
             vmem((16, 16, 128), f32),
@@ -1144,6 +1350,8 @@
             vmem((8, 512), f32),
             vmem((32, 16, 128), f32),
             vmem((16, 16, 128), f32),
+            vmem((256, 1024)),
+            vmem((256, 1024)),
             dma((144,)),
             dma((144,)),
             dma((7,)),
@@ -1160,29 +1368,9 @@
         ),
         name="backward_attention",
     )(
-        lengths, pairs, o_full, lse, x_t, normed_t, context_t, d_second, scaled, spread, gain, g_reduce, vec_in,
-        slope, w_reduce, w_expand, w_out, w_qkv,
-    )
-
-
-def swap(x):
-    return lax.ppermute(x, "fsdp", [(0, 1), (1, 0)])
-
-
-def halves(left_t):
-    core = lax.axis_index("fsdp")
-    h = left_t.shape[0] // 2
-    own = lax.dynamic_slice_in_dim(left_t, core * h, h, 0)
-    return own, swap(lax.dynamic_slice_in_dim(left_t, (1 - core) * h, h, 0))
-
-
-def chip_sum(left, right):
-    core = lax.axis_index("fsdp")
-    h = left.shape[1] // 2
-    own = lax.dynamic_slice_in_dim(left, core * h, h, 1)
-    other = swap(lax.dynamic_slice_in_dim(left, (1 - core) * h, h, 1))
-    grad = outer_sum(own, right) + outer_sum(other, swap(right))
-    return grad.astype(jnp.bfloat16).reshape(16, h // 16, right.shape[1])
+        lengths, pairs, o_full, lse, rows_t, active_t, cotangent, scaled, spread, vectors,
+        active, slope, w_reduce, w_expand, w_out, w_qkv,
+    )
 
 
 def fast_shards(
@@ -1215,51 +1403,18 @@
     small = [b_out, first_gain, first_shift, b_expand, b_reduce, second_gain, second_shift]
     vec = sum(jnp.pad(b[None, :], ((r, part - 1 - r), (0, 128 - b.shape[0]))) for r, b in enumerate(small))
     flat_rows = inputs.reshape(total, width)
-    g_vec, g_out, g_expand, g_reduce, g_qkv, pairs, context_t, o_full, lse = forward_attention(
-        flat_rows, lengths, qkv, bias, vec, w_out, w_expand, w_reduce, 1
-    )
-    full_out = g_out.reshape(width, width)
-    full_expand = g_expand.reshape(width, ff)
-    full_reduce = g_reduce.reshape(ff, width)
-    bias_out, gain_first, shift_first, bias_expand, bias_reduce, gain_second, shift_second = (
-        g_vec[:, r, : b.shape[0]].reshape(1, -1).astype(f32) for r, b in enumerate(small)
-    )
-    own_first = lax.axis_index("ctx") * count
-    positions = own_first + jnp.arange(count, dtype=jnp.int32)
-    valid_rows = (positions[None, :] < lengths[:, None]).astype(f32).reshape(total, 1)
-    context_t = context_t.reshape(width, total)
-    residual = flat_rows.astype(f32) + outer_sum(context_t, full_out) + bias_out
-    center = residual - jnp.mean(residual, -1, keepdims=True)
-    spread = lax.rsqrt(jnp.mean(center * center, -1, keepdims=True) + epsilon)
-    scaled = center * spread
-    normed = scaled * gain_first + shift_first
-    normed_low = normed.astype(bf16)
-    expanded = product(normed_low, full_expand) + bias_expand
-    share = 0.5 * (1.0 + lax.erf(expanded * math.sqrt(0.5)))
-    slope = (share + expanded * jnp.exp(-0.5 * expanded * expanded) * (1.0 / math.sqrt(2.0 * math.pi))).astype(bf16)
-    activated_low = (expanded * share).astype(bf16)
-    reduced = product(activated_low, full_reduce) + bias_reduce
-    final_rows, second_pull = jax.vjp(layer_norm, normed + reduced, gain_second, shift_second)
-    layer_out = (final_rows * valid_rows).astype(bf16).reshape(inputs.shape)
-    d_output = cotangent.reshape(total, width).astype(f32) * valid_rows
-    d_second, second_gain_grad, second_shift_grad = second_pull(d_output)
-    d_reduced = d_second.astype(bf16)
-    reduce_grad = chip_sum(activated_low, d_reduced)
-    reduce_bias_grad = jnp.sum(d_reduced.astype(f32), 0)
-    vec_in = sum(
-        jnp.pad(g.reshape(32, 1, part), ((0, 0), (r, 15 - r), (0, 128 - part)))
-        for r, g in ((4, reduce_bias_grad), (5, second_gain_grad), (6, second_shift_grad))
-    )
-    both = lambda rows_t: jnp.concatenate(halves(rows_t), 1)
-    s_reduce, s_expand, s_out, s_vec, s_qkv, input_grad, s_bias = backward_attention(
-        lengths, pairs, o_full, lse, both(flat_rows.T), both(normed_low.T), both(context_t), d_second, scaled, spread,
-        gain_first, reduce_grad, vec_in, slope, g_reduce, g_expand, g_out, g_qkv, 2,
+    (
+        g_out, g_expand, g_reduce, g_qkv, pairs, o_full, lse, vectors, scaled, spread, active, slope, rows_t, active_t,
+    ) = forward_attention(flat_rows, lengths, qkv, bias, vec, w_out, w_expand, w_reduce, 1)
+    layer_out, s_reduce, s_expand, s_out, s_vec, s_qkv, input_grad, s_bias = backward_attention(
+        lengths, pairs, o_full, lse, rows_t, active_t, cotangent.reshape(total, width), scaled, spread, vectors,
+        active, slope, g_reduce, g_expand, g_out, g_qkv, 2,
     )
     s_query, s_key, s_value = (s_qkv[:, width * i : width * (i + 1)] for i in range(3))
     s_bias = jnp.sum(s_bias, -1)
     v = [s_vec[r, : b.shape[0]] for r, b in enumerate(small)]
     return (
-        layer_out,
+        layer_out.reshape(inputs.shape),
         input_grad.reshape(inputs.shape),
         s_query,
         s_bias[0],

time: 399 us -> 349 us (0.87)
  matrix products: 26 us -> 0 us
  local copies, waits for them, and re-layouts: 22.7 us -> 10.4 us
  other arithmetic: 16.8 us -> 4.55 us
  Pallas kernels: 328 us -> 332 us
    dot_general x5 -> x0, matrix products: 26 us -> none  [the longest x3 15.5 us: outer_sum(): jnp.einsum('rd,re->de', left, right, preferred_element_type=jnp.float32)]
    dynamic_slice x4 -> x0, local copies, waits for them, and re-layouts: 6.76 us -> none  [the longest x3 4.44 us: halves(): own = lax.dynamic_slice_in_dim(left_t, core * h, h, 0)]
  transfers between devices with their start and end apart: 5 -> 0, of which waited for: 0 -> 0; matrix products, arithmetic and copies ran while one was open for 5% -> 0% of each run, Pallas kernels for 0% -> 0%
where the time goes in v4:
time: 349 us; the launch traced here: 347 us
  Pallas kernels  332 us (95%)
  local copies, waits for them, and re-layouts  10.4 us (3%)
  other arithmetic  4.55 us (1%)
    pallas_call x1, Pallas kernels, backward_attention(): pl.pallas_call(bwd_kernel, out_shape=[jax.ShapeDtypeStruct((256, 1024), b...  172 us
    pallas_call x1, Pallas kernels, forward_attention(): pl.pallas_call(fwd_kernel, out_shape=[gathered(w_out), gathered(w_expand)...  160 us

profile of v4, /device:TPU:0, one launch (start us, length us, event | category | flops | bytes accessed | tf_op | source)
XLA Modules:
  0.0 347.4 jit_solution(8693586342055753644)
XLA Ops:
  0.7 0.7 pad_maximum_fusion.1
  1.4 1.4 pad_add_fusion.s_vec
  2.8 0.7 add.37.s_bias
  3.5 1.6 pad_maximum_fusion.s_qkv
  5.0 159.6 %forward_attention.1 = (bf16[32,32,1024]{2,1,0:T(8,128)(2,1)}, bf16[32,32,4096]{2,1,0:T(8,128)(2,1)}, bf16[32,128,1024]{2,1,0:T(8,128)(2,1)}, bf16[32,32,3072]{2...) custom-call(bf16[256,1024]{1,0:T(8,128)(2,1)} %bitcast.31, ...), custom_call_target="tpu_custom_call" | custom-call | tf_op jit(solution)/shard_map/forward_attention/pallas_call | solution.py:760
  164.7 172.1 %backward_attention.1 = (bf16[256,1024]{1,0:T(8,128)(2,1)}, f32[128,1024]{1,0:T(8,128)}, f32[32,4096]{1,0:T(8,128)}, f32[32,1024]{1,0:T(8,128)}, f32[16,128]{1,0...) custom-call(s32[2]{0:T(128)} %refs_0_.1, ...), custom_call_target="tpu_custom_call" | custom-call | tf_op jit(solution)/shard_map/backward_attention/pallas_call | solution.py:1313
  336.8 0.0 copy-start
  336.8 0.0 copy-start.3
  336.8 1.3 slice_bitcast_fusion.3
  338.1 0.8 reduce_sum.9
  338.9 1.4 slice_bitcast_fusion
  340.4 0.0 copy-start.2
  340.4 1.8 fusion
  342.2 0.0 copy-start.1
  342.2 1.9 copy.40
  344.2 0.0 copy-done
  344.2 1.0 copy.41
  345.1 0.0 copy-done.3
  345.1 0.7 copy.42
  345.8 0.0 copy-done.2
  345.8 0.8 copy.43
  346.6 0.0 copy-done.1
  346.6 0.8 copy.44
Async XLA Ops:
  336.8 7.4 %copy-start = (f32[256,1024]{1,0:T(8,128)S(1)}, f32[256,1024]{1,0:T(8,128)}, u32[]{:S(2)}) copy-start(f32[256,1024]{1,0:T(8,128)} %get-tuple-element.54) | copy-start | bytes 3145732
  336.8 8.3 %copy-start.3 = (f32[32,1024]{1,0:T(8,128)S(1)}, f32[32,1024]{1,0:T(8,128)}, u32[]{:S(2)}) copy-start(f32[32,1024]{1,0:T(8,128)} %get-tuple-element.98) | copy-start | bytes 393220
  340.4 5.4 %copy-start.2 = (f32[32,4096]{1,0:T(8,128)S(1)}, f32[32,4096]{1,0:T(8,128)}, u32[]{:S(2)}) copy-start(f32[32,4096]{1,0:T(8,128)} %get-tuple-element.102) | copy-start | bytes 1572868
  342.2 4.4 %copy-start.1 = (f32[128,1024]{1,0:T(8,128)S(1)}, f32[128,1024]{1,0:T(8,128)}, u32[]{:S(2)}) copy-start(f32[128,1024]{1,0:T(8,128)} %get-tuple-element.104) | copy-start | bytes 1572868

commit v5 on v4

--- a/solution.py
+++ b/solution.py
@@ -366,9 +366,32 @@
             self.pair(name, like, like, peer).wait_send()
 
 
+class Line:
+    def __init__(self, chip):
+        self.z = lax.div(chip, 4)
+        self.rest = chip - 4 * self.z
+        even = lax.rem(self.z, 2) == 0
+        low = self.z < 2
+        one, two, three = jnp.int32(1), jnp.int32(2), jnp.int32(3)
+        near = jnp.where(even, one, -one)
+        mid = jnp.where(low, jnp.where(even, two, one), jnp.where(even, -one, -two))
+        far = jnp.where(low, jnp.where(even, three, two), jnp.where(even, -two, -three))
+        self.offsets = [jnp.int32(0), near, mid, far]
+
+    def source(self, k):
+        return self.z + self.offsets[k]
+
+    def onward_up(self, k):
+        return (self.offsets[k] < 0) & (self.z < 3)
+
+    def onward_down(self, k):
+        return (self.offsets[k] > 0) & (self.z > 0)
+
+
 class Gather:
-    def __init__(self, copies, name, src, out, local_sem):
-        self.copies, self.name, self.src, self.out, self.local_sem = copies, name, src, out, local_sem
+    def __init__(self, copies, line, name, src, out, local_sem, zsend, zrecv):
+        self.copies, self.line, self.name, self.src, self.out, self.local_sem = copies, line, name, src, out, local_sem
+        self.zsend, self.zrecv = zsend, zrecv
         self.core, self.chip = place()
         self.sib = (1 - self.core, self.chip)
         self.half = src.shape[0] // 2
@@ -376,11 +399,15 @@
     def at(self, bits):
         return (self.core, flip(self.chip, bits))
 
-    def block(self, bits, core=None):
-        return self.out.at[(self.core if core is None else core) * 16 + flip(self.chip, bits)]
-
-    def part(self, bits, upper):
-        return self.out.at[self.core * 16 + flip(self.chip, bits), pl.ds(self.half if upper else 0, self.half)]
+    def index(self, k, bits, core=None):
+        core = self.core if core is None else core
+        return core * 16 + self.line.source(k) * 4 + flip(self.line.rest, bits)
+
+    def block(self, k, bits, core=None):
+        return self.out.at[self.index(k, bits, core)]
+
+    def part(self, k, bits, upper):
+        return self.out.at[self.index(k, bits), pl.ds(self.half if upper else 0, self.half)]
 
     def send(self, tag, src, dst, peer, half=False):
         like = self.src.at[pl.ds(0, self.half)] if half else self.src
@@ -389,42 +416,88 @@
     def arrived(self, tag, dst):
         self.copies.arrived((self.name, tag), dst, self.sib)
 
+    def along(self, slot, source, src, dst, up):
+        return pltpu.make_async_remote_copy(
+            src_ref=src,
+            dst_ref=dst,
+            send_sem=self.zsend.at[self.name * 6 + slot],
+            recv_sem=self.zrecv.at[self.name * 4 + source],
+            device_id=(self.core, self.chip + 4 if up else self.chip - 4),
+            device_id_type=MESH,
+        )
+
     def start_z(self):
-        for z in (12, 8, 4):
-            self.send(("z", z), self.src, self.block(0), self.at(z))
+        z = self.line.z
+
+        @pl.when(z < 3)
+        def _():
+            self.along(4, z, self.src, self.block(0, 0), True).start()
+
+        @pl.when(z > 0)
+        def _():
+            self.along(5, z, self.src, self.block(0, 0), False).start()
 
     def start_plane(self):
-        self.send(("x", 0), self.src, self.block(0), self.at(1))
-        self.send(("y", 0), self.src, self.block(0), self.at(2))
-        self.send(("s", 0), self.src, self.block(0), self.sib)
-        self.local = pltpu.make_async_copy(self.src, self.block(0), self.local_sem)
+        self.send(("x", 0), self.src, self.block(0, 0), self.at(1))
+        self.send(("y", 0), self.src, self.block(0, 0), self.at(2))
+        self.send(("s", 0, 0), self.src, self.block(0, 0), self.sib)
+        self.local = pltpu.make_async_copy(self.src, self.block(0, 0), self.local_sem)
         self.local.start()
 
-    def on_z(self, z):
-        b = self.block(z)
-        self.arrived(("z", z), b)
-        self.send(("x", z), b, b, self.at(1))
-        self.send(("y", z), b, b, self.at(2))
-        self.send(("s", z), b, b, self.sib)
-
-    def on_plane(self, z):
+    def on_z(self, k):
+        b = self.block(k, 0)
+        source = self.line.source(k)
+        self.along(source, source, b, b, True).wait_recv()
+
+        @pl.when(self.line.onward_up(k))
+        def _():
+            self.along(source, source, b, b, True).start()
+
+        @pl.when(self.line.onward_down(k))
+        def _():
+            self.along(source, source, b, b, False).start()
+
+        self.send(("x", k), b, b, self.at(1))
+        self.send(("y", k), b, b, self.at(2))
+        self.send(("s", k, 0), b, b, self.sib)
+
+    def on_plane(self, k):
         for bit, tag, further, upper in ((1, "x", 2, False), (2, "y", 1, True)):
-            b = self.block(z + bit)
-            self.arrived((tag, z), b)
-            h = self.part(z + bit, upper)
-            self.send(("d" + tag, z), h, h, self.at(further), True)
-            self.send(("s", z + bit), b, b, self.sib)
-
-    def on_diagonal(self, z):
-        self.arrived(("dx", z), self.part(z + 3, False))
-        self.arrived(("dy", z), self.part(z + 3, True))
-        b = self.block(z + 3)
-        self.send(("s", z + 3), b, b, self.sib)
+            b = self.block(k, bit)
+            self.arrived((tag, k), b)
+            h = self.part(k, bit, upper)
+            self.send(("d" + tag, k), h, h, self.at(further), True)
+            self.send(("s", k, bit), b, b, self.sib)
+
+    def on_diagonal(self, k):
+        self.arrived(("dx", k), self.part(k, 3, False))
+        self.arrived(("dy", k), self.part(k, 3, True))
+        b = self.block(k, 3)
+        self.send(("s", k, 3), b, b, self.sib)
 
     def on_sibling(self):
-        for bits in range(16):
-            self.arrived(("s", bits), self.block(bits, 1 - self.core))
+        for k in range(4):
+            for bits in range(4):
+                self.arrived(("s", k, bits), self.block(k, bits, 1 - self.core))
         self.local.wait()
+
+    def drain(self):
+        z = self.line.z
+
+        @pl.when(z < 3)
+        def _():
+            self.along(4, z, self.src, self.src, True).wait_send()
+
+        @pl.when(z > 0)
+        def _():
+            self.along(5, z, self.src, self.src, True).wait_send()
+
+        for k in range(1, 4):
+            source = self.line.source(k)
+
+            @pl.when(self.line.onward_up(k) | self.line.onward_down(k))
+            def _():
+                self.along(source, source, self.src, self.src, True).wait_send()
 
 
 def load_sequence(r_ref, s, kk_ref, vt_ref=None, vv_ref=None):
@@ -442,23 +515,24 @@
     o_out, o_expand, o_reduce, o_qkv, o_pairs, o_full, lse_ref,
     o_rows, o_scaled, o_spread, o_active, o_slope, o_turned, o_active_t,
     w_qkv, w_bias, w_vec, w_out, w_expand, send_blk, recv_blk, ctx_blk, ctx_recv, kk, vt,
-    e_row, x_turned, n_turned, normed, stage, turned, active_t, ctx_sib,
-    send_sem, recv_sem, local_sem, hsend, hrecv, csend, crecv, tsend, trecv, wsem,
+    e_row, x_turned, n_turned, normed, stage, turned, active_t, ctx_sib, active_all, slope_all,
+    send_sem, recv_sem, local_sem, hsend, hrecv, csend, crecv, tsend, trecv, wsem, zsend, zrecv, ksem,
 ):
     f32, bf16 = jnp.float32, jnp.bfloat16
     core, chip = place()
     sib = (1 - core, chip)
     greet([sib] + [(core, flip(chip, b)) for b in range(1, 16)])
     copies = Copies(send_sem, recv_sem)
+    line = Line(chip)
     first = [
-        Gather(copies, 0, s_qkv, w_qkv, local_sem.at[0]),
-        Gather(copies, 1, s_bias, w_bias, local_sem.at[1]),
+        Gather(copies, line, 0, s_qkv, w_qkv, local_sem.at[0], zsend, zrecv),
+        Gather(copies, line, 1, s_bias, w_bias, local_sem.at[1], zsend, zrecv),
     ]
     rest = [
-        Gather(copies, 2, s_out, o_out, local_sem.at[2]),
-        Gather(copies, 3, s_vec, w_vec, local_sem.at[3]),
-        Gather(copies, 4, s_expand, o_expand, local_sem.at[4]),
-        Gather(copies, 5, s_reduce, o_reduce, local_sem.at[5]),
+        Gather(copies, line, 2, s_out, o_out, local_sem.at[2], zsend, zrecv),
+        Gather(copies, line, 3, s_vec, w_vec, local_sem.at[3], zsend, zrecv),
+        Gather(copies, line, 4, s_expand, o_expand, local_sem.at[4], zsend, zrecv),
+        Gather(copies, line, 5, s_reduce, o_reduce, local_sem.at[5], zsend, zrecv),
     ]
     for g in first:
         g.start_z()
@@ -480,17 +554,17 @@
     for i in range(4):
         x_turned[i // 2, 256 * (i % 2) : 256 * (i % 2) + 256] = x_ref[:, 256 * i : 256 * i + 256].astype(f32).T.astype(bf16)
     swaps = [turn(0, x_turned.at[1 - core], x_turned.at[core])]
-    for z in (4, 8, 12):
+    for z in (1, 2, 3):
         for g in first:
             g.on_z(z)
     for g in rest[:3]:
         g.start_z()
-    for z in (0, 4, 8, 12):
+    for z in range(4):
         for g in first:
             g.on_plane(z)
     for g in rest:
         g.start_plane()
-    for z in (0, 4, 8, 12):
+    for z in range(4):
         for g in first:
             g.on_diagonal(z)
     for g in first:
@@ -498,6 +572,8 @@
     keep = pltpu.make_async_copy(w_qkv, o_qkv, local_sem.at[6])
     keep.start()
 
+    for g in rest[:3]:
+        g.on_z(1)
     for part in range(3):
 
         @pl.loop(0, 4)
@@ -513,6 +589,8 @@
                     rows = rows + jnp.concatenate([bias, bias], 1)
                 send_blk[h, pl.ds(64 * part, 64)] = rows.astype(bf16)
 
+    for g in rest[:3]:
+        g.on_z(2)
     heads = []
     for s in range(2):
         for b in FULL_ORDER:
@@ -540,19 +618,18 @@
 
     rest[3].start_z()
     events = [lambda: [g.on_plane(0) for g in rest]]
-    for z in (4, 8, 12):
-        events.append(lambda z=z: [g.on_z(z) for g in rest[:3]])
+    events.append(lambda: [g.on_z(3) for g in rest[:3]])
     events.append(lambda: [g.on_diagonal(0) for g in rest])
-    for z in (4, 8, 12):
+    for z in (1, 2, 3):
         events.append(lambda z=z: [g.on_plane(z) for g in rest[:3]])
-    for z in (4, 8, 12):
+    for z in (1, 2, 3):
         events.append(lambda z=z: [rest[3].on_z(z)])
-    for z in (4, 8, 12):
+    for z in (1, 2, 3):
         events.append(lambda z=z: [g.on_diagonal(z) for g in rest[:3]])
     READY = len(events)
-    for z in (4, 8, 12):
+    for z in (1, 2, 3):
         events.append(lambda z=z: [rest[3].on_plane(z)])
-    for z in (4, 8, 12):
+    for z in (1, 2, 3):
         events.append(lambda z=z: [rest[3].on_diagonal(z)])
 
     def attend_sequence(s, during):
@@ -594,7 +671,7 @@
 
         ctx_recv[chip, :, pl.ds(128 * s, 128)] = ctx_blk[s, chip]
 
-    PRE, FIRST, SECOND = 5, 3, 3
+    PRE, FIRST, SECOND = 3, 3, 5
     for event in events[:PRE]:
         event()
     heads_here(0)
@@ -690,6 +767,12 @@
             device_id_type=MESH,
         )
 
+    def keep_chunk(c):
+        return (
+            pltpu.make_async_copy(active_all.at[c], o_active.at[c], ksem.at[0, c]),
+            pltpu.make_async_copy(slope_all.at[c], o_slope.at[c], ksem.at[1, c]),
+        )
+
     last_events = events[READY:]
 
     @pl.loop(0, 8)
@@ -710,9 +793,11 @@
         expanded = jnp.dot(normed[...], w_expand[slot].reshape(1024, 512), preferred_element_type=f32) + e_row[pl.ds(c, 1)]
         share = 0.5 * (1.0 + lax.erf(expanded * math.sqrt(0.5)))
         bell = jnp.exp(-0.5 * expanded * expanded) * (1.0 / math.sqrt(2.0 * math.pi))
-        o_slope[c] = (share + expanded * bell).astype(bf16)
+        slope_all[c] = (share + expanded * bell).astype(bf16)
         active = (expanded * share).astype(bf16)
-        o_active[c] = active
+        active_all[c] = active
+        for copy in keep_chunk(c):
+            copy.start()
         across = active.astype(f32).T.astype(bf16)
         j = lax.rem(c, 4)
 
@@ -727,17 +812,28 @@
 
     for event in last_events[8:]:
         event()
-    rest[3].on_sibling()
     for c in swaps:
         c.wait()
     turned[2, 1] = ctx_sib[...].reshape(512, 256)
     for j in range(4):
         active_copy(j).wait()
-    o_turned[...] = turned[...]
-    o_active_t[...] = active_t[...]
+    kept = [
+        pltpu.make_async_copy(turned, o_turned, local_sem.at[0]),
+        pltpu.make_async_copy(active_t, o_active_t, local_sem.at[1]),
+    ]
+    for c in kept:
+        c.start()
+    rest[3].on_sibling()
+    for c in range(8):
+        for copy in keep_chunk(c):
+            copy.wait()
+    for c in kept:
+        c.wait()
     for c in heads:
         c.wait_send()
     copies.drain(sib)
+    for g in first + rest:
+        g.drain()
     keep.wait()
     pairs_out.wait()
 
@@ -776,7 +872,7 @@
             array((2, 4, 512, 256), bf16),
         ],
         in_specs=[v, pl.BlockSpec(memory_space=pltpu.SMEM)] + [hbm] * 6,
-        out_specs=[hbm] * 5 + [v] * 9,
+        out_specs=[hbm] * 5 + [v] * 5 + [hbm] * 4,
         scratch_shapes=[
             vmem((32,) + qkv.shape),
             vmem((32,) + bias.shape),
@@ -797,6 +893,8 @@
             vmem((3, 2, 512, 256)),
             vmem((2, 4, 512, 256)),
             vmem((8, 64, 256)),
+            vmem((8, 256, 512)),
+            vmem((8, 256, 512)),
             dma((210,)),
             dma((210,)),
             dma((9,)),
@@ -807,6 +905,9 @@
             dma((7,)),
             dma((7,)),
             dma((2,)),
+            dma((36,)),
+            dma((24,)),
+            dma((2, 8)),
         ],
         compiler_params=pltpu.CompilerParams(
             collective_id=collective_id, has_side_effects=True, vmem_limit_bytes=60 * MIB
@@ -926,15 +1027,15 @@
 def bwd_kernel(*refs):
     f32, bf16 = jnp.float32, jnp.bfloat16
     (
-        lengths_ref, pairs, o_full, lse_ref, rows_t, active_t, cotangent, scaled, spread, vectors,
+        lengths_ref, h_pairs, h_full, lse_ref, h_rows, h_active_t, cotangent, scaled, spread, vectors,
         h_active, h_slope, h_reduce, h_expand, h_out, h_qkv,
     ) = refs[:16]
     (o_layer, o_reduce, o_expand, o_out, o_vec, o_qkv, o_input, o_bias) = refs[16:24]
     bufs = [refs[24 + 3 * i : 27 + 3 * i] for i in range(5)]
     (
         g_reduce, g_expand, g_out, g_vec, g_qkv, w_qkv, d_recv, kk, vv, kt, acc, d_send, d_own, d_sib, b_own, b_sib, b_in,
-        slopes, w_reduce, w_expand, w_out, e_own, e_sib, d_first, a_own, a_sib, d_ctx, rows_sum, e_sum, vec_own, vec_sib, r_own, r_sib,
-        send_sem, recv_sem, local_sem, dsend, drecv, qsend, qrecv, esend, erecv, wsem,
+        slopes, w_reduce, w_expand, w_out, e_own, e_sib, d_first, a_own, a_sib, d_ctx, rows_sum, e_sum, vec_own, vec_sib, r_own, r_sib, pairs, o_full, rows_t, active_t,
+        send_sem, recv_sem, local_sem, dsend, drecv, qsend, qrecv, esend, erecv, wsem, lsem,
     ) = refs[39:]
     core, chip = place()
     sib = (1 - core, chip)
@@ -959,6 +1060,12 @@
         return copies_in
 
     for c in fetch(0, 0, False):
+        c.start()
+    loads = [
+        pltpu.make_async_copy(src, dst, lsem.at[i])
+        for i, (src, dst) in enumerate(((h_active_t, active_t), (h_rows, rows_t), (h_pairs, pairs), (h_full, o_full)))
+    ]
+    for c in loads:
         c.start()
     d_first[...] = scaled[...] * vectors[1:2] + (vectors[2:3] + vectors[4:5])
 
@@ -1006,6 +1113,8 @@
 
     copies.send("r", r_own, r_sib, sib, r_own)
     copies.arrived("r", r_sib, sib)
+    for c in loads:
+        c.wait()
 
     @pl.loop(0, 4)
     def _(j):
@@ -1059,6 +1168,8 @@
         rows_sum[1:2] += jnp.sum(d_normed * x_hat, 0, keepdims=True)
         rows_sum[2:3] += jnp.sum(d_normed, 0, keepdims=True)
 
+    for k in range(4):
+        rest[0].on_first(k)
     out_weights.wait()
 
     @pl.loop(0, 4)
@@ -1112,8 +1223,6 @@
     own_half, other_half = pl.ds(core * 16, 16), pl.ds((1 - core) * 16, 16)
     copies.send("v", vec_own.at[other_half], vec_sib, sib, vec_sib)
 
-    for k in range(4):
-        rest[0].on_first(k)
 
     @pl.loop(0, 8)
     def _(c):
@@ -1251,6 +1360,8 @@
         def _():
             b_in[...] = b_sib[:, rows]
 
+    for event in events[FIRST + SECOND + WAIT :]:
+        event()
     for i in range(4):
         fetch_qkv(i, i % 2).wait()
         t = None
@@ -1263,8 +1374,6 @@
         cols = slice(256 * i, 256 * i + 256)
         o_input[:, cols] = d_first[:, cols] + t.T
 
-    for event in events[FIRST + SECOND + WAIT :]:
-        event()
     for k in range(4):
         last.on_first(k)
     for r in rest:
@@ -1315,7 +1424,7 @@
         out_shape=[jax.ShapeDtypeStruct((256, 1024), bf16)]
         + [jax.ShapeDtypeStruct(block, f32) for block, _ in blocks]
         + [jax.ShapeDtypeStruct((256, 1024), f32), jax.ShapeDtypeStruct((2, 32, 128), f32)],
-        in_specs=[pl.BlockSpec(memory_space=pltpu.SMEM)] + [v] * 9 + [hbm] * 6,
+        in_specs=[pl.BlockSpec(memory_space=pltpu.SMEM), hbm, hbm, v, hbm, hbm] + [v] * 4 + [hbm] * 6,
         out_specs=[v] * 8,
         scratch_shapes=bufs
         + [
@@ -1352,6 +1461,10 @@
             vmem((16, 16, 128), f32),
             vmem((256, 1024)),
             vmem((256, 1024)),
+            vmem((2, 16, 192, 128)),
+            vmem((2, 64, 2048), f32),
+            vmem((3, 2, 512, 256)),
+            vmem((2, 4, 512, 256)),
             dma((144,)),
             dma((144,)),
             dma((7,)),
@@ -1362,6 +1475,7 @@
             dma((8,)),
             dma((8,)),
             dma((2, 3)),
+            dma((4,)),
         ],
         compiler_params=pltpu.CompilerParams(
             collective_id=collective_id, has_side_effects=True, vmem_limit_bytes=63 * MIB

time: 349 us -> 343 us (0.983)
  Pallas kernels: 332 us -> 326 us
    pallas_call x1, Pallas kernels: 172 us -> 167 us  [backward_attention(): pl.pallas_call(bwd_kernel, out_shape=[jax.ShapeDtypeStruct((256, 1024), b...]
where the time goes in v5:
time: 343 us; the launch traced here: 342 us
  Pallas kernels  326 us (95%)
  local copies, waits for them, and re-layouts  10.4 us (3%)
  other arithmetic  4.55 us (1%)
    pallas_call x1, Pallas kernels, backward_attention(): pl.pallas_call(bwd_kernel, out_shape=[jax.ShapeDtypeStruct((256, 1024), b...  167 us
    pallas_call x1, Pallas kernels, forward_attention(): pl.pallas_call(fwd_kernel, out_shape=[gathered(w_out), gathered(w_expand)...  159 us

profile of v5, /device:TPU:0, one launch (start us, length us, event | category | flops | bytes accessed | tf_op | source)
XLA Modules:
  0.0 341.6 jit_solution(9887187194002727538)
XLA Ops:
  0.7 0.7 pad_maximum_fusion.1
  1.4 1.4 pad_add_fusion.s_vec
  2.8 0.7 add.37.s_bias
  3.5 1.6 pad_maximum_fusion.s_qkv
  5.0 158.5 %forward_attention.1 = (bf16[32,32,1024]{2,1,0:T(8,128)(2,1)}, bf16[32,32,4096]{2,1,0:T(8,128)(2,1)}, bf16[32,128,1024]{2,1,0:T(8,128)(2,1)}, bf16[32,32,3072]{2...) custom-call(bf16[256,1024]{1,0:T(8,128)(2,1)} %bitcast.31, ...), custom_call_target="tpu_custom_call" | custom-call | tf_op jit(solution)/shard_map/forward_attention/pallas_call | solution.py:856
  163.6 167.4 %backward_attention.1 = (bf16[256,1024]{1,0:T(8,128)(2,1)}, f32[128,1024]{1,0:T(8,128)}, f32[32,4096]{1,0:T(8,128)}, f32[32,1024]{1,0:T(8,128)}, f32[16,128]{1,0...) custom-call(s32[2]{0:T(128)} %refs_0_.1, ...), custom_call_target="tpu_custom_call" | custom-call | tf_op jit(solution)/shard_map/backward_attention/pallas_call | solution.py:1422
  331.0 0.0 copy-start
  331.0 0.0 copy-start.3
  331.1 1.3 slice_bitcast_fusion.3
  332.3 0.8 reduce_sum.9
  333.2 1.4 slice_bitcast_fusion
  334.6 0.0 copy-start.2
  334.6 1.8 fusion
  336.5 0.0 copy-start.1
  336.5 1.9 copy.40
  338.4 0.0 copy-done
  338.4 1.0 copy.41
  339.4 0.0 copy-done.3
  339.4 0.7 copy.42
  340.0 0.0 copy-done.2
  340.0 0.8 copy.43
  340.8 0.0 copy-done.1
  340.8 0.8 copy.44
Async XLA Ops:
  331.0 7.4 %copy-start = (f32[256,1024]{1,0:T(8,128)S(1)}, f32[256,1024]{1,0:T(8,128)}, u32[]{:S(2)}) copy-start(f32[256,1024]{1,0:T(8,128)} %get-tuple-element.54) | copy-start | bytes 3145732
  331.0 8.3 %copy-start.3 = (f32[32,1024]{1,0:T(8,128)S(1)}, f32[32,1024]{1,0:T(8,128)}, u32[]{:S(2)}) copy-start(f32[32,1024]{1,0:T(8,128)} %get-tuple-element.98) | copy-start | bytes 393220
  334.6 5.4 %copy-start.2 = (f32[32,4096]{1,0:T(8,128)S(1)}, f32[32,4096]{1,0:T(8,128)}, u32[]{:S(2)}) copy-start(f32[32,4096]{1,0:T(8,128)} %get-tuple-element.102) | copy-start | bytes 1572868
  336.5 4.4 %copy-start.1 = (f32[128,1024]{1,0:T(8,128)S(1)}, f32[128,1024]{1,0:T(8,128)}, u32[]{:S(2)}) copy-start(f32[128,1024]{1,0:T(8,128)} %get-tuple-element.104) | copy-start | bytes 1572868

commit v6 on v5

--- a/solution.py
+++ b/solution.py
@@ -671,7 +671,7 @@
 
         ctx_recv[chip, :, pl.ds(128 * s, 128)] = ctx_blk[s, chip]
 
-    PRE, FIRST, SECOND = 3, 3, 5
+    PRE, FIRST, SECOND = 3, 4, 4
     for event in events[:PRE]:
         event()
     heads_here(0)
@@ -1302,7 +1302,7 @@
         rest[0].on_second(k)
     events = [lambda k=k: [r.on_first(k) for r in rest[1:]] for k in range(4)]
     events += [lambda k=k: [r.on_second(k) for r in rest[1:]] for k in range(4)]
-    FIRST, SECOND, WAIT = 0, 0, 4
+    FIRST, SECOND, WAIT = 0, 0, 5
     for b in FULL_ORDER:
         exchange_in(0, b, d_recv.at[0, flip(chip, b)], dsend, drecv)
     back_sequence(0, events[:FIRST])

time: 343 us -> 342 us (level)
  no operation moved by 1% of the time
where the time goes in v6:
time: 342 us; the launch traced here: 341 us
  Pallas kernels  326 us (95%)
  local copies, waits for them, and re-layouts  10.4 us (3%)
  other arithmetic  4.55 us (1%)
    pallas_call x1, Pallas kernels, backward_attention(): pl.pallas_call(bwd_kernel, out_shape=[jax.ShapeDtypeStruct((256, 1024), b...  166 us
    pallas_call x1, Pallas kernels, forward_attention(): pl.pallas_call(fwd_kernel, out_shape=[gathered(w_out), gathered(w_expand)...  160 us

profile of v6, /device:TPU:0, one launch (start us, length us, event | category | flops | bytes accessed | tf_op | source)
XLA Modules:
  0.0 341.4 jit_solution(14884289579895310868)
XLA Ops:
  0.7 0.7 pad_maximum_fusion.1
  1.4 1.4 pad_add_fusion.s_vec
  2.8 0.7 add.37.s_bias
  3.5 1.6 pad_maximum_fusion.s_qkv
  5.0 159.5 %forward_attention.1 = (bf16[32,32,1024]{2,1,0:T(8,128)(2,1)}, bf16[32,32,4096]{2,1,0:T(8,128)(2,1)}, bf16[32,128,1024]{2,1,0:T(8,128)(2,1)}, bf16[32,32,3072]{2...) custom-call(bf16[256,1024]{1,0:T(8,128)(2,1)} %bitcast.31, ...), custom_call_target="tpu_custom_call" | custom-call | tf_op jit(solution)/shard_map/forward_attention/pallas_call | solution.py:856
  164.6 166.2 %backward_attention.1 = (bf16[256,1024]{1,0:T(8,128)(2,1)}, f32[128,1024]{1,0:T(8,128)}, f32[32,4096]{1,0:T(8,128)}, f32[32,1024]{1,0:T(8,128)}, f32[16,128]{1,0...) custom-call(s32[2]{0:T(128)} %refs_0_.1, ...), custom_call_target="tpu_custom_call" | custom-call | tf_op jit(solution)/shard_map/backward_attention/pallas_call | solution.py:1422
  330.8 0.0 copy-start
  330.8 0.0 copy-start.3
  330.8 1.3 slice_bitcast_fusion.3
  332.1 0.8 reduce_sum.9
  333.0 1.4 slice_bitcast_fusion
  334.4 0.0 copy-start.2
  334.4 1.8 fusion
  336.3 0.0 copy-start.1
  336.3 1.9 copy.40
  338.2 0.0 copy-done
  338.2 1.0 copy.41
  339.2 0.0 copy-done.3
  339.2 0.7 copy.42
  339.8 0.0 copy-done.2
  339.8 0.8 copy.43
  340.6 0.0 copy-done.1
  340.6 0.8 copy.44
Async XLA Ops:
  330.8 7.4 %copy-start = (f32[256,1024]{1,0:T(8,128)S(1)}, f32[256,1024]{1,0:T(8,128)}, u32[]{:S(2)}) copy-start(f32[256,1024]{1,0:T(8,128)} %get-tuple-element.54) | copy-start | bytes 3145732
  330.8 8.3 %copy-start.3 = (f32[32,1024]{1,0:T(8,128)S(1)}, f32[32,1024]{1,0:T(8,128)}, u32[]{:S(2)}) copy-start(f32[32,1024]{1,0:T(8,128)} %get-tuple-element.98) | copy-start | bytes 393220
  334.4 5.4 %copy-start.2 = (f32[32,4096]{1,0:T(8,128)S(1)}, f32[32,4096]{1,0:T(8,128)}, u32[]{:S(2)}) copy-start(f32[32,4096]{1,0:T(8,128)} %get-tuple-element.102) | copy-start | bytes 1572868
  336.3 4.4 %copy-start.1 = (f32[128,1024]{1,0:T(8,128)S(1)}, f32[128,1024]{1,0:T(8,128)}, u32[]{:S(2)}) copy-start(f32[128,1024]{1,0:T(8,128)} %get-tuple-element.104) | copy-start | bytes 1572868

commit v7 on v6

--- a/solution.py
+++ b/solution.py
@@ -589,6 +589,7 @@
                     rows = rows + jnp.concatenate([bias, bias], 1)
                 send_blk[h, pl.ds(64 * part, 64)] = rows.astype(bf16)
 
+    rest[3].start_z()
     for g in rest[:3]:
         g.on_z(2)
     heads = []
@@ -616,7 +617,6 @@
                 src_ref=here, dst_ref=here, send_sem=hsend.at[i], recv_sem=hrecv.at[i], device_id=sib, device_id_type=MESH
             ).wait_recv()
 
-    rest[3].start_z()
     events = [lambda: [g.on_plane(0) for g in rest]]
     events.append(lambda: [g.on_z(3) for g in rest[:3]])
     events.append(lambda: [g.on_diagonal(0) for g in rest])

time: 342 us -> 344 us (level)
  no operation moved by 1% of the time
where the time goes in v7:
time: 344 us; the launch traced here: 343 us
  Pallas kernels  327 us (95%)
  local copies, waits for them, and re-layouts  10.4 us (3%)
  other arithmetic  4.55 us (1%)
    pallas_call x1, Pallas kernels, backward_attention(): pl.pallas_call(bwd_kernel, out_shape=[jax.ShapeDtypeStruct((256, 1024), b...  166 us
    pallas_call x1, Pallas kernels, forward_attention(): pl.pallas_call(fwd_kernel, out_shape=[gathered(w_out), gathered(w_expand)...  161 us

profile of v7, /device:TPU:0, one launch (start us, length us, event | category | flops | bytes accessed | tf_op | source)
XLA Modules:
  0.0 342.7 jit_solution(12735291567589721470)
XLA Ops:
  0.7 0.7 pad_maximum_fusion.1
  1.4 1.4 pad_add_fusion.s_vec
  2.8 0.7 add.37.s_bias
  3.5 1.6 pad_maximum_fusion.s_qkv
  5.0 161.0 %forward_attention.1 = (bf16[32,32,1024]{2,1,0:T(8,128)(2,1)}, bf16[32,32,4096]{2,1,0:T(8,128)(2,1)}, bf16[32,128,1024]{2,1,0:T(8,128)(2,1)}, bf16[32,32,3072]{2...) custom-call(bf16[256,1024]{1,0:T(8,128)(2,1)} %bitcast.31, ...), custom_call_target="tpu_custom_call" | custom-call | tf_op jit(solution)/shard_map/forward_attention/pallas_call | solution.py:856
  166.0 166.1 %backward_attention.1 = (bf16[256,1024]{1,0:T(8,128)(2,1)}, f32[128,1024]{1,0:T(8,128)}, f32[32,4096]{1,0:T(8,128)}, f32[32,1024]{1,0:T(8,128)}, f32[16,128]{1,0...) custom-call(s32[2]{0:T(128)} %refs_0_.1, ...), custom_call_target="tpu_custom_call" | custom-call | tf_op jit(solution)/shard_map/backward_attention/pallas_call | solution.py:1422
  332.1 0.0 copy-start
  332.1 0.0 copy-start.3
  332.2 1.3 slice_bitcast_fusion.3
  333.4 0.8 reduce_sum.9
  334.3 1.4 slice_bitcast_fusion
  335.7 0.0 copy-start.2
  335.7 1.8 fusion
  337.6 0.0 copy-start.1
  337.6 1.9 copy.40
  339.5 0.0 copy-done
  339.5 1.0 copy.41
  340.5 0.0 copy-done.3
  340.5 0.7 copy.42
  341.1 0.0 copy-done.2
  341.1 0.8 copy.43
  341.9 0.0 copy-done.1
  341.9 0.8 copy.44
Async XLA Ops:
  332.1 7.4 %copy-start = (f32[256,1024]{1,0:T(8,128)S(1)}, f32[256,1024]{1,0:T(8,128)}, u32[]{:S(2)}) copy-start(f32[256,1024]{1,0:T(8,128)} %get-tuple-element.54) | copy-start | bytes 3145732
  332.1 8.3 %copy-start.3 = (f32[32,1024]{1,0:T(8,128)S(1)}, f32[32,1024]{1,0:T(8,128)}, u32[]{:S(2)}) copy-start(f32[32,1024]{1,0:T(8,128)} %get-tuple-element.98) | copy-start | bytes 393220
  335.7 5.4 %copy-start.2 = (f32[32,4096]{1,0:T(8,128)S(1)}, f32[32,4096]{1,0:T(8,128)}, u32[]{:S(2)}) copy-start(f32[32,4096]{1,0:T(8,128)} %get-tuple-element.102) | copy-start | bytes 1572868
  337.6 4.4 %copy-start.1 = (f32[128,1024]{1,0:T(8,128)S(1)}, f32[128,1024]{1,0:T(8,128)}, u32[]{:S(2)}) copy-start(f32[128,1024]{1,0:T(8,128)} %get-tuple-element.104) | copy-start | bytes 1572868
